TPU v7x, 32 devices: a whole 2x2x4 slice. The times are simulated.
32 devices in a mesh: ctx: 8 (over y, x, core), head: 4 (over z).
Axes of the slice: x: 2, y: 2, z: 4, core: 2. Of those that a mesh axis runs over, the one named last changes fastest.
Arguments:
- tokens: bfloat16 [2, 2, 1536, 2560], P(None, None, 'ctx'), may hold values from -6 to 6
- lengths: int32 [2, 2], replicated, may hold values from 1024 to 1536, as said below
- cotangent: bfloat16 [2, 2, 1536, 2560], P(None, None, 'ctx'), may hold values from -6 to 6
- attn_gain: bfloat16 [2560], P('ctx'), may hold values from 0.5 to 1.5
- query_weight: bfloat16 [2560, 2560], P('ctx', 'head'), may hold values from -0.125 to 0.125
- key_weight: bfloat16 [2560, 640], P('ctx', 'head'), may hold values from -0.125 to 0.125
- value_weight: bfloat16 [2560, 640], P('ctx', 'head'), may hold values from -0.125 to 0.125
- out_weight: bfloat16 [2560, 2560], P('head', 'ctx'), may hold values from -1.25 to 1.25
- ffn_gain: bfloat16 [2560], P('ctx'), may hold values from 0.5 to 1.5
- gate_weight: bfloat16 [2560, 6912], P('ctx', 'head'), may hold values from -0.125 to 0.125
- up_weight: bfloat16 [2560, 6912], P('ctx', 'head'), may hold values from -0.125 to 0.125
- down_weight: bfloat16 [6912, 2560], P('head', 'ctx'), may hold values from -0.078125 to 0.078125
Outputs:
- mixed: bfloat16 [2, 2, 1536, 2560], P(None, None, 'ctx')
- token_grad: float32 [2, 2, 1536, 2560], P(None, None, 'ctx')
- attn_gain_grad: float32 [2560], P('ctx')
- query_grad: float32 [2560, 2560], P('ctx', 'head')
- key_grad: float32 [2560, 640], P('ctx', 'head')
- value_grad: float32 [2560, 640], P('ctx', 'head')
- out_grad: float32 [2560, 2560], P('head', 'ctx')
- ffn_gain_grad: float32 [2560], P('ctx')
- gate_grad: float32 [2560, 6912], P('ctx', 'head')
- up_grad: float32 [2560, 6912], P('ctx', 'head')
- down_grad: float32 [6912, 2560], P('head', 'ctx')
Inputs may be any that keep to these rules, and one draw needn't show every extreme that they name: `lengths`: in each micro-batch one sequence, chosen by the seed, has all 1536 slots live.
All inputs are finite; a program needn't handle non-finite values.
Results may differ from a plain program's by a relative error of at most 0.022.
Values may be sent and summed in bfloat16 or wider, within the bound.
No kernel may reach another device: no remote copies, remote signals or barrier semaphores. Data moves between devices by JAX's collectives and lax.ppermute only.
A program may use at most 320 MiB of HBM per device.

v0:
```python
import jax
import jax.numpy as jnp
from jax import lax
from jax.sharding import PartitionSpec as P

HD = 80
WINDOW = 4096


EPSILON = 1e-05
THETA_BASE = 10000.0
NEGATIVE = -1e30


def inner_rows(left, right):
    return lax.dot_general(
        left, right, (((0,), (0,)), ((), ())), preferred_element_type=jnp.float32
    )


def outer_back(left, right):
    return lax.dot_general(
        left, right, (((1,), (1,)), ((), ())), preferred_element_type=jnp.float32
    )


def tables(positions, width):
    half = width // 2
    freq = THETA_BASE ** (-jnp.arange(half, dtype=jnp.float32) * 2.0 / width)
    angle = positions.astype(jnp.float32)[:, None] * freq[None, :]
    return (jnp.cos(angle)[None, :, None, :], jnp.sin(angle)[None, :, None, :])


def rotate(values, cosine, sine):
    half = values.shape[-1] // 2
    first = values[..., :half]
    second = values[..., half:]
    return jnp.concatenate(
        [first * cosine - second * sine, second * cosine + first * sine], axis=-1
    )


def rotate_back(grads, cosine, sine):
    half = grads.shape[-1] // 2
    first = grads[..., :half]
    second = grads[..., half:]
    return jnp.concatenate(
        [first * cosine + second * sine, second * cosine - first * sine], axis=-1
    )


def per_device(
    tokens,
    lengths,
    cotangent,
    attn_gain,
    query_weight,
    key_weight,
    value_weight,
    out_weight,
    ffn_gain,
    gate_weight,
    up_weight,
    down_weight,
):
    micro_count, seq_count, local_tokens, model_width = tokens.shape
    gathered = (
        lax.all_gather(attn_gain, "ctx", axis=0, tiled=True),
        lax.all_gather(query_weight, "ctx", axis=0, tiled=True),
        lax.all_gather(key_weight, "ctx", axis=0, tiled=True),
        lax.all_gather(value_weight, "ctx", axis=0, tiled=True),
        lax.all_gather(out_weight, "ctx", axis=1, tiled=True),
        lax.all_gather(ffn_gain, "ctx", axis=0, tiled=True),
        lax.all_gather(gate_weight, "ctx", axis=0, tiled=True),
        lax.all_gather(up_weight, "ctx", axis=0, tiled=True),
        lax.all_gather(down_weight, "ctx", axis=1, tiled=True),
    )
    gain_attn = gathered[0].astype(jnp.float32)
    full_query = gathered[1]
    full_key = gathered[2]
    full_value = gathered[3]
    full_out = gathered[4]
    gain_ffn = gathered[5].astype(jnp.float32)
    full_gate = gathered[6]
    full_up = gathered[7]
    full_down = gathered[8]
    local_heads = full_query.shape[1] // HD
    local_groups = full_key.shape[1] // HD
    group_size = local_heads // local_groups
    span_total = local_tokens * lax.axis_size("ctx")
    first_slot = lax.axis_index("ctx") * local_tokens
    query_slots = first_slot + jnp.arange(local_tokens)
    key_slots = jnp.arange(span_total)
    cosine, sine = tables(query_slots, HD)
    scale = HD ** (-0.5)
    row_count = seq_count * local_tokens
    mixed_parts = []
    token_parts = []
    totals = None
    for batch_index in range(micro_count):
        seq_lengths = lengths[batch_index]
        allowed = (
            (key_slots[None, None, :] <= query_slots[None, :, None])
            & (query_slots[None, :, None] - key_slots[None, None, :] < WINDOW)
            & (key_slots[None, None, :] < seq_lengths[:, None, None])
        )
        allowed = allowed[:, None, None]
        live_rows = (
            (query_slots[None, :] < seq_lengths[:, None]).astype(jnp.float32).reshape(row_count, 1)
        )
        resid_in = tokens[batch_index].astype(jnp.float32).reshape(row_count, model_width)
        scale_one = lax.rsqrt(jnp.mean(resid_in * resid_in, axis=-1, keepdims=True) + EPSILON)
        normed_one = resid_in * scale_one
        input_one = (normed_one * gain_attn).astype(jnp.bfloat16)
        query_proj = jnp.dot(input_one, full_query, preferred_element_type=jnp.float32)
        key_proj = jnp.dot(input_one, full_key, preferred_element_type=jnp.float32)
        value_proj = jnp.dot(input_one, full_value, preferred_element_type=jnp.float32)
        query_rot = rotate(
            query_proj.reshape(seq_count, local_tokens, local_heads, HD), cosine, sine
        ).astype(jnp.bfloat16)
        query_rot = query_rot.reshape(seq_count, local_tokens, local_groups, group_size, HD)
        key_rot = rotate(
            key_proj.reshape(seq_count, local_tokens, local_groups, HD), cosine, sine
        ).astype(jnp.bfloat16)
        value_low = value_proj.reshape(seq_count, local_tokens, local_groups, HD).astype(
            jnp.bfloat16
        )
        key_all, value_all = (
            lax.all_gather(key_rot, "ctx", axis=1, tiled=True),
            lax.all_gather(value_low, "ctx", axis=1, tiled=True),
        )
        scores = (
            jnp.einsum("stkgd,spkd->skgtp", query_rot, key_all, preferred_element_type=jnp.float32)
            * scale
        )
        scores = jnp.where(allowed, scores, NEGATIVE)
        top_score = jnp.max(scores, axis=-1, keepdims=True)
        exponent = jnp.exp(scores - top_score)
        total_weight = jnp.sum(exponent, axis=-1, keepdims=True)
        probs_low = (exponent / total_weight).astype(jnp.bfloat16)
        log_total = top_score + jnp.log(total_weight)
        attended = jnp.einsum(
            "skgtp,spkd->stkgd", probs_low, value_all, preferred_element_type=jnp.float32
        )
        attended_low = attended.reshape(row_count, local_heads * HD).astype(jnp.bfloat16)
        grad_out = (
            cotangent[batch_index].astype(jnp.float32).reshape(row_count, model_width) * live_rows
        )
        grad_low = grad_out.astype(jnp.bfloat16)
        attn_branch = lax.psum(
            jnp.dot(attended_low, full_out, preferred_element_type=jnp.float32), "head"
        )
        hidden = resid_in + attn_branch
        scale_two = lax.rsqrt(jnp.mean(hidden * hidden, axis=-1, keepdims=True) + EPSILON)
        normed_two = hidden * scale_two
        input_two = (normed_two * gain_ffn).astype(jnp.bfloat16)
        gate_proj = jnp.dot(input_two, full_gate, preferred_element_type=jnp.float32)
        up_proj = jnp.dot(input_two, full_up, preferred_element_type=jnp.float32)
        sigmoid_gate = jax.nn.sigmoid(gate_proj)
        silu_gate = gate_proj * sigmoid_gate
        activation = (silu_gate * up_proj).astype(jnp.bfloat16)
        down_term = inner_rows(activation, grad_low)
        grad_act = outer_back(grad_low, full_down)
        grad_gate = (
            grad_act * up_proj * sigmoid_gate * (1.0 + gate_proj * (1.0 - sigmoid_gate))
        ).astype(jnp.bfloat16)
        grad_up = (grad_act * silu_gate).astype(jnp.bfloat16)
        gate_term = inner_rows(input_two, grad_gate)
        up_term = inner_rows(input_two, grad_up)
        ffn_branch = lax.psum(
            jnp.dot(activation, full_down, preferred_element_type=jnp.float32).astype(jnp.bfloat16),
            "head",
        ).astype(jnp.float32)
        mixed_parts.append(
            (hidden + ffn_branch).astype(jnp.bfloat16).reshape(seq_count, local_tokens, model_width)
        )
        grad_two = lax.psum(outer_back(grad_gate, full_gate) + outer_back(grad_up, full_up), "head")
        scaled_two = grad_two * gain_ffn
        gain_two_term = jnp.sum(grad_two * normed_two, axis=0)
        grad_hidden = grad_out + scale_two * (
            scaled_two - normed_two * jnp.mean(scaled_two * normed_two, axis=-1, keepdims=True)
        )
        hidden_low = grad_hidden.astype(jnp.bfloat16)
        out_term = inner_rows(attended_low, hidden_low)
        grad_att = outer_back(hidden_low, full_out).astype(jnp.bfloat16)
        grad_att = grad_att.reshape(seq_count, local_tokens, local_groups, group_size, HD)
        key_back, value_back = (key_all, value_all)
        scores_back = (
            jnp.einsum("stkgd,spkd->skgtp", query_rot, key_back, preferred_element_type=jnp.float32)
            * scale
        )
        scores_back = jnp.where(allowed, scores_back, NEGATIVE)
        probs_back = jnp.exp(scores_back - log_total)
        grad_probs = jnp.einsum(
            "stkgd,spkd->skgtp", grad_att, value_back, preferred_element_type=jnp.float32
        )
        row_dot = jnp.sum(probs_back * grad_probs, axis=-1, keepdims=True)
        grad_scores = (probs_back * (grad_probs - row_dot)).astype(jnp.bfloat16)
        grad_query = (
            jnp.einsum(
                "skgtp,spkd->stkgd", grad_scores, key_back, preferred_element_type=jnp.float32
            )
            * scale
        )
        key_partial = (
            jnp.einsum(
                "skgtp,stkgd->spkd", grad_scores, query_rot, preferred_element_type=jnp.float32
            )
            * scale
        )
        value_partial = jnp.einsum(
            "skgtp,stkgd->spkd",
            probs_back.astype(jnp.bfloat16),
            grad_att,
            preferred_element_type=jnp.float32,
        )
        key_grad_rot, value_grad_rows = (
            lax.psum_scatter(
                key_partial.astype(jnp.bfloat16), "ctx", scatter_dimension=1, tiled=True
            ).astype(jnp.float32),
            lax.psum_scatter(
                value_partial.astype(jnp.bfloat16), "ctx", scatter_dimension=1, tiled=True
            ).astype(jnp.float32),
        )
        query_pre = rotate_back(
            grad_query.reshape(seq_count, local_tokens, local_heads, HD), cosine, sine
        )
        query_pre = query_pre.reshape(row_count, local_heads * HD).astype(jnp.bfloat16)
        key_pre = (
            rotate_back(key_grad_rot, cosine, sine)
            .reshape(row_count, local_groups * HD)
            .astype(jnp.bfloat16)
        )
        value_pre = value_grad_rows.reshape(row_count, local_groups * HD).astype(jnp.bfloat16)
        query_term = inner_rows(input_one, query_pre)
        key_term = inner_rows(input_one, key_pre)
        value_term = inner_rows(input_one, value_pre)
        grad_one = lax.psum(
            (
                outer_back(query_pre, full_query)
                + outer_back(key_pre, full_key)
                + outer_back(value_pre, full_value)
            ).astype(jnp.bfloat16),
            "head",
        ).astype(jnp.float32)
        scaled_one = grad_one * gain_attn
        gain_one_term = jnp.sum(grad_one * normed_one, axis=0)
        token_back = grad_hidden + scale_one * (
            scaled_one - normed_one * jnp.mean(scaled_one * normed_one, axis=-1, keepdims=True)
        )
        token_parts.append(token_back.reshape(seq_count, local_tokens, model_width))
        terms = (
            gain_one_term,
            query_term,
            key_term,
            value_term,
            out_term,
            gain_two_term,
            gate_term,
            up_term,
            down_term,
        )
        totals = (
            terms
            if totals is None
            else tuple((first + second for first, second in zip(totals, terms)))
        )
    totals = (
        lax.psum_scatter(
            totals[0].astype(jnp.bfloat16), "ctx", scatter_dimension=0, tiled=True
        ).astype(jnp.float32),
        lax.psum_scatter(
            totals[1].astype(jnp.bfloat16), "ctx", scatter_dimension=0, tiled=True
        ).astype(jnp.float32),
        lax.psum_scatter(
            totals[2].astype(jnp.bfloat16), "ctx", scatter_dimension=0, tiled=True
        ).astype(jnp.float32),
        lax.psum_scatter(
            totals[3].astype(jnp.bfloat16), "ctx", scatter_dimension=0, tiled=True
        ).astype(jnp.float32),
        lax.psum_scatter(
            totals[4].astype(jnp.bfloat16), "ctx", scatter_dimension=1, tiled=True
        ).astype(jnp.float32),
        lax.psum_scatter(
            totals[5].astype(jnp.bfloat16), "ctx", scatter_dimension=0, tiled=True
        ).astype(jnp.float32),
        lax.psum_scatter(
            totals[6].astype(jnp.bfloat16), "ctx", scatter_dimension=0, tiled=True
        ).astype(jnp.float32),
        lax.psum_scatter(
            totals[7].astype(jnp.bfloat16), "ctx", scatter_dimension=0, tiled=True
        ).astype(jnp.float32),
        lax.psum_scatter(
            totals[8].astype(jnp.bfloat16), "ctx", scatter_dimension=1, tiled=True
        ).astype(jnp.float32),
    )
    mixed = jnp.stack(mixed_parts, axis=0)
    token_grad = jnp.stack(token_parts, axis=0)
    return (
        mixed,
        token_grad,
        totals[0],
        totals[1],
        totals[2],
        totals[3],
        totals[4],
        totals[5],
        totals[6],
        totals[7],
        totals[8],
    )


def solution(mesh):
    placed = (
        P(None, None, "ctx", None),
        P(),
        P(None, None, "ctx", None),
        P("ctx"),
        P("ctx", "head"),
        P("ctx", "head"),
        P("ctx", "head"),
        P("head", "ctx"),
        P("ctx"),
        P("ctx", "head"),
        P("ctx", "head"),
        P("head", "ctx"),
    )
    return jax.shard_map(
        per_device,
        mesh=mesh,
        in_specs=placed,
        out_specs=(
            P(None, None, "ctx", None),
            P(None, None, "ctx", None),
            P("ctx"),
            P("ctx", "head"),
            P("ctx", "head"),
            P("ctx", "head"),
            P("head", "ctx"),
            P("ctx"),
            P("ctx", "head"),
            P("ctx", "head"),
            P("head", "ctx"),
        ),
        check_vma=False,
    )
```

profile of v0, /device:TPU:0, one launch (start us, length us, event | category | flops | bytes accessed | tf_op | source)
XLA Modules:
  0.0 1976.9 jit_solution(13090060415415140912)
XLA Ops:
  13.7 25.9 %all-reduce.7 = (bf16[2560]{0:T(1024)(128)(2,1)S(1)}, bf16[2560]{0:T(1024)(128)(2,1)}) all-reduce(bf16[2560]{0:T(1024)(128)(2,1)S(1)} %dynamic-update-slice, bf16[2560]{0:T(1024)(128)(2,1)S(1)} %dynamic-update-slice.1), channel_id=1, replica_groups=mesh['ctx'=8,'head'=4] {'ctx'}, use_global_device_ids=true, to_apply=%add | all-reduce | flops 5120 | bytes 20480
  51.6 13.3 all-gather
  79.0 14.5 all_gather.51
  97.0 14.1 all_gather.43
  115.8 13.9 all_gather.50
  134.6 14.1 all_gather.41
  244.7 264.5 %all-reduce.15.cloned.1.call-done = (f32[384,2560]{1,0:T(8,128)}, f32[384,2560]{1,0:T(8,128)}) async-done(((f32[384,2560]{1,0:T(8,128)}, f32[384,2560]{1,0:T(8,128)}), (f32[384,2560]{1,0:T(8,128)}, f32[384,2560]{1,0:T(8,128)})) %all-reduce.15.cloned.1.call-update) | async-done | bytes 7864336 | tf_op jit(solution)/shard_map/psum | solution.py:150
  520.1 47.5 %all-gather.14.cloned.1.call-done = bf16[2560,1728]{1,0:T(8,128)(2,1)} async-done(((bf16[320,1728]{1,0:T(8,128)(2,1)}), bf16[2560,1728]{1,0:T(8,128)(2,1)}) %all-gather.14.cloned.1.call-update) | async-done | bytes 8847376 | tf_op jit(solution)/shard_map/all_gather | solution.py:75
  578.1 49.0 %all-gather.12.cloned.1.call-done = bf16[2560,1728]{1,0:T(8,128)(2,1)} async-done(((bf16[320,1728]{1,0:T(8,128)(2,1)}), bf16[2560,1728]{1,0:T(8,128)(2,1)}) %all-gather.12.cloned.1.call-update) | async-done | bytes 8847376 | tf_op jit(solution)/shard_map/all_gather | solution.py:74
  653.2 33.3 %all-gather.16.cloned.1.call-done = bf16[1728,2560]{0,1:T(8,128)(2,1)} async-done(((bf16[1728,320]{0,1:T(8,128)(2,1)}), bf16[1728,2560]{0,1:T(8,128)(2,1)}) %all-gather.16.cloned.1.call-update) | async-done | bytes 8847376 | tf_op jit(solution)/shard_map/all_gather | solution.py:76
  706.7 14.4 multiply_convert_fusion.4
  748.7 273.6 %all-reduce.13.cloned.1.call-done = (f32[384,2560]{1,0:T(8,128)}, f32[384,2560]{1,0:T(8,128)}) async-done(((f32[384,2560]{1,0:T(8,128)}, f32[384,2560]{1,0:T(8,128)}), (f32[384,2560]{1,0:T(8,128)}, f32[384,2560]{1,0:T(8,128)})) %all-reduce.13.cloned.1.call-update) | async-done | bytes 7864336 | tf_op jit(solution)/shard_map/psum | solution.py:177
  1133.4 13.3 fusion.2
  1165.8 18.6 reduce-scatter.34.cloned.1.call-done
  1185.6 39.1 %reduce-scatter.38.cloned.1.call-done = bf16[192,320]{1,0:T(8,128)(2,1)} async-done(((bf16[1536,320]{1,0:T(8,128)(2,1)}), bf16[192,320]{1,0:T(8,128)(2,1)}) %reduce-scatter.38.cloned.1.call-update) | async-done | bytes 122896
  1268.8 13.6 fusion.122
  1294.2 13.4 fusion.121
  1319.2 13.9 fusion.120
  1379.9 26.3 %reduce-scatter.24.cloned.1.call-done = bf16[320,640]{1,0:T(8,128)(2,1)} async-done(((bf16[2560,640]{1,0:T(8,128)(2,1)}), bf16[320,640]{1,0:T(8,128)(2,1)}) %reduce-scatter.24.cloned.1.call-update) | async-done | bytes 409616 | tf_op jit(solution)/shard_map/reduce_scatter | solution.py:272
  1408.1 76.6 %reduce-scatter.32.cloned.1.call-done = bf16[1728,320]{0,1:T(8,128)(2,1)} async-done(((bf16[1728,2560]{0,1:T(8,128)(2,1)}), bf16[1728,320]{0,1:T(8,128)(2,1)}) %reduce-scatter.32.cloned.1.call-update) | async-done | bytes 1105936 | tf_op jit(solution)/shard_map/reduce_scatter | solution.py:293
  1487.5 76.2 %reduce-scatter.30.cloned.1.call-done = bf16[320,1728]{1,0:T(8,128)(2,1)} async-done(((bf16[2560,1728]{1,0:T(8,128)(2,1)}), bf16[320,1728]{1,0:T(8,128)(2,1)}) %reduce-scatter.30.cloned.1.call-update) | async-done | bytes 1105936 | tf_op jit(solution)/shard_map/reduce_scatter | solution.py:290
  1566.5 75.7 %reduce-scatter.28.cloned.1.call-done = bf16[320,1728]{1,0:T(8,128)(2,1)} async-done(((bf16[2560,1728]{1,0:T(8,128)(2,1)}), bf16[320,1728]{1,0:T(8,128)(2,1)}) %reduce-scatter.28.cloned.1.call-update) | async-done | bytes 1105936 | tf_op jit(solution)/shard_map/reduce_scatter | solution.py:287
  1645.0 274.9 %all-reduce.17.cloned.1.call-done = (bf16[384,2560]{1,0:T(8,128)(2,1)}, bf16[384,2560]{1,0:T(8,128)(2,1)}, bf16[384,2560]{1,0:T(8,128)(2,1)}, bf16[384,2560]{1,0:T(8,128)(2,1)}) async-done(((bf16[384,2560]{1,0:T(8,128)(2,1)}, bf16[384,2560]{1,0:T(8,128)(2,1)}, bf16[384,2560]{1,0:T(8,128)(2,1)}, bf16[384,2560]{1,0:T(8,128)(2,1)}), (bf16[384,2560]{1,0:T(8,128)(2,1)}, bf16[384,2560]{1,0:T(8,128)(2,1)}, ...) | async-done | bytes 7864336 | tf_op jit(solution)/shard_map/psum | solution.py:170
  1931.0 24.0 %all-reduce.6 = (bf16[2560]{0:T(1024)(128)(2,1)S(1)}, bf16[2560]{0:T(1024)(128)(2,1)S(1)}) all-reduce(bf16[2560]{0:T(1024)(128)(2,1)S(1)} %add_convert_fusion.12, bf16[2560]{0:T(1024)(128)(2,1)S(1)} %add_convert_fusion.11), channel_id=6, replica_groups=mesh['ctx'=8,'head'=4] {'ctx'}, use_global_device_ids=true, to_apply=%region_28.29.clone | all-reduce | flops 5120 | bytes 20480
  (436 shorter events, 516.1 us)
Async XLA Ops:
  7.2 148.6 %all-gather.8.cloned.1.call-start = ((), (), s32[]{:S(2)}) async-start(), calls=%async_computation.11 | async-start | bytes 3686400 | tf_op jit(solution)/shard_map/all_gather | solution.py:69
  8.0 217.5 %all-gather.10.cloned.1.call-start = ((), (), s32[]{:S(2)}) async-start(), calls=%async_computation.12 | async-start | bytes 3686400 | tf_op jit(solution)/shard_map/all_gather | solution.py:72
  8.7 500.5 %all-reduce.15.cloned.1.call-start = ((), (), s32[]{:S(2)}) async-start(), calls=%async_computation.28 | async-start | bytes 15728640 | tf_op jit(solution)/shard_map/psum | solution.py:150
  70.0 91.5 %copy-start.11 = (bf16[1,2,192,2560]{3,2,1,0:T(8,128)(2,1)}, bf16[1,2,192,2560]{3,2,1,0:T(8,128)(2,1)S(1)}, u32[]{:S(2)}) copy-start(bf16[1,2,192,2560]{3,2,1,0:T(8,128)(2,1)S(1)} %get-tuple-element.47) | copy-start | bytes 5898244
  74.5 78.9 %copy-start.97 = (s32[2]{0:T(128)}, s32[2]{0:T(128)S(1)}, u32[]{:S(2)}) copy-start(s32[2]{0:T(128)S(1)} %get-tuple-element.86) | copy-start | bytes 28
  97.0 101.4 %copy-start.29 = (bf16[2,1536,2,80,1]{1,3,4,2,0:T(8,128)(2,1)}, bf16[2,1536,2,80,1]{1,3,4,2,0:T(8,128)(2,1)S(1)}, u32[]{:S(2)}) copy-start(bf16[2,1536,2,80,1]{1,3,4,2,0:T(8,128)(2,1)S(1)} %copy.78) | copy-start | bytes 2949124
  235.0 332.6 %all-gather.14.cloned.1.call-start = ((), (), s32[]{:S(2)}) async-start(), calls=%async_computation.14 | async-start | bytes 10321920 | tf_op jit(solution)/shard_map/all_gather | solution.py:75
  235.5 391.5 %all-gather.12.cloned.1.call-start = ((), (), s32[]{:S(2)}) async-start(), calls=%async_computation.13 | async-start | bytes 10321920 | tf_op jit(solution)/shard_map/all_gather | solution.py:74
  236.1 450.4 %all-gather.16.cloned.1.call-start = ((), (), s32[]{:S(2)}) async-start(), calls=%async_computation.15 | async-start | bytes 10321920 | tf_op jit(solution)/shard_map/all_gather | solution.py:76
  236.7 785.5 %all-reduce.13.cloned.1.call-start = ((), (), s32[]{:S(2)}) async-start(), calls=%async_computation.27 | async-start | bytes 15728640 | tf_op jit(solution)/shard_map/psum | solution.py:177
  520.1 124.3 %copy-start.9 = (bf16[384,2560]{1,0:T(8,128)(2,1)}, bf16[384,2560]{1,0:T(8,128)(2,1)S(1)}, u32[]{:S(2)}) copy-start(bf16[384,2560]{1,0:T(8,128)(2,1)S(1)} %get-tuple-element.81) | copy-start | bytes 5898244
  747.9 279.3 %copy-start.25 = (bf16[1,2,192,2560]{3,2,1,0:T(8,128)(2,1)S(1)}, bf16[1,2,192,2560]{3,2,1,0:T(8,128)(2,1)}, u32[]{:S(2)}) copy-start(bf16[1,2,192,2560]{3,2,1,0:T(8,128)(2,1)} %copy-done.24) | copy-start | bytes 5898244
  748.0 411.2 %reduce-scatter.40.cloned.1.call-start = ((), (), s32[]{:S(2)}) async-start(), calls=%async_computation.24 | async-start | bytes 1327104
  1068.2 92.4 %reduce-scatter.36.cloned.1.call-start = ((), (), s32[]{:S(2)}) async-start(), calls=%async_computation.22 | async-start | bytes 1327104
  1096.0 88.4 %reduce-scatter.34.cloned.1.call-start = ((), (), s32[]{:S(2)}) async-start(), calls=%async_computation.21 | async-start | bytes 1327104
  1133.3 91.4 %reduce-scatter.38.cloned.1.call-start = ((), (), s32[]{:S(2)}) async-start(), calls=%async_computation.23 | async-start | bytes 1327104
  1158.7 215.7 %reduce-scatter.44.cloned.1.call-start = ((), (), s32[]{:S(2)}) async-start(), calls=%async_computation.26 | async-start | bytes 1474560
  1165.7 210.5 %reduce-scatter.42.cloned.1.call-start = ((), (), s32[]{:S(2)}) async-start(), calls=%async_computation.25 | async-start | bytes 1474560
  1232.4 145.6 %reduce-scatter.26.cloned.1.call-start = ((), (), s32[]{:S(2)}) async-start(), calls=%async_computation.17 | async-start | bytes 3686400 | tf_op jit(solution)/shard_map/reduce_scatter | solution.py:281
  1241.0 165.2 %reduce-scatter.24.cloned.1.call-start = ((), (), s32[]{:S(2)}) async-start(), calls=%async_computation.16 | async-start | bytes 3686400 | tf_op jit(solution)/shard_map/reduce_scatter | solution.py:272
  1268.5 216.2 %reduce-scatter.32.cloned.1.call-start = ((), (), s32[]{:S(2)}) async-start(), calls=%async_computation.20 | async-start | bytes 10321920 | tf_op jit(solution)/shard_map/reduce_scatter | solution.py:293
  1293.9 269.8 %reduce-scatter.30.cloned.1.call-start = ((), (), s32[]{:S(2)}) async-start(), calls=%async_computation.19 | async-start | bytes 10321920 | tf_op jit(solution)/shard_map/reduce_scatter | solution.py:290
  1318.7 323.6 %reduce-scatter.28.cloned.1.call-start = ((), (), s32[]{:S(2)}) async-start(), calls=%async_computation.18 | async-start | bytes 10321920 | tf_op jit(solution)/shard_map/reduce_scatter | solution.py:287
  1344.4 575.5 %all-reduce.17.cloned.1.call-start = ((), (), s32[]{:S(2)}) async-start(), calls=%async_computation.29 | async-start | bytes 15728640 | tf_op jit(solution)/shard_map/psum | solution.py:170
  (104 other events, 979.5 us)
Sparse Core Ops, SparseCore 0:
  9.9 36.3 all-gather.7
  48.3 35.1 all-gather.9
  235.1 274.0 all-reduce.14
  511.0 56.5 all-gather.13
  569.3 57.7 all-gather.11
  628.8 57.7 all-gather.15
  748.1 274.1 all-reduce.12
  1068.4 35.6 reduce-scatter.39
  1107.7 36.7 reduce-scatter.35
  1147.5 36.7 reduce-scatter.33
  1187.9 36.7 reduce-scatter.37
  1227.8 37.3 reduce-scatter.43
  1268.4 37.3 reduce-scatter.41
  1309.1 46.8 reduce-scatter.25
  1359.3 46.8 reduce-scatter.23
  1409.7 75.0 reduce-scatter.31
  1488.6 75.0 reduce-scatter.29
  1567.2 75.0 reduce-scatter.27
  1645.0 274.8 all-reduce.16
where the time goes:
time: 1990 us; the launch traced here: 1980 us
  waiting for transfers between devices  1260 us (63%)
  matrix products  341 us (17%)
  blocking collectives  131 us (7%)
  other arithmetic  119 us (6%)
  local copies, waits for them, and re-layouts  107 us (5%)
    psum x1, waiting for transfers between devices, per_device(): lax.psum(jnp.dot(activation, full_down, preferred_element_type=jnp.float3...  275 us
    psum x1, waiting for transfers between devices, per_device(): lax.psum(outer_back(grad_gate, full_gate) + outer_back(grad_up, full_up),...  274 us
    psum x1, waiting for transfers between devices, per_device(): lax.psum(jnp.dot(attended_low, full_out, preferred_element_type=jnp.float...  264 us
    dot_general x14, matrix products, inner_rows(): lax.dot_general(left, right, (((0,), (0,)), ((), ())), preferred_element_...  92.7 us
    dot_general x14, matrix products, outer_back(): lax.dot_general(left, right, (((1,), (1,)), ((), ())), preferred_element_...  77.5 us
    reduce_scatter x1, waiting for transfers between devices, per_device(): lax.psum_scatter(totals[8].astype(jnp.bfloat16), 'ctx', scatter_dimension...  76.6 us
    reduce_scatter x1, waiting for transfers between devices, per_device(): lax.psum_scatter(totals[7].astype(jnp.bfloat16), 'ctx', scatter_dimension...  76.2 us
    reduce_scatter x1, waiting for transfers between devices, per_device(): lax.psum_scatter(totals[6].astype(jnp.bfloat16), 'ctx', scatter_dimension...  75.7 us
  transfers between devices with their start and end apart: 19, of which 12 were waited for; matrix products, arithmetic and copies ran while one was open for 21% of the time, Pallas kernels for 0%

commit v1 on v0

v1 whole, which is shorter than its diff:
```python
import jax
import jax.numpy as jnp
from jax import lax
from jax.sharding import PartitionSpec as P

HD = 80
WINDOW = 4096

EPSILON = 1e-05
THETA_BASE = 10000.0
NEGATIVE = -1e30
LOW = jnp.bfloat16


def dot(left, right, a, b):
    return lax.dot_general(
        left, right, (((a,), (b,)), ((), ())), preferred_element_type=jnp.float32
    )


def tables(positions, width):
    half = width // 2
    freq = THETA_BASE ** (-jnp.arange(half, dtype=jnp.float32) * 2.0 / width)
    angle = positions.astype(jnp.float32)[:, None] * freq[None, :]
    return (jnp.cos(angle)[None, :, None, :], jnp.sin(angle)[None, :, None, :])


def rotate(values, cosine, sine):
    half = values.shape[-1] // 2
    first = values[..., :half]
    second = values[..., half:]
    return jnp.concatenate(
        [first * cosine - second * sine, second * cosine + first * sine], axis=-1
    )


def take_chunk(rows, index, size):
    return lax.dynamic_slice_in_dim(rows, index * size, size, axis=0)


def line_scatter(partial):
    n = lax.axis_size("head")
    z = lax.axis_index("head")
    size = partial.shape[0] // n
    up = down = None
    for step in range(n - 1):
        rising = take_chunk(partial, n - 1 - step + z, size)
        falling = take_chunk(partial, step + z - (n - 1), size)
        if step:
            rising = (rising.astype(jnp.float32) + up.astype(jnp.float32)).astype(LOW)
            falling = (falling.astype(jnp.float32) + down.astype(jnp.float32)).astype(LOW)
        up = lax.ppermute(rising, "head", [(i, i + 1) for i in range(step + 1)])
        down = lax.ppermute(
            falling, "head", [(i, i - 1) for i in range(n - 1 - step, n)]
        )
    mine = take_chunk(partial, z, size).astype(jnp.float32)
    return mine + up.astype(jnp.float32) + down.astype(jnp.float32)


def line_gather(chunk):
    n = lax.axis_size("head")
    z = lax.axis_index("head")
    size = chunk.shape[0]
    ups, downs = [], []
    up = down = chunk
    for step in range(n - 1):
        up = lax.ppermute(up, "head", [(i, i + 1) for i in range(step, n - 1)])
        down = lax.ppermute(down, "head", [(i, i - 1) for i in range(1, n - step)])
        ups.append(up)
        downs.append(down)
    whole = jnp.zeros((n * size,) + chunk.shape[1:], chunk.dtype)
    whole = lax.dynamic_update_slice_in_dim(whole, chunk, z * size, axis=0)
    for step in range(n - 1):
        got = jnp.where(z > step, ups[step], downs[n - 2 - step])
        place = lax.rem(z - 1 - step + n, n)
        whole = lax.dynamic_update_slice_in_dim(whole, got, place * size, axis=0)
    return whole


def norm_scale(values):
    return lax.rsqrt(jnp.mean(values * values, axis=-1, keepdims=True) + EPSILON)


def norm_back(grad, gain, normed, scale):
    scaled = grad * gain
    return scale * (scaled - normed * jnp.mean(scaled * normed, axis=-1, keepdims=True))


def per_device(
    tokens,
    lengths,
    cotangent,
    attn_gain,
    query_weight,
    key_weight,
    value_weight,
    out_weight,
    ffn_gain,
    gate_weight,
    up_weight,
    down_weight,
):
    micro_count, seq_count, local_tokens, width = tokens.shape
    z = lax.axis_index("head")
    lines = lax.axis_size("head")
    q_cols = query_weight.shape[1]
    kv_cols = key_weight.shape[1]
    units = gate_weight.shape[1]

    qkv_shard = jnp.concatenate([query_weight, key_weight, value_weight], axis=1)
    full_qkv = lax.all_gather(qkv_shard, "ctx", axis=0, tiled=True)
    gains = lax.all_gather(jnp.stack([attn_gain, ffn_gain]), "ctx", axis=1, tiled=True)
    gain_attn = gains[0].astype(jnp.float32)
    gain_ffn = gains[1].astype(jnp.float32)
    full_out = lax.all_gather(out_weight.T, "ctx", axis=0, tiled=True)
    full_gate = lax.all_gather(gate_weight, "ctx", axis=0, tiled=True)
    full_up = lax.all_gather(up_weight, "ctx", axis=0, tiled=True)
    full_down = lax.all_gather(down_weight.T, "ctx", axis=0, tiled=True)

    local_heads = q_cols // HD
    local_groups = kv_cols // HD
    group_size = local_heads // local_groups
    span_total = local_tokens * lax.axis_size("ctx")
    first_slot = lax.axis_index("ctx") * local_tokens
    query_slots = first_slot + jnp.arange(local_tokens)
    key_slots = jnp.arange(span_total)
    cosine, sine = tables(query_slots, HD)
    scale = HD ** (-0.5)
    piece_rows = seq_count * local_tokens
    rows = micro_count * piece_rows
    chunk = piece_rows // lines

    flat = tokens.reshape(rows, width)
    resid = flat.astype(jnp.float32)
    normed_one = resid * norm_scale(resid)
    input_one = (normed_one * gain_attn).astype(LOW)
    qkv = dot(input_one, full_qkv, 1, 0)
    batch = micro_count * seq_count
    query_rot = rotate(
        qkv[:, :q_cols].reshape(batch, local_tokens, local_heads, HD), cosine, sine
    ).astype(LOW)
    key_rot = rotate(
        qkv[:, q_cols : q_cols + kv_cols].reshape(batch, local_tokens, local_groups, HD),
        cosine,
        sine,
    ).astype(LOW)
    value_low = qkv[:, q_cols + kv_cols :].astype(LOW)
    kv = jnp.concatenate([key_rot.reshape(rows, kv_cols), value_low], axis=1)
    kv_all = lax.all_gather(
        kv.reshape(batch, local_tokens, 2 * kv_cols), "ctx", axis=1, tiled=True
    )

    live = (
        query_slots[None, None, :] < lengths[:, :, None]
    ).astype(jnp.float32).reshape(rows, 1)
    grad_out = (cotangent.reshape(rows, width).astype(jnp.float32) * live).astype(LOW)

    pieces = range(micro_count)
    saved = []
    hidden_parts = []
    for piece in pieces:
        seqs = slice(piece * seq_count, (piece + 1) * seq_count)
        query = query_rot[seqs].reshape(
            seq_count, local_tokens, local_groups, group_size, HD
        )
        key_all = kv_all[seqs, :, :kv_cols].reshape(seq_count, span_total, local_groups, HD)
        value_all = kv_all[seqs, :, kv_cols:].reshape(seq_count, span_total, local_groups, HD)
        allowed = (
            (key_slots[None, None, :] <= query_slots[None, :, None])
            & (query_slots[None, :, None] - key_slots[None, None, :] < WINDOW)
            & (key_slots[None, None, :] < lengths[piece][:, None, None])
        )[:, None, None]
        scores = (
            jnp.einsum("stkgd,spkd->skgtp", query, key_all, preferred_element_type=jnp.float32)
            * scale
        )
        scores = jnp.where(allowed, scores, NEGATIVE)
        top_score = jnp.max(scores, axis=-1, keepdims=True)
        exponent = jnp.exp(scores - top_score)
        total_weight = jnp.sum(exponent, axis=-1, keepdims=True)
        probs_low = (exponent / total_weight).astype(LOW)
        log_total = top_score + jnp.log(total_weight)
        attended = jnp.einsum(
            "skgtp,spkd->stkgd", probs_low, value_all, preferred_element_type=jnp.float32
        )
        attended_low = attended.reshape(piece_rows, q_cols).astype(LOW)
        saved.append((query, key_all, value_all, allowed, log_total, attended_low))
        branch = dot(attended_low, full_out, 1, 1).astype(LOW)
        summed = line_scatter(branch)
        piece_tokens = take_chunk(flat[piece * piece_rows : (piece + 1) * piece_rows], z, chunk)
        hidden_parts.append(piece_tokens.astype(jnp.float32) + summed)

    inputs_two, mixed_parts, grads_two = [], [], []
    acts, grad_gates, grad_ups = [], [], []
    grad_hidden_parts, gain_two_terms, grads_low = [], [], []
    for piece in pieces:
        hidden = hidden_parts[piece]
        scale_two = norm_scale(hidden)
        normed_two = hidden * scale_two
        input_two = line_gather((normed_two * gain_ffn).astype(LOW))
        inputs_two.append(input_two)
        dy = grad_out[piece * piece_rows : (piece + 1) * piece_rows]
        gate = dot(input_two, full_gate, 1, 0)
        up = dot(input_two, full_up, 1, 0)
        sigmoid = jax.nn.sigmoid(gate)
        silu = gate * sigmoid
        act = (silu * up).astype(LOW)
        grad_act = dot(dy, full_down, 1, 0)
        grad_gate = (grad_act * up * sigmoid * (1.0 + gate * (1.0 - sigmoid))).astype(LOW)
        grad_up = (grad_act * silu).astype(LOW)
        acts.append(act)
        grad_gates.append(grad_gate)
        grad_ups.append(grad_up)
        grad_two = line_scatter(
            (dot(grad_gate, full_gate, 1, 1) + dot(grad_up, full_up, 1, 1)).astype(LOW)
        )
        ffn = line_scatter(dot(act, full_down, 1, 1).astype(LOW))
        mixed_parts.append(line_gather((hidden + ffn).astype(LOW)))
        gain_two_terms.append(jnp.sum(grad_two * normed_two, axis=0))
        grad_hidden = take_chunk(dy, z, chunk).astype(jnp.float32) + norm_back(
            grad_two, gain_ffn, normed_two, scale_two
        )
        grad_hidden_parts.append(grad_hidden)
        grads_low.append(line_gather(grad_hidden.astype(LOW)))

    act_all = jnp.concatenate(acts, axis=0)
    gate_back = jnp.concatenate(grad_gates, axis=0)
    up_back = jnp.concatenate(grad_ups, axis=0)
    two_all = jnp.concatenate(inputs_two, axis=0)
    hidden_low = jnp.concatenate(grads_low, axis=0)
    attended_all = jnp.concatenate([s[5] for s in saved], axis=0)

    def scatter_weight(term):
        return lax.psum_scatter(term, "ctx", scatter_dimension=0, tiled=True)

    down_grad = scatter_weight(dot(grad_out, act_all, 0, 0).astype(LOW))
    gate_grad = scatter_weight(dot(two_all, gate_back, 0, 0).astype(LOW))
    up_grad = scatter_weight(dot(two_all, up_back, 0, 0).astype(LOW))
    out_grad = scatter_weight(dot(hidden_low, attended_all, 0, 0).astype(LOW))

    query_parts, kv_parts = [], []
    for piece in pieces:
        query, key_all, value_all, allowed, log_total, attended_low = saved[piece]
        grad_att = dot(grads_low[piece], full_out, 1, 0).astype(LOW)
        grad_att = grad_att.reshape(seq_count, local_tokens, local_groups, group_size, HD)
        scores = (
            jnp.einsum("stkgd,spkd->skgtp", query, key_all, preferred_element_type=jnp.float32)
            * scale
        )
        scores = jnp.where(allowed, scores, NEGATIVE)
        probs = jnp.exp(scores - log_total)
        grad_probs = jnp.einsum(
            "stkgd,spkd->skgtp", grad_att, value_all, preferred_element_type=jnp.float32
        )
        row_dot = jnp.sum(probs * grad_probs, axis=-1, keepdims=True)
        grad_scores = (probs * (grad_probs - row_dot)).astype(LOW)
        grad_query = (
            jnp.einsum("skgtp,spkd->stkgd", grad_scores, key_all, preferred_element_type=jnp.float32)
            * scale
        )
        key_partial = (
            jnp.einsum("skgtp,stkgd->spkd", grad_scores, query, preferred_element_type=jnp.float32)
            * scale
        )
        value_partial = jnp.einsum(
            "skgtp,stkgd->spkd", probs.astype(LOW), grad_att, preferred_element_type=jnp.float32
        )
        query_parts.append(
            rotate(
                grad_query.reshape(seq_count, local_tokens, local_heads, HD), cosine, -sine
            ).reshape(piece_rows, q_cols).astype(LOW)
        )
        both = jnp.concatenate(
            [
                key_partial.reshape(seq_count, span_total, kv_cols),
                value_partial.reshape(seq_count, span_total, kv_cols),
            ],
            axis=-1,
        ).astype(LOW)
        kv_parts.append(both)
    kv_back = lax.psum_scatter(
        jnp.concatenate(kv_parts, axis=0), "ctx", scatter_dimension=1, tiled=True
    )
    key_back = rotate(
        kv_back[..., :kv_cols].astype(jnp.float32).reshape(batch, local_tokens, local_groups, HD),
        cosine,
        -sine,
    ).reshape(rows, kv_cols).astype(LOW)
    value_back = kv_back[..., kv_cols:].reshape(rows, kv_cols)
    qkv_back = jnp.concatenate(
        [jnp.concatenate(query_parts, axis=0), key_back, value_back], axis=1
    )
    qkv_grad = scatter_weight(dot(input_one, qkv_back, 0, 0).astype(LOW)).astype(jnp.float32)

    token_parts = []
    gain_one_terms = []
    for piece in pieces:
        span = slice(piece * piece_rows, (piece + 1) * piece_rows)
        grad_one = line_scatter(dot(qkv_back[span], full_qkv, 1, 1).astype(LOW))
        piece_tokens = take_chunk(flat[span], z, chunk).astype(jnp.float32)
        scale_one = norm_scale(piece_tokens)
        normed = piece_tokens * scale_one
        gain_one_terms.append(jnp.sum(grad_one * normed, axis=0))
        back = grad_hidden_parts[piece] + norm_back(grad_one, gain_attn, normed, scale_one)
        token_parts.append(line_gather(back.astype(LOW)))
    gain_terms = lax.psum(
        jnp.stack([sum(gain_one_terms), sum(gain_two_terms)]), ("head", "ctx")
    )
    gain_terms = lax.dynamic_slice_in_dim(
        gain_terms, lax.axis_index("ctx") * attn_gain.shape[0], attn_gain.shape[0], axis=1
    )
    mixed = jnp.stack(mixed_parts, axis=0).reshape(tokens.shape)
    token_grad = jnp.stack(token_parts, axis=0).reshape(tokens.shape).astype(jnp.float32)
    return (
        mixed,
        token_grad,
        gain_terms[0],
        qkv_grad[:, :q_cols],
        qkv_grad[:, q_cols : q_cols + kv_cols],
        qkv_grad[:, q_cols + kv_cols :],
        out_grad.T.astype(jnp.float32),
        gain_terms[1],
        gate_grad.astype(jnp.float32),
        up_grad.astype(jnp.float32),
        down_grad.T.astype(jnp.float32),
    )


def solution(mesh):
    placed = (
        P(None, None, "ctx", None),
        P(),
        P(None, None, "ctx", None),
        P("ctx"),
        P("ctx", "head"),
        P("ctx", "head"),
        P("ctx", "head"),
        P("head", "ctx"),
        P("ctx"),
        P("ctx", "head"),
        P("ctx", "head"),
        P("head", "ctx"),
    )
    return jax.shard_map(
        per_device,
        mesh=mesh,
        in_specs=placed,
        out_specs=(
            P(None, None, "ctx", None),
            P(None, None, "ctx", None),
            P("ctx"),
            P("ctx", "head"),
            P("ctx", "head"),
            P("ctx", "head"),
            P("head", "ctx"),
            P("ctx"),
            P("ctx", "head"),
            P("ctx", "head"),
            P("head", "ctx"),
        ),
        check_vma=False,
    )
```

time: 1990 us -> 1190 us (0.60)
  waiting for transfers between devices: 1260 us -> 350 us
  starting transfers between devices: 2.91 us -> 234 us
  blocking collectives: 131 us -> 53.9 us
  matrix products: 341 us -> 281 us
  other arithmetic: 119 us -> 144 us
    psum x3 -> x0, waiting for transfers between devices: 813 us -> none  [the longest x1 275 us: per_device(): lax.psum(jnp.dot(activation, full_down, preferred_element_type=jnp.float3...]
    reduce_scatter x5, waiting for transfers between devices: 255 us -> 0.01 us  [scatter_weight(): return lax.psum_scatter(term, 'ctx', scatter_dimension=0, tiled=True)]
    ppermute x0 -> x96, waiting for transfers between devices: none -> 246 us  [the longest x24 105 us: line_scatter(): up = lax.ppermute(rising, 'head', [(i, i + 1) for i in range(step + 1)])]
    ppermute x0 -> x96, starting transfers between devices: none -> 233 us  [the longest x24 107 us: line_scatter(): up = lax.ppermute(rising, 'head', [(i, i + 1) for i in range(step + 1)])]
    all_gather x5 -> x6, waiting for transfers between devices: 130 us -> 41.4 us  [the longest x1 24.2 us: per_device(): full_qkv = lax.all_gather(qkv_shard, 'ctx', axis=0, tiled=True)]
    all_gather x6 -> x1, blocking collectives: 80.8 us -> 10.4 us  [per_device(): lax.all_gather(jnp.stack([attn_gain, ffn_gain]), 'ctx', axis=1, tiled=True)]
    dot_general x52 -> x34, matrix products: 324 us -> 263 us  [the longest x24 182 us: dot(): lax.dot_general(left, right, (((a,), (b,)), ((), ())), preferred_element_...]
    unnamed x2 -> x0, blocking collectives: 49.9 us -> none
  transfers between devices with their start and end apart: 19 -> 108, of which waited for: 12 -> 41; matrix products, arithmetic and copies ran while one was open for 21% -> 34% of each run, Pallas kernels for 0% -> 0%
where the time goes in v1:
time: 1190 us; the launch traced here: 1170 us
  waiting for transfers between devices  350 us (29%)
  matrix products  281 us (24%)
  starting transfers between devices  234 us (20%)
  other arithmetic  144 us (12%)
  local copies, waits for them, and re-layouts  91.3 us (8%)
  blocking collectives  53.9 us (5%)
  between operations  17.8 us (1%)
    dot_general x24, matrix products, dot(): lax.dot_general(left, right, (((a,), (b,)), ((), ())), preferred_element_...  182 us
    ppermute x24, starting transfers between devices, line_scatter(): up = lax.ppermute(rising, 'head', [(i, i + 1) for i in range(step + 1)])  107 us
    ppermute x24, waiting for transfers between devices, line_scatter(): up = lax.ppermute(rising, 'head', [(i, i + 1) for i in range(step + 1)])  105 us
    ppermute x24, waiting for transfers between devices, line_gather(): down = lax.ppermute(down, 'head', [(i, i - 1) for i in range(1, n - step)])  82.3 us
    ppermute x24, starting transfers between devices, line_gather(): up = lax.ppermute(up, 'head', [(i, i + 1) for i in range(step, n - 1)])  72.4 us
    unnamed x13, waiting for transfers between devices  62.7 us
    ppermute x24, waiting for transfers between devices, line_scatter(): lax.ppermute(falling, 'head', [(i, i - 1) for i in range(n - 1 - step, n)])  58.6 us
    psum x1, blocking collectives, per_device(): lax.psum(jnp.stack([sum(gain_one_terms), sum(gain_two_terms)]), ('head',...  43.5 us
  transfers between devices with their start and end apart: 108, of which 41 were waited for; matrix products, arithmetic and copies ran while one was open for 34% of the time, Pallas kernels for 0%

profile of v1, /device:TPU:0, one launch (start us, length us, event | category | flops | bytes accessed | tf_op | source)
XLA Modules:
  0.0 1172.2 jit_solution(16166512935168286849)
XLA Ops:
  31.1 24.2 %all-gather.8.cloned.1.call-done = bf16[2560,960]{1,0:T(8,128)(2,1)} async-done(((bf16[320,960]{1,0:T(8,128)(2,1)}), bf16[2560,960]{1,0:T(8,128)(2,1)}) %all-gather.8.cloned.1.call-update) | async-done | bytes 4915216 | tf_op jit(solution)/shard_map/all_gather | solution.py:111
  89.2 17.1 %all-gather.10.cloned.1.call-done = bf16[4,1536,320]{2,0,1:T(4,128)(2,1)} async-done(((bf16[4,192,320]{2,0,1:T(4,128)(2,1)}), bf16[4,1536,320]{2,0,1:T(4,128)(2,1)}) %all-gather.10.cloned.1.call-update) | async-done | bytes 3932176 | tf_op jit(solution)/shard_map/all_gather | solution.py:149
  106.3 10.9 fusion.99
  255.1 13.3 %collective-permute-done.26 = bf16[96,2560]{1,0:T(8,128)(2,1)S(1)} collective-permute-done((bf16[96,2560]{1,0:T(8,128)(2,1)S(1)}, bf16[96,2560]{1,0:T(8,128)(2,1)S(1)}, u32[]{:S(2)}, u32[]{:S(2)}) %collective-permute-start.26) | collective-permute-done | bytes 491552 | tf_op jit(solution)/shard_map/ppermute | solution.py:52
  295.4 10.7 fusion.95
  337.8 10.5 fusion.110
  348.3 12.6 %multiply_convert_fusion = (bf16[384,1728]{0,1:T(8,128)(2,1)S(1)}, bf16[384,1728]{0,1:T(8,128)(2,1)S(1)}, bf16[384,1728]{0,1:T(8,128)(2,1)}) fusion(f32[384,1728]{0,1:T(8,128)} %fusion.93, f32[384,1728]{0,1:T(8,128)} %fusion.110, bf16[384,2560]{1,0:T(8,128)(2,1)} %select_dynamic-update-slice_fusion.6, bf16[2560,1728]{1,0:T(8,128)(2,1)} %all-gather.14.cloned.1.call-done), kind=kOutput, calls=%fused_computation.75 | convolution fusion | flops 3407339520 | bytes 20103168 | tf_op jit(solution)/shard_map/dot_general | solution.py:16
  385.7 10.5 fusion.109
  396.2 12.6 %multiply_convert_fusion.2 = (bf16[384,1728]{0,1:T(8,128)(2,1)S(1)}, bf16[384,1728]{0,1:T(8,128)(2,1)S(1)}, bf16[384,1728]{0,1:T(8,128)(2,1)}) fusion(f32[384,1728]{0,1:T(8,128)} %fusion.95, f32[384,1728]{0,1:T(8,128)} %fusion.109, bf16[384,2560]{1,0:T(8,128)(2,1)} %select_dynamic-update-slice_fusion.9, bf16[2560,1728]{1,0:T(8,128)(2,1)} %all-gather.14.cloned.1.call-done), kind=kOutput, calls=%fused_computation.77 | convolution fusion | flops 3407339520 | bytes 20103168 | tf_op jit(solution)/shard_map/dot_general | solution.py:16
  447.0 12.3 %collective-permute-start.62 = (bf16[96,2560]{1,0:T(8,128)(2,1)S(1)}, bf16[96,2560]{1,0:T(8,128)(2,1)S(1)}, u32[]{:S(2)}, u32[]{:S(2)}) collective-permute-start(bf16[96,2560]{1,0:T(8,128)(2,1)S(1)} %get-tuple-element.143), channel_id=1, source_target_pairs={{0,1},{1,2},{2,3},{4,5},{5,6},{6,7},{8,9},{9,10},{10,11},{12,13},{... | collective-permute-start | bytes 1474568 | tf_op jit(solution)/shard_map/ppermute | solution.py:52
  563.1 12.1 %fusion.3 = (f32[2,2,4,192]{3,2,1,0:T(4,128)S(1)}, f32[2,2,1536,192,4]{2,3,4,1,0:T(8,128)}) fusion(f32[2,2,4,192,1536]{4,3,2,1,0:T(8,128)} %get-tuple-element.197, f32[2,2,4,192]{3,2,1,0:T(4,128)S(1)} %bitcast.270, bf16[2,1536,2,80,1]{1,3,4,2,0:T(8,128)(2,1)S(1)} %bitcast.258, bf16[2,192,2,4,80]{1,4,3,2,0:T(8,128)(2,1)S(1)} %copy.173), kind=kOutput, calls=%fused_computation.7 | convolution fusion | flops 769127424 | bytes 39247872 | tf_op jit(solution)/shard_map/stkgd,spkd->skgtp/dot_general | solution.py:252
  591.4 12.1 %fusion = (f32[2,2,4,192]{3,2,1,0:T(4,128)S(1)}, f32[2,2,1536,192,4]{2,3,4,1,0:T(8,128)}) fusion(f32[2,2,4,192,1536]{4,3,2,1,0:T(8,128)} %get-tuple-element.195, f32[2,2,4,192]{3,2,1,0:T(4,128)S(1)} %bitcast.267, bf16[2,1536,2,80,1]{1,3,4,2,0:T(8,128)(2,1)S(1)} %bitcast.256, bf16[2,192,2,4,80]{1,4,3,2,0:T(8,128)(2,1)S(1)} %copy.177), kind=kOutput, calls=%fused_computation.2 | convolution fusion | flops 769127424 | bytes 39247872 | tf_op jit(solution)/shard_map/stkgd,spkd->skgtp/dot_general | solution.py:252
  612.6 13.0 %fusion.5 = bf16[2,2,4,192,1536]{4,3,2,1,0:T(8,128)(2,1)S(1)} fusion(f32[2,2,1536,192,4]{2,3,4,1,0:T(8,128)} %get-tuple-element.201, f32[2,2,4,192,1536]{4,3,2,1,0:T(8,128)} %get-tuple-element.197, f32[2,2,4,192]{3,2,1,0:T(4,128)S(1)} %get-tuple-element.200, f32[2,2,4,192]{3,2,1,0:T(4,128)S(1)} %bitcast.272), kind=kLoop, calls=%fused_computation.9 | loop fusion | flops 18874368 | bytes 47210496 | tf_op jit(solution)/shard_map/convert_element_type | solution.py:256
  634.2 13.0 %fusion.2 = bf16[2,2,4,192,1536]{4,3,2,1,0:T(8,128)(2,1)S(1)} fusion(f32[2,2,1536,192,4]{2,3,4,1,0:T(8,128)} %get-tuple-element.199, f32[2,2,4,192,1536]{4,3,2,1,0:T(8,128)} %get-tuple-element.195, f32[2,2,4,192]{3,2,1,0:T(4,128)S(1)} %get-tuple-element.198, f32[2,2,4,192]{3,2,1,0:T(4,128)S(1)} %bitcast.269), kind=kLoop, calls=%fused_computation.4 | loop fusion | flops 18874368 | bytes 47210496 | tf_op jit(solution)/shard_map/convert_element_type | solution.py:256
  660.6 13.3 %maximum_maximum_fusion = bf16[4,1536,320]{2,0,1:T(4,128)(2,1)} fusion(bf16[2,1536,160]{2,0,1:T(2,128)(2,1)} %copy.185, bf16[2,1536,160]{2,0,1:T(2,128)(2,1)} %copy.184, bf16[2,1536,160]{2,0,1:T(2,128)(2,1)S(1)} %copy.182, bf16[2,1536,160]{2,0,1:T(2,128)(2,1)S(1)} %copy.181), kind=kLoop, calls=%fused_computation.39 | loop fusion | flops 15728640 | bytes 7864320 | tf_op jit(solution)/shard_map/concatenate | solution.py:282
  704.9 60.4 %all-reduce.3.cloned.1.call-done = bf16[4,1536,320]{2,0,1:T(4,128)(2,1)} async-done(((bf16[4,1536,320]{2,0,1:T(4,128)(2,1)}), bf16[4,1536,320]{2,0,1:T(4,128)(2,1)}) %all-reduce.3.cloned.1.call-update) | async-done | bytes 3932176
  768.4 10.5 convolution_convert_fusion.3
  780.4 12.0 %convolution_convert_fusion.1 = bf16[2560,1728]{1,0:T(8,128)(2,1)} fusion(bf16[384,1728]{0,1:T(8,128)(2,1)S(1)} %copy-done.60, bf16[384,1728]{0,1:T(8,128)(2,1)} %copy-done.61, bf16[384,2560]{1,0:T(8,128)(2,1)} %select_dynamic-update-slice_fusion.6, bf16[384,2560]{1,0:T(8,128)(2,1)} %select_dynamic-update-slice_fusion.9), kind=kOutput, calls=%fused_computation.23 | convolution fusion | flops 6812368896 | bytes 15433728 | tf_op jit(solution)/shard_map/dot_general | solution.py:16
  793.7 11.6 convolution_convert_fusion.2
  870.9 12.4 %collective-permute-done.17 = bf16[96,2560]{1,0:T(8,128)(2,1)S(1)} collective-permute-done((bf16[96,2560]{1,0:T(8,128)(2,1)S(1)}, bf16[96,2560]{1,0:T(8,128)(2,1)S(1)}, u32[]{:S(2)}, u32[]{:S(2)}) %collective-permute-start.17) | collective-permute-done | bytes 491552 | tf_op jit(solution)/shard_map/ppermute | solution.py:53
  927.8 12.2 %convolution_convert_fusion = bf16[2560,1728]{1,0:T(8,128)(2,1)} fusion(bf16[768,2560]{1,0:T(8,128)(2,1)} %fusion.18, bf16[384,1728]{0,1:T(8,128)(2,1)} %get-tuple-element.116, bf16[384,1728]{0,1:T(8,128)(2,1)} %get-tuple-element.113), kind=kOutput, calls=%fused_computation.22 | convolution fusion | flops 6804504576 | bytes 15433728 | tf_op jit(solution)/shard_map/dot_general | solution.py:16
  1023.7 17.6 %collective-permute-done.89 = bf16[96,2560]{1,0:T(8,128)(2,1)S(1)} collective-permute-done((bf16[96,2560]{1,0:T(8,128)(2,1)S(1)}, bf16[96,2560]{1,0:T(8,128)(2,1)S(1)}, u32[]{:S(2)}, u32[]{:S(2)}) %collective-permute-start.89) | collective-permute-done | bytes 491552 | tf_op jit(solution)/shard_map/ppermute | solution.py:53
  1041.3 10.5 collective-permute-done.77
  1085.6 43.5 %psum.7 = f32[2,2560]{1,0:T(2,128)S(1)} all-reduce(f32[2,2560]{1,0:T(2,128)S(1)} %pad_maximum_fusion.13), channel_id=1, replica_groups=mesh['ctx'=8,'head'=4] {'head','ctx'}, use_global_device_ids=true, to_apply=%region_20.21 | all-reduce | flops 5120 | bytes 40960 | tf_op jit(solution)/shard_map/psum | solution.py:306
  (570 shorter events, 765.4 us)
Async XLA Ops:
  7.2 48.1 %all-gather.8.cloned.1.call-start = ((), (), s32[]{:S(2)}) async-start(), calls=%async_computation.5 | async-start | bytes 5898240 | tf_op jit(solution)/shard_map/all_gather | solution.py:111
  11.3 95.0 %all-gather.10.cloned.1.call-start = ((), (), s32[]{:S(2)}) async-start(), calls=%async_computation.6 | async-start | bytes 5308416 | tf_op jit(solution)/shard_map/all_gather | solution.py:149
  67.3 124.3 %all-gather.12.cloned.1.call-start = ((), (), s32[]{:S(2)}) async-start(), calls=%async_computation.7 | async-start | bytes 3686400 | tf_op jit(solution)/shard_map/all_gather | solution.py:115
  68.0 227.4 %all-gather.18.cloned.1.call-start = ((), (), s32[]{:S(2)}) async-start(), calls=%async_computation.10 | async-start | bytes 10321920 | tf_op jit(solution)/shard_map/all_gather | solution.py:118
  68.6 269.2 %all-gather.16.cloned.1.call-start = ((), (), s32[]{:S(2)}) async-start(), calls=%async_computation.9 | async-start | bytes 10321920 | tf_op jit(solution)/shard_map/all_gather | solution.py:117
  69.2 279.1 %all-gather.14.cloned.1.call-start = ((), (), s32[]{:S(2)}) async-start(), calls=%async_computation.8 | async-start | bytes 10321920 | tf_op jit(solution)/shard_map/all_gather | solution.py:116
  69.7 695.5 %all-reduce.3.cloned.1.call-start = ((), (), s32[]{:S(2)}) async-start(), calls=%async_computation.16 | async-start | bytes 9437184
  322.5 58.4 %collective-permute-start.9 = (bf16[96,2560]{1,0:T(8,128)(2,1)}, bf16[96,2560]{1,0:T(8,128)(2,1)}, u32[]{:S(2)}, u32[]{:S(2)}) collective-permute-start(bf16[96,2560]{1,0:T(8,128)(2,1)} %collective-permute-done.8), channel_id=1, source_target_pairs={{1,0},{5,4},{9,8},{13,12},{17,16},{21,20},{25,24},{29,28}} | collective-permute-start | bytes 1474568 | tf_op jit(solution)/shard_map/ppermute | solution.py:68
  323.8 61.0 %collective-permute-start.11 = (bf16[96,2560]{1,0:T(8,128)(2,1)}, bf16[96,2560]{1,0:T(8,128)(2,1)}, u32[]{:S(2)}, u32[]{:S(2)}) collective-permute-start(bf16[96,2560]{1,0:T(8,128)(2,1)} %collective-permute-done.10), channel_id=1, source_target_pairs={{2,3},{6,7},{10,11},{14,15},{18,19},{22,23},{26,27},{30,31}} | collective-permute-start | bytes 1474568 | tf_op jit(solution)/shard_map/ppermute | solution.py:67
  375.9 50.0 %collective-permute-start.60 = (bf16[96,2560]{1,0:T(8,128)(2,1)S(1)}, bf16[96,2560]{1,0:T(8,128)(2,1)S(1)}, u32[]{:S(2)}, u32[]{:S(2)}) collective-permute-start(bf16[96,2560]{1,0:T(8,128)(2,1)S(1)} %get-tuple-element.145), channel_id=1, source_target_pairs={{0,1},{4,5},{8,9},{12,13},{16,17},{20,21},{24,25},{28,29}} | collective-permute-start | bytes 1474568 | tf_op jit(solution)/shard_map/ppermute | solution.py:52
  380.2 65.8 %collective-permute-start.63 = (bf16[96,2560]{1,0:T(8,128)(2,1)S(1)}, bf16[96,2560]{1,0:T(8,128)(2,1)S(1)}, u32[]{:S(2)}, u32[]{:S(2)}) collective-permute-start(bf16[96,2560]{1,0:T(8,128)(2,1)S(1)} %get-tuple-element.146), channel_id=1, source_target_pairs={{3,2},{7,6},{11,10},{15,14},{19,18},{23,22},{27,26},{31,30}} | collective-permute-start | bytes 1474568 | tf_op jit(solution)/shard_map/ppermute | solution.py:53
  545.9 38.5 %collective-permute-start.69 = (bf16[96,2560]{1,0:T(8,128)(2,1)}, bf16[96,2560]{1,0:T(8,128)(2,1)}, u32[]{:S(2)}, u32[]{:S(2)}) collective-permute-start(bf16[96,2560]{1,0:T(8,128)(2,1)} %collective-permute-done.68), channel_id=1, source_target_pairs={{1,0},{5,4},{9,8},{13,12},{17,16},{21,20},{25,24},{29,28}} | collective-permute-start | bytes 1474568 | tf_op jit(solution)/shard_map/ppermute | solution.py:68
  547.2 39.7 %collective-permute-start.71 = (bf16[96,2560]{1,0:T(8,128)(2,1)}, bf16[96,2560]{1,0:T(8,128)(2,1)}, u32[]{:S(2)}, u32[]{:S(2)}) collective-permute-start(bf16[96,2560]{1,0:T(8,128)(2,1)} %collective-permute-done.70), channel_id=1, source_target_pairs={{2,3},{6,7},{10,11},{14,15},{18,19},{22,23},{26,27},{30,31}} | collective-permute-start | bytes 1474568 | tf_op jit(solution)/shard_map/ppermute | solution.py:67
  674.0 460.0 %reduce-scatter.8.cloned.1.call-start = ((), (), s32[]{:S(2)}) async-start(), calls=%async_computation.12 | async-start | bytes 3686400 | tf_op jit(solution)/shard_map/reduce_scatter | solution.py:234
  682.3 470.6 %reduce-scatter.6.cloned.1.call-start = ((), (), s32[]{:S(2)}) async-start(), calls=%async_computation.11 | async-start | bytes 5898240 | tf_op jit(solution)/shard_map/reduce_scatter | solution.py:234
  779.0 377.8 %reduce-scatter.12.cloned.1.call-start = ((), (), s32[]{:S(2)}) async-start(), calls=%async_computation.14 | async-start | bytes 10321920 | tf_op jit(solution)/shard_map/reduce_scatter | solution.py:234
  792.4 367.1 %reduce-scatter.10.cloned.1.call-start = ((), (), s32[]{:S(2)}) async-start(), calls=%async_computation.13 | async-start | bytes 10321920 | tf_op jit(solution)/shard_map/reduce_scatter | solution.py:234
  805.3 357.0 %reduce-scatter.14.cloned.1.call-start = ((), (), s32[]{:S(2)}) async-start(), calls=%async_computation.15 | async-start | bytes 10321920 | tf_op jit(solution)/shard_map/reduce_scatter | solution.py:234
  940.8 78.2 %collective-permute-start.23 = (bf16[96,2560]{1,0:T(8,128)(2,1)}, bf16[96,2560]{1,0:T(8,128)(2,1)S(1)}, u32[]{:S(2)}, u32[]{:S(2)}) collective-permute-start(bf16[96,2560]{1,0:T(8,128)(2,1)} %collective-permute-done.22), channel_id=1, source_target_pairs={{2,3},{6,7},{10,11},{14,15},{18,19},{22,23},{26,27},{30,31}} | collective-permute-start | bytes 1474568 | tf_op jit(solution)/shard_map/ppermute | solution.py:67
  942.8 128.3 %collective-permute-start.47 = (bf16[96,2560]{1,0:T(8,128)(2,1)}, bf16[96,2560]{1,0:T(8,128)(2,1)S(1)}, u32[]{:S(2)}, u32[]{:S(2)}) collective-permute-start(bf16[96,2560]{1,0:T(8,128)(2,1)} %collective-permute-done.46), channel_id=1, source_target_pairs={{2,3},{6,7},{10,11},{14,15},{18,19},{22,23},{26,27},{30,31}} | collective-permute-start | bytes 1474568 | tf_op jit(solution)/shard_map/ppermute | solution.py:67
  1072.3 57.5 %collective-permute-start.82 = (bf16[96,2560]{1,0:T(8,128)(2,1)S(1)}, bf16[96,2560]{1,0:T(8,128)(2,1)}, u32[]{:S(2)}, u32[]{:S(2)}) collective-permute-start(bf16[96,2560]{1,0:T(8,128)(2,1)S(1)} %collective-permute-done.78), channel_id=1, source_target_pairs={{1,2},{2,3},{5,6},{6,7},{9,10},{10,11},{13,14},{14,15},{17,18},{18... | collective-permute-start | bytes 1474568 | tf_op jit(solution)/shard_map/ppermute | solution.py:67
  1078.9 52.3 %collective-permute-start.92 = (bf16[96,2560]{1,0:T(8,128)(2,1)S(1)}, bf16[96,2560]{1,0:T(8,128)(2,1)}, u32[]{:S(2)}, u32[]{:S(2)}) collective-permute-start(bf16[96,2560]{1,0:T(8,128)(2,1)S(1)} %collective-permute-done.91), channel_id=1, source_target_pairs={{1,0},{2,1},{5,4},{6,5},{9,8},{10,9},{13,12},{14,13},{17,16},{18,1... | collective-permute-start | bytes 1474568 | tf_op jit(solution)/shard_map/ppermute | solution.py:68
  1080.2 52.3 %collective-permute-start.94 = (bf16[96,2560]{1,0:T(8,128)(2,1)}, bf16[96,2560]{1,0:T(8,128)(2,1)}, u32[]{:S(2)}, u32[]{:S(2)}) collective-permute-start(bf16[96,2560]{1,0:T(8,128)(2,1)} %collective-permute-done.90), channel_id=1, source_target_pairs={{1,2},{2,3},{5,6},{6,7},{9,10},{10,11},{13,14},{14,15},{17,18},{18... | collective-permute-start | bytes 1474568 | tf_op jit(solution)/shard_map/ppermute | solution.py:67
  1084.3 51.7 %collective-permute-start.81 = (bf16[96,2560]{1,0:T(8,128)(2,1)}, bf16[96,2560]{1,0:T(8,128)(2,1)}, u32[]{:S(2)}, u32[]{:S(2)}) collective-permute-start(bf16[96,2560]{1,0:T(8,128)(2,1)} %collective-permute-done.80), channel_id=1, source_target_pairs={{1,0},{5,4},{9,8},{13,12},{17,16},{21,20},{25,24},{29,28}} | collective-permute-start | bytes 1474568 | tf_op jit(solution)/shard_map/ppermute | solution.py:68
  (155 other events, 3045.9 us)
Sparse Core Ops, SparseCore 0:
  11.4 43.8 all-gather.7
  67.4 38.9 all-gather.9
  108.2 32.8 all-gather.11
  142.9 57.7 all-gather.17
  202.3 57.7 all-gather.15
  261.8 57.7 all-gather.13
  674.1 91.0 all-reduce.2
  769.0 46.9 reduce-scatter.7
  819.8 56.5 reduce-scatter.5
  879.9 75.0 reduce-scatter.11
  959.0 75.0 reduce-scatter.9
  1037.6 75.1 reduce-scatter.13

commit v2 on v1

v2 whole, which is shorter than its diff:
```python
import functools

import jax
import jax.numpy as jnp
from jax import lax
from jax.experimental.layout import Layout, with_layout_constraint
from jax.experimental import pallas as pl
from jax.experimental.pallas import tpu as pltpu
from jax.sharding import PartitionSpec as P

HD = 80
WINDOW = 4096

EPSILON = 1e-05
THETA_BASE = 10000.0
NEGATIVE = -1e30
LOG2E = 1.4426950408889634
LOW = jnp.bfloat16
VMEM_LIMIT = 48 * 1024 * 1024
COST = 2


def dot(left, right, a, b):
    return lax.dot_general(
        left, right, (((a,), (b,)), ((), ())), preferred_element_type=jnp.float32
    )


def after(value, *others):
    if not others:
        return value
    return lax.optimization_barrier((value, others))[0]


def angles(positions):
    half = HD // 2
    freq = THETA_BASE ** (-jnp.arange(half, dtype=jnp.float32) * 2.0 / HD)
    angle = positions.astype(jnp.float32)[:, None] * freq[None, :]
    return jnp.cos(angle), jnp.sin(angle)


def add_low(*terms):
    return sum(term.astype(jnp.float32) for term in terms).astype(LOW)


def flip(bit):
    n = lax.axis_size("ctx")
    return [(i, i ^ bit) for i in range(n)]


def chip_bits():
    bits, bit = [], 2
    while bit < lax.axis_size("ctx"):
        bits.append(bit)
        bit *= 2
    return bits


def cube_gather(part, bits):
    own, places = part[None], [0]
    for bit in bits:
        got = lax.ppermute(own, "ctx", flip(bit))
        own = jnp.concatenate([own, got], axis=0)
        places = places + [place ^ (bit // 2) for place in places]
    order = [places.index(m) for m in range(len(places))]
    if order != sorted(order):
        own = jnp.stack([own[at] for at in order], axis=0)
    return own, lax.ppermute(own, "ctx", flip(1))


def line_bits():
    bits, bit = [], 1
    while bit < lax.axis_size("head"):
        bits.append(bit)
        bit *= 2
    return bits


def line_swap(value, bit):
    n = lax.axis_size("head")
    return lax.ppermute(value, "head", [(i, i ^ bit) for i in range(n)])


def line_place(z):
    place = z * 0
    for bit in line_bits():
        place = place * 2 + lax.rem(z // bit, 2)
    return place


class Scatter:
    def __init__(self, partial, *others):
        self.held = after(partial, *others)
        self.bits = line_bits()
        self.send()

    def send(self):
        half = self.held.shape[0] // 2
        mine = lax.rem(lax.axis_index("head") // self.bits[0], 2)
        self.landed = line_swap(
            take_chunk(self.held, 1 - mine, half).astype(LOW), self.bits[0]
        )
        self.kept = take_chunk(self.held, mine, half).astype(jnp.float32)
        self.bits = self.bits[1:]

    def land(self):
        self.held = self.kept + self.landed.astype(jnp.float32)

    def next(self, *others):
        self.landed = after(self.landed, *others)
        self.land()
        self.send()
        return self

    def finish(self, *others):
        while self.bits:
            self.next()
        self.landed = after(self.landed, *others)
        self.land()
        return self.held


class Gather:
    def __init__(self, chunk, *others):
        self.held = after(chunk, *others)
        self.bits = line_bits()[::-1]
        self.send()

    def send(self):
        self.mine = lax.rem(lax.axis_index("head") // self.bits[0], 2)
        self.landed = line_swap(self.held, self.bits[0])
        self.bits = self.bits[1:]

    def land(self):
        first = jnp.where(self.mine == 0, self.held, self.landed)
        second = jnp.where(self.mine == 0, self.landed, self.held)
        self.held = jnp.concatenate([first, second], axis=0)

    def next(self, *others):
        self.landed = after(self.landed, *others)
        self.land()
        self.send()
        return self

    def finish(self, *others):
        while self.bits:
            self.next()
        self.landed = after(self.landed, *others)
        self.land()
        return self.held


class ChainScatter:
    def __init__(self, partial, *others):
        self.partial = after(partial, *others)
        self.step = 0
        self.send()

    def block(self, z):
        n = lax.axis_size("head")
        size = self.partial.shape[0] // n
        return take_chunk(self.partial, line_place(jnp.clip(z, 0, n - 1)), size)

    def send(self):
        n = lax.axis_size("head")
        z = lax.axis_index("head")
        step = self.step
        rising = self.block(n - 1 - step + z)
        falling = self.block(step + z - (n - 1))
        if step:
            rising = add_low(rising, self.landed[0])
            falling = add_low(falling, self.landed[1])
        self.landed = (
            lax.ppermute(rising, "head", [(i, i + 1) for i in range(step + 1)]),
            lax.ppermute(falling, "head", [(i, i - 1) for i in range(n - 1 - step, n)]),
        )
        self.step += 1

    def next(self, *others):
        self.landed = (after(self.landed[0], *others), self.landed[1])
        self.send()
        return self

    def finish(self, *others):
        while self.step < lax.axis_size("head") - 1:
            self.next()
        mine = after(self.block(lax.axis_index("head")), *others)
        return sum(part.astype(jnp.float32) for part in (mine,) + self.landed)


class ChainGather:
    def __init__(self, chunk, *others):
        self.chunk = after(chunk, *others)
        self.landed = (self.chunk, self.chunk)
        self.got = []
        self.send()

    def send(self):
        n = lax.axis_size("head")
        step = len(self.got)
        self.landed = (
            lax.ppermute(self.landed[0], "head", [(i, i + 1) for i in range(step, n - 1)]),
            lax.ppermute(self.landed[1], "head", [(i, i - 1) for i in range(1, n - step)]),
        )
        self.got.append(self.landed)

    def next(self, *others):
        self.landed = (after(self.landed[0], *others), self.landed[1])
        self.send()
        return self

    def finish(self, *others):
        n = lax.axis_size("head")
        z = lax.axis_index("head")
        while len(self.got) < n - 1:
            self.next()
        size = self.chunk.shape[0]
        whole = jnp.zeros((n * size,) + self.chunk.shape[1:], self.chunk.dtype)
        whole = lax.dynamic_update_slice_in_dim(
            whole, after(self.chunk, *others), line_place(z) * size, axis=0
        )
        for step in range(n - 1):
            block = jnp.where(z > step, self.got[step][0], self.got[n - 2 - step][1])
            at = line_place(lax.rem(z - 1 - step + n, n)) * size
            whole = lax.dynamic_update_slice_in_dim(whole, block, at, axis=0)
        return whole


class Reduce:
    def __init__(self, own, other, bits):
        self.bits = bits[::-1]
        self.kept = own
        self.landed = lax.ppermute(other, "ctx", flip(1))

    def next(self, *others):
        landed = after(self.landed, *others)
        bit, self.bits = self.bits[0], self.bits[1:]
        half = self.kept.shape[0] // 2
        sent = add_low(self.kept[half:], landed[half:])
        self.kept = add_low(self.kept[:half], landed[:half])
        self.landed = lax.ppermute(sent, "ctx", flip(bit))

    def finish(self):
        while self.bits:
            self.next()
        return self.kept[0], self.landed[0]


def project_kernel(tokens_ref, gain_ref, weight_ref, cos_ref, ahead_ref, behind_ref, normed_ref, query_ref, kv_ref):
    values = tokens_ref[...].astype(jnp.float32)
    scale = lax.rsqrt(jnp.mean(values * values, axis=-1, keepdims=True) + EPSILON)
    normed = (values * scale * gain_ref[...]).astype(LOW)
    normed_ref[...] = normed
    out = dot(normed, weight_ref[...], 1, 0)
    local, padded = cos_ref.shape
    q_cols, kv_cols = query_ref.shape[1], kv_ref.shape[1]
    for start in range(0, out.shape[0], local):
        part = out[start : start + local]
        turned = (
            part * cos_ref[...]
            + pltpu.roll(part, padded - HD // 2, 1) * ahead_ref[...]
            + pltpu.roll(part, HD // 2, 1) * behind_ref[...]
        ).astype(LOW)
        query_ref[start : start + local, :] = turned[:, :q_cols]
        kv_ref[start : start + local, :] = turned[:, q_cols : q_cols + kv_cols]


def project(flat, gain, weight, cos, ahead, behind, pieces, q_cols, kv_cols):
    rows, width = flat.shape
    size = rows // pieces
    padded = weight.shape[1]
    whole = lambda shape: pl.BlockSpec(shape, lambda i: (0,) * len(shape))
    strip = lambda columns: pl.BlockSpec((size, columns), lambda i: (i, 0))
    return pl.pallas_call(
        project_kernel,
        grid=(pieces,),
        in_specs=[
            strip(width),
            whole((1, width)),
            whole((width, padded)),
            whole(cos.shape),
            whole(cos.shape),
            whole(cos.shape),
        ],
        out_specs=[strip(width), strip(q_cols), strip(kv_cols)],
        out_shape=[
            jax.ShapeDtypeStruct((rows, width), LOW),
            jax.ShapeDtypeStruct((rows, q_cols), LOW),
            jax.ShapeDtypeStruct((rows, kv_cols), LOW),
        ],
        compiler_params=pltpu.CompilerParams(vmem_limit_bytes=VMEM_LIMIT),
        cost_estimate=pl.CostEstimate(
            flops=2 * rows * width * padded,
            bytes_accessed=4 * rows * width + 2 * width * padded,
            transcendentals=0,
        ),
        name="project",
    )(flat, gain, weight, cos, ahead, behind)


def feed_kernel(input_ref, grad_ref, gate_ref, up_ref, down_ref, act_ref, grad_gate_ref, grad_up_ref):
    gate = dot(input_ref[...], gate_ref[...], 1, 0)
    up = dot(input_ref[...], up_ref[...], 1, 0)
    grad_act = dot(grad_ref[...], down_ref[...], 1, 0)
    sigmoid = jax.nn.sigmoid(gate)
    silu = gate * sigmoid
    act_ref[...] = (silu * up).astype(LOW)
    grad_gate_ref[...] = (grad_act * up * sigmoid * (1.0 + gate * (1.0 - sigmoid))).astype(LOW)
    grad_up_ref[...] = (grad_act * silu).astype(LOW)


def feed(inputs, grads, gate, up, down):
    rows, width = inputs.shape
    units = gate.shape[1]
    tile = 256
    whole = pl.BlockSpec((rows, width), lambda i: (0, 0))
    weight = pl.BlockSpec((width, tile), lambda i: (0, i))
    out = pl.BlockSpec((rows, tile), lambda i: (0, i))
    return pl.pallas_call(
        feed_kernel,
        grid=((units + tile - 1) // tile,),
        in_specs=[whole, whole, weight, weight, weight],
        out_specs=[out, out, out],
        out_shape=[jax.ShapeDtypeStruct((rows, units), LOW)] * 3,
        compiler_params=pltpu.CompilerParams(vmem_limit_bytes=VMEM_LIMIT),
        cost_estimate=pl.CostEstimate(
            flops=6 * rows * width * units // COST,
            bytes_accessed=(6 * width * units + 4 * rows * width + 6 * rows * units) // COST,
            transcendentals=0,
        ),
        name="feed",
    )(inputs, grads, gate, up, down)


def back_kernel(*refs):
    out_ref = refs[-1]
    count = (len(refs) - 1) // 2
    total = dot(refs[0][...], refs[count][...], 1, 1)
    for at in range(1, count):
        total += dot(refs[at][...], refs[count + at][...], 1, 1)
    out_ref[...] = total.astype(LOW)


def back_through(values, weights):
    rows, units = values[0].shape
    width = weights[0].shape[0]
    tile = 256
    count = len(values)
    return pl.pallas_call(
        back_kernel,
        grid=((width + tile - 1) // tile,),
        in_specs=[pl.BlockSpec((rows, units), lambda i: (0, 0))] * count
        + [pl.BlockSpec((tile, units), lambda i: (i, 0))] * count,
        out_specs=pl.BlockSpec((rows, tile), lambda i: (0, i)),
        out_shape=jax.ShapeDtypeStruct((rows, width), LOW),
        compiler_params=pltpu.CompilerParams(vmem_limit_bytes=VMEM_LIMIT),
        cost_estimate=pl.CostEstimate(
            flops=2 * count * rows * width * units // COST,
            bytes_accessed=(2 * count * (width + rows) * units + 2 * rows * width) // COST,
            transcendentals=0,
        ),
        name="back_through",
    )(*values, *weights)


def join_kernel(query_ref, kept_ref, landed_ref, cos_ref, ahead_ref, behind_ref, out_ref):
    q_cols, kv_cols = query_ref.shape[1], kept_ref.shape[1]
    local, padded = cos_ref.shape
    out_ref[:, :q_cols] = query_ref[...]
    for start in range(0, kept_ref.shape[0], local):
        rows = slice(start, start + local)
        part = kept_ref[rows, :].astype(jnp.float32) + landed_ref[rows, :].astype(jnp.float32)
        if padded > kv_cols:
            part = jnp.concatenate(
                [part, jnp.zeros((local, padded - kv_cols), jnp.float32)], axis=1
            )
        turned = (
            part * cos_ref[...]
            - pltpu.roll(part, padded - HD // 2, 1) * ahead_ref[...]
            - pltpu.roll(part, HD // 2, 1) * behind_ref[...]
        ).astype(LOW)
        out_ref[rows, q_cols : q_cols + kv_cols] = turned[:, :kv_cols]


def join_back(query, kept, landed, cos, ahead, behind):
    rows, q_cols = query.shape
    return pl.pallas_call(
        join_kernel,
        out_shape=jax.ShapeDtypeStruct((rows, q_cols + kept.shape[1]), LOW),
        compiler_params=pltpu.CompilerParams(vmem_limit_bytes=VMEM_LIMIT),
        cost_estimate=pl.CostEstimate(flops=0, bytes_accessed=8 * kept.size, transcendentals=0),
        name="join_back",
    )(query, kept, landed, cos, ahead, behind)


def stack_heads(block, group, per):
    return jnp.concatenate(
        [block[:, (group * per + h) * HD : (group * per + h + 1) * HD] for h in range(per)],
        axis=0,
    )


def key_block(own_ref, other_ref, at, column):
    return jnp.concatenate(
        [own_ref[at, :, column : column + HD], other_ref[at, :, column : column + HD]],
        axis=0,
    )


def key_limits(meta_ref, slots_ref, local):
    me, length = meta_ref[0], meta_ref[1 + pl.program_id(0)]
    pair = 2 * local
    full = lax.div(jnp.minimum(me * local + 1, length), pair)
    some = lax.div(jnp.minimum((me + 1) * local, length) + pair - 1, pair)
    limit = jnp.minimum(slots_ref[...], length - 1)
    row = lax.broadcasted_iota(jnp.int32, (pair, 1), 0)
    core = lax.rem(me, 2)
    within = jnp.where(row < local, core * local + row, (1 - core) * local + row - local)
    return me, length, full, some, limit, within


def keep_allowed(scores, base, within, limit, slots, window):
    place = base + within
    allowed = place <= limit
    if window:
        allowed = allowed & (slots - place < WINDOW)
    return jnp.where(allowed, scores, NEGATIVE)


def attend_kernel(meta_ref, slots_ref, query_ref, own_ref, other_ref, att_ref, lse_ref, stacked, total, *, groups, per, window):
    local = query_ref.shape[0]
    pair = 2 * local
    kv_cols = groups * HD
    me, _, full, some, limit, within = key_limits(meta_ref, slots_ref, local)
    if window:
        full = full * 0
    factor = HD ** (-0.5) * LOG2E
    for g in range(groups):
        stacked[g] = stack_heads(query_ref[...], g, per)
        total[g] = jnp.zeros(total.shape[1:], jnp.float32)

    def step(m, carry, masked):
        at = jnp.bitwise_xor(m, lax.div(me, 2))
        out = []
        for g in range(groups):
            top, weight = carry[g]
            keys = key_block(own_ref, other_ref, at, g * HD)
            values = key_block(own_ref, other_ref, at, kv_cols + g * HD)
            scores = dot(keys, stacked[g], 1, 1) * factor
            if masked:
                scores = keep_allowed(scores, m * pair, within, limit, slots_ref[...], window)
            higher = jnp.maximum(top, jnp.max(scores, axis=0, keepdims=True))
            probs = jnp.exp2(scores - higher)
            shrink = jnp.exp2(top - higher)
            total[g] = total[g] * shrink + dot(values, probs.astype(LOW), 0, 0)
            out.append(
                (higher, weight * shrink + jnp.sum(probs, axis=0, keepdims=True))
            )
        return tuple(out)

    row = (1, per * local)
    carry = tuple(
        (jnp.full(row, NEGATIVE, jnp.float32), jnp.zeros(row, jnp.float32))
        for _ in range(groups)
    )
    carry = lax.fori_loop(0, full, lambda m, c: step(m, c, False), carry)
    carry = lax.fori_loop(full, some, lambda m, c: step(m, c, True), carry)
    for g in range(groups):
        top, weight = carry[g]
        lse_ref[0, g : g + 1, :] = top + jnp.log2(weight)
        out = (total[g] / weight).T.astype(LOW)
        for h in range(per):
            at = (g * per + h) * HD
            att_ref[:, at : at + HD] = out[h * local : (h + 1) * local]


def attend_back_kernel(
    meta_ref, slots_ref, cos_ref, sin_ref, query_ref, own_ref, other_ref, att_ref, grad_ref, lse_ref,
    grad_query_ref, grad_own_ref, grad_other_ref, stacked, stacked_grad, total, row_dot, *, groups, per, window,
):
    local = query_ref.shape[0]
    pair = 2 * local
    kv_cols = groups * HD
    me, length, full, some, limit, within = key_limits(meta_ref, slots_ref, local)
    if window:
        full = full * 0
    scale = HD ** (-0.5)
    live = me * local < length
    full = jnp.where(live, full, 0)
    some = jnp.where(live, some, 0)
    chips = own_ref.shape[0]
    chip = lax.div(me, 2)

    for g in range(groups):
        stacked[g] = stack_heads(query_ref[...], g, per)
        grads = stack_heads(grad_ref[...], g, per)
        stacked_grad[g] = grads
        product = grads.astype(jnp.float32) * stack_heads(att_ref[...], g, per).astype(jnp.float32)
        row_dot[g : g + 1, :] = jnp.sum(product.T, axis=0, keepdims=True)
        total[g] = jnp.zeros(total.shape[1:], jnp.float32)

    def clear(m, carry):
        at = jnp.bitwise_xor(m, chip)
        grad_own_ref[at] = jnp.zeros(grad_own_ref.shape[1:], LOW)
        grad_other_ref[at] = jnp.zeros(grad_other_ref.shape[1:], LOW)
        return carry

    def step(m, carry, masked):
        at = jnp.bitwise_xor(m, chip)
        for g in range(groups):
            keys = key_block(own_ref, other_ref, at, g * HD)
            values = key_block(own_ref, other_ref, at, kv_cols + g * HD)
            scores = dot(keys, stacked[g], 1, 1) * (scale * LOG2E)
            if masked:
                scores = keep_allowed(scores, m * pair, within, limit, slots_ref[...], window)
            probs = jnp.exp2(scores - lse_ref[0, g : g + 1, :])
            grad_probs = dot(values, stacked_grad[g], 1, 1)
            grad_scores = (probs * (grad_probs - row_dot[g : g + 1, :])).astype(LOW)
            grad_values = dot(probs.astype(LOW), stacked_grad[g], 1, 0).astype(LOW)
            grad_keys = (dot(grad_scores, stacked[g], 1, 0) * scale).astype(LOW)
            total[g] += dot(keys, grad_scores, 0, 0)
            for column, grads in ((g * HD, grad_keys), (kv_cols + g * HD, grad_values)):
                grad_own_ref[at, :, column : column + HD] = grads[:local]
                grad_other_ref[at, :, column : column + HD] = grads[local:]
        return carry

    lax.fori_loop(0, full, lambda m, c: step(m, c, False), 0)
    lax.fori_loop(full, some, lambda m, c: step(m, c, True), 0)
    lax.fori_loop(some, chips, clear, 0)
    half = HD // 2
    cos, sin = cos_ref[...], sin_ref[...]
    for g in range(groups):
        grads = total[g] * scale
        first, second = grads[:half], grads[half:]
        turned = jnp.concatenate(
            [first * cos + second * sin, second * cos - first * sin], axis=0
        ).T.astype(LOW)
        for h in range(per):
            at = (g * per + h) * HD
            grad_query_ref[:, at : at + HD] = turned[h * local : (h + 1) * local]


def attention_specs(seqs, local, q_cols, kv_both, chips, groups, columns):
    meta = pl.BlockSpec(memory_space=pltpu.SMEM)
    whole = lambda shape: pl.BlockSpec(shape, lambda s: (0,) * len(shape))
    queries = pl.BlockSpec((local, q_cols), lambda s: (s, 0))
    keys = pl.BlockSpec((chips, local, kv_both), lambda s: (0, s, 0))
    lse = pl.BlockSpec((1, groups, columns), lambda s: (s, 0, 0))
    return meta, whole, queries, keys, lse


def attend(meta, slots, query, own, other, groups, window):
    seqs = meta.shape[0] - 1
    rows, q_cols = query.shape
    local = rows // seqs
    chips, _, kv_both = own.shape
    per = q_cols // HD // groups
    columns = per * local
    smem, whole, queries, keys, lse = attention_specs(
        seqs, local, q_cols, kv_both, chips, groups, columns
    )
    pairs = rows * q_cols // HD * 2 * chips * local
    return pl.pallas_call(
        functools.partial(attend_kernel, groups=groups, per=per, window=window),
        grid=(seqs,),
        in_specs=[smem, whole((1, columns)), queries, keys, keys],
        out_specs=[queries, lse],
        out_shape=[
            jax.ShapeDtypeStruct((rows, q_cols), LOW),
            jax.ShapeDtypeStruct((seqs, groups, columns), jnp.float32),
        ],
        scratch_shapes=[
            pltpu.VMEM((groups, columns, HD), LOW),
            pltpu.VMEM((groups, HD, columns), jnp.float32),
        ],
        compiler_params=pltpu.CompilerParams(vmem_limit_bytes=VMEM_LIMIT),
        cost_estimate=pl.CostEstimate(
            flops=12 * pairs * HD, bytes_accessed=4 * own.size, transcendentals=pairs
        ),
        name="attend",
    )(meta, slots, query, own, other)


def attend_back(meta, slots, cos, sin, query, own, other, att, grad, lse_rows, groups, window):
    seqs = meta.shape[0] - 1
    rows, q_cols = query.shape
    local = rows // seqs
    chips, _, kv_both = own.shape
    per = q_cols // HD // groups
    columns = per * local
    smem, whole, queries, keys, lse = attention_specs(
        seqs, local, q_cols, kv_both, chips, groups, columns
    )
    pairs = rows * q_cols // HD * 2 * chips * local
    return pl.pallas_call(
        functools.partial(attend_back_kernel, groups=groups, per=per, window=window),
        grid=(seqs,),
        in_specs=[
            smem, whole((1, columns)), whole(cos.shape), whole(cos.shape),
            queries, keys, keys, queries, queries, lse,
        ],
        out_specs=[queries, keys, keys],
        out_shape=[
            jax.ShapeDtypeStruct((rows, q_cols), LOW),
            jax.ShapeDtypeStruct(own.shape, LOW),
            jax.ShapeDtypeStruct(own.shape, LOW),
        ],
        scratch_shapes=[
            pltpu.VMEM((groups, columns, HD), LOW),
            pltpu.VMEM((groups, columns, HD), LOW),
            pltpu.VMEM((groups, HD, columns), jnp.float32),
            pltpu.VMEM((groups, columns), jnp.float32),
        ],
        compiler_params=pltpu.CompilerParams(vmem_limit_bytes=VMEM_LIMIT),
        cost_estimate=pl.CostEstimate(
            flops=30 * pairs * HD, bytes_accessed=8 * own.size, transcendentals=pairs
        ),
        name="attend_back",
    )(meta, slots, cos, sin, query, own, other, att, grad, lse_rows)


def take_chunk(rows, index, size):
    return lax.dynamic_slice_in_dim(rows, index * size, size, axis=0)


def norm_scale(values):
    return lax.rsqrt(jnp.mean(values * values, axis=-1, keepdims=True) + EPSILON)


def norm_back(grad, gain, normed, scale):
    scaled = grad * gain
    return scale * (scaled - normed * jnp.mean(scaled * normed, axis=-1, keepdims=True))


def per_device(
    tokens,
    lengths,
    cotangent,
    attn_gain,
    query_weight,
    key_weight,
    value_weight,
    out_weight,
    ffn_gain,
    gate_weight,
    up_weight,
    down_weight,
):
    micro_count, seq_count, local_tokens, width = tokens.shape
    place = line_place(lax.axis_index("head"))
    me = lax.axis_index("ctx")
    lines = lax.axis_size("head")
    q_cols = query_weight.shape[1]
    kv_cols = key_weight.shape[1]
    used = q_cols + 2 * kv_cols
    padded = (used + 2 + 127) // 128 * 128

    qkv_shard = jnp.concatenate(
        [
            query_weight,
            key_weight,
            value_weight,
            attn_gain[:, None],
            ffn_gain[:, None],
            jnp.zeros((query_weight.shape[0], padded - used - 2), LOW),
        ],
        axis=1,
    )
    full_qkv = lax.all_gather(qkv_shard, "ctx", axis=0, tiled=True)
    full_out = lax.all_gather(out_weight.T, "ctx", axis=0, tiled=True)
    full_gate = lax.all_gather(gate_weight, "ctx", axis=0, tiled=True)
    full_up = lax.all_gather(up_weight, "ctx", axis=0, tiled=True)
    full_down = lax.all_gather(down_weight.T, "ctx", axis=0, tiled=True)
    gains = full_qkv[:, used : used + 2].T.astype(jnp.float32)
    gain_attn = gains[0:1]
    gain_ffn = gains[1:2]

    heads = q_cols // HD
    groups = kv_cols // HD
    per = heads // groups
    span_total = local_tokens * lax.axis_size("ctx")
    window = span_total > WINDOW
    query_slots = me * local_tokens + jnp.arange(local_tokens, dtype=jnp.int32)
    cosine, sine = angles(query_slots)
    piece_rows = seq_count * local_tokens
    rows = micro_count * piece_rows
    chunk = piece_rows // lines
    pieces = range(micro_count)

    nothing = jnp.zeros_like(sine)
    turning = heads + groups
    rest = padded - turning * HD
    cos_wide = jnp.concatenate(
        [cosine] * (2 * turning) + [jnp.ones((local_tokens, rest), jnp.float32)], axis=1
    )
    ahead = jnp.concatenate(
        [-sine, nothing] * turning + [jnp.zeros((local_tokens, rest), jnp.float32)], axis=1
    )
    behind = jnp.concatenate(
        [nothing, sine] * turning + [jnp.zeros((local_tokens, rest), jnp.float32)], axis=1
    )
    both = 2 * kv_cols
    rest = (both + 127) // 128 * 128 - groups * HD
    key_tables = (
        jnp.concatenate(
            [cosine] * (2 * groups) + [jnp.ones((local_tokens, rest), jnp.float32)], axis=1
        ),
        jnp.concatenate(
            [-sine, nothing] * groups + [jnp.zeros((local_tokens, rest), jnp.float32)], axis=1
        ),
        jnp.concatenate(
            [nothing, sine] * groups + [jnp.zeros((local_tokens, rest), jnp.float32)], axis=1
        ),
    )
    cos_tall = jnp.concatenate([cosine.T] * per, axis=1)
    sin_tall = jnp.concatenate([sine.T] * per, axis=1)
    slots = jnp.concatenate([query_slots] * per)[None]

    flat = tokens.reshape(rows, width)
    input_one, query_rot, kv = project(
        flat, gain_attn, full_qkv, cos_wide, ahead, behind, micro_count, q_cols, 2 * kv_cols
    )

    def piece_of(array, piece):
        return array[piece * piece_rows : (piece + 1) * piece_rows]

    live = (query_slots[None, None, :] < lengths[:, :, None]).reshape(rows, 1)
    grad_out = jnp.where(live, cotangent.reshape(rows, width), 0)

    metas = [
        jnp.concatenate([me.astype(jnp.int32)[None], lengths[piece]]) for piece in pieces
    ]
    bits = chip_bits()
    keys = [
        cube_gather(piece_of(kv, piece), bits if piece % 2 == 0 else bits[::-1])
        for piece in pieces
    ]

    def attend_piece(piece, *others):
        own, other = keys[piece]
        query = after(piece_of(query_rot, piece), *others)
        att, lse = attend(metas[piece], slots, query, own, other, groups, window)
        return att, lse, dot(att, full_out, 1, 1).astype(LOW)

    def residual(piece, summed):
        piece_tokens = take_chunk(piece_of(flat, piece), place, chunk).astype(jnp.float32)
        hidden = piece_tokens + summed
        scale = norm_scale(hidden)
        normed = hidden * scale
        return hidden, scale, normed, (normed * gain_ffn).astype(LOW)

    def hidden_back(piece, grad_two, kept):
        _, scale, normed, _ = kept
        gain_term = jnp.sum(grad_two * normed, axis=0)
        grad_hidden = take_chunk(piece_of(grad_out, piece), place, chunk).astype(
            jnp.float32
        ) + norm_back(grad_two, gain_ffn, normed, scale)
        return gain_term, grad_hidden, grad_hidden.astype(LOW)

    def scatter_weight(term):
        return lax.psum_scatter(term, "ctx", scatter_dimension=0, tiled=True)

    def weight_grad(left, right, *others):
        term = dot(after(left, *others), right, 0, 0).astype(LOW)
        return with_layout_constraint(term, Layout((0, 1)))

    def attention_back(piece, grad_low, *others):
        grad_att = dot(after(grad_low, *others), full_out, 1, 0).astype(LOW)
        own, other = keys[piece]
        return attend_back(
            metas[piece], slots, cos_tall, sin_tall, piece_of(query_rot, piece), own, other,
            atts[piece], grad_att, lses[piece], groups, window,
        )

    def one_back(back, *others):
        return dot(after(back, *others), full_qkv[:, :used], 1, 1).astype(LOW)

    def tokens_back(piece, grad_one, grad_hidden):
        piece_tokens = take_chunk(piece_of(flat, piece), place, chunk).astype(jnp.float32)
        scale = norm_scale(piece_tokens)
        normed = piece_tokens * scale
        gain_term = jnp.sum(grad_one * normed, axis=0)
        total = grad_hidden + norm_back(grad_one, gain_attn, normed, scale)
        return gain_term, total.astype(LOW)

    att0, lse0, branch0 = attend_piece(0)
    sum0 = ChainScatter(branch0)
    sum0.next()
    att1, lse1, branch1 = attend_piece(1, branch0)
    atts, lses = (att0, att1), (lse0, lse1)
    sum1 = ChainScatter(branch1, *sum0.landed)
    kept0 = residual(0, sum0.finish())
    two0 = ChainGather(kept0[3])
    sum1.next()
    two0.next()
    two0.next(full_gate, full_up)
    kept1 = residual(1, sum1.finish())
    two1 = ChainGather(kept1[3])
    input0 = two0.finish()

    act0, grad_gate0, grad_up0 = feed(
        after(input0, kept1[3]), piece_of(grad_out, 0), full_gate, full_up, full_down
    )
    two1.next(full_down)
    back_two0 = back_through((after(grad_gate0, two1.landed), grad_up0), (full_gate, full_up))
    back_sum0 = Scatter(back_two0)
    input1 = two1.finish()
    act1, grad_gate1, grad_up1 = feed(
        after(input1, back_two0), piece_of(grad_out, 1), full_gate, full_up, full_down
    )
    back_sum0.next(act1)
    back_two1 = back_through((grad_gate1, grad_up1), (full_gate, full_up))
    back_sum1 = Scatter(back_two1)
    acts = jnp.concatenate([act0, act1], axis=0)
    ffn = back_through((after(acts, back_two1),), (full_down,))
    gain0, grad_hidden0, low0 = hidden_back(0, back_sum0.finish(back_two1), kept0)
    hidden0 = Gather(low0)
    down_term = weight_grad(grad_out, acts, ffn, back_sum1.landed)
    down_grad = scatter_weight(down_term)
    back_sum1.next()
    input_two = jnp.concatenate([input0, input1], axis=0)
    gate_term = weight_grad(
        input_two, jnp.concatenate([grad_gate0, grad_gate1], axis=0), down_term, hidden0.landed
    )
    gate_grad = scatter_weight(gate_term)
    hidden0.next()
    up_term = weight_grad(
        input_two, jnp.concatenate([grad_up0, grad_up1], axis=0), gate_term, back_sum1.landed
    )
    up_grad = scatter_weight(up_term)
    gain1, grad_hidden1, low1 = hidden_back(1, back_sum1.finish(), kept1)
    hidden1 = Gather(low1)
    whole0 = hidden0.finish()
    mixed0 = Scatter(piece_of(ffn, 0), whole0)
    query0, own0, other0 = attention_back(0, whole0, low1, up_term)
    keys0 = Reduce(own0, other0, bits)
    hidden1.next()
    mixed1 = Scatter(piece_of(ffn, 1), hidden1.landed)
    whole1 = hidden1.finish()
    query1, own1, other1 = attention_back(1, whole1, query0, mixed0.landed)
    mixed0.next()
    keys1 = Reduce(own1, other1, bits)
    keys0.next()
    keys1.next()
    out_term = weight_grad(
        jnp.concatenate([whole0, whole1], axis=0),
        jnp.concatenate([att0, att1], axis=0),
        query1,
        mixed1.landed,
        gate_grad,
    )
    out_grad = scatter_weight(out_term)
    mixed1.next()
    back0 = join_back(query0, *keys0.finish(), *key_tables)
    back_one0 = one_back(back0, out_term, mixed0.landed)
    one0 = Scatter(back_one0)
    whole_mixed0 = Gather((kept0[0] + mixed0.finish()).astype(LOW))
    back1 = join_back(query1, *keys1.finish(), *key_tables)
    back_one1 = one_back(back1, back_one0, mixed1.landed)
    one1 = Scatter(back_one1, one0.landed)
    qkv_term = weight_grad(input_one, jnp.concatenate([back0, back1], axis=0), back_one1, up_grad)
    qkv_grad = scatter_weight(qkv_term).astype(jnp.float32)
    whole_mixed1 = Gather((kept1[0] + mixed1.finish()).astype(LOW), qkv_term)
    one0.next()
    whole_mixed0.next()
    gain2, total0 = tokens_back(0, one0.finish(), grad_hidden0)
    tokens0 = Gather(total0)
    one1.next()
    whole_mixed1.next()
    tokens0.next()
    gain3, total1 = tokens_back(1, one1.finish(), grad_hidden1)
    tokens1 = Gather(total1)
    mixed_parts = [whole_mixed0.finish(), whole_mixed1.finish()]
    token_parts = [tokens0.finish(), tokens1.finish()]
    gain_terms = jnp.stack([gain2 + gain3, gain0 + gain1])
    for bit in line_bits():
        gain_terms = gain_terms + line_swap(gain_terms, bit)
    gain_terms = jnp.swapaxes(
        gain_terms.reshape(2, lax.axis_size("ctx"), attn_gain.shape[0]), 0, 1
    )
    for bit in (bits[::-1] + [1]):
        half = gain_terms.shape[0] // 2
        mine = lax.rem(me // bit, 2)
        got = lax.ppermute(take_chunk(gain_terms, 1 - mine, half), "ctx", flip(bit))
        gain_terms = take_chunk(gain_terms, mine, half) + got
    gain_terms = gain_terms[0]
    mixed = jnp.stack(mixed_parts, axis=0).reshape(tokens.shape)
    token_grad = jnp.stack(token_parts, axis=0).reshape(tokens.shape).astype(jnp.float32)
    return (
        mixed,
        token_grad,
        gain_terms[0],
        qkv_grad[:, :q_cols],
        qkv_grad[:, q_cols : q_cols + kv_cols],
        qkv_grad[:, q_cols + kv_cols :],
        out_grad.T.astype(jnp.float32),
        gain_terms[1],
        gate_grad.astype(jnp.float32),
        up_grad.astype(jnp.float32),
        down_grad.T.astype(jnp.float32),
    )


def solution(mesh):
    placed = (
        P(None, None, "ctx", None),
        P(),
        P(None, None, "ctx", None),
        P("ctx"),
        P("ctx", "head"),
        P("ctx", "head"),
        P("ctx", "head"),
        P("head", "ctx"),
        P("ctx"),
        P("ctx", "head"),
        P("ctx", "head"),
        P("head", "ctx"),
    )
    return jax.shard_map(
        per_device,
        mesh=mesh,
        in_specs=placed,
        out_specs=(
            P(None, None, "ctx", None),
            P(None, None, "ctx", None),
            P("ctx"),
            P("ctx", "head"),
            P("ctx", "head"),
            P("ctx", "head"),
            P("head", "ctx"),
            P("ctx"),
            P("ctx", "head"),
            P("ctx", "head"),
            P("head", "ctx"),
        ),
        check_vma=False,
    )
```

time: 1190 us -> 937 us (0.79)
  matrix products: 281 us -> 67.7 us
  Pallas kernels: 0 us -> 112 us
  blocking collectives: 53.9 us -> 0 us
  other arithmetic: 144 us -> 90.2 us
  starting transfers between devices: 234 us -> 185 us
    dot_general x24 -> x11, matrix products: 182 us -> 67.7 us  [dot(): lax.dot_general(left, right, (((a,), (b,)), ((), ())), preferred_element_...]
    pallas_call x0 -> x12, Pallas kernels: none -> 112 us  [the longest x3 41.4 us: back_through(): pl.pallas_call(back_kernel, grid=((width + tile - 1) // tile,), in_specs=...]
    dot_general x12 -> x0, matrix products: 98.4 us -> none  [the longest x2 24.2 us: per_device(): jnp.einsum('stkgd,spkd->skgtp', grad_att, value_all, preferred_element_ty...]
    ppermute x96 -> x65, waiting for transfers between devices: 246 us -> 320 us  [the longest x26 227 us: line_swap(): return lax.ppermute(value, 'head', [(i, i ^ bit) for i in range(n)])]
    unnamed x13 -> x10, waiting for transfers between devices: 62.7 us -> 2.02 us
    ppermute x96 -> x65, starting transfers between devices: 233 us -> 184 us  [the longest x26 70.5 us: line_swap(): return lax.ppermute(value, 'head', [(i, i ^ bit) for i in range(n)])]
    psum x1 -> x0, blocking collectives: 43.5 us -> none  [per_device(): lax.psum(jnp.stack([sum(gain_one_terms), sum(gain_two_terms)]), ('head',...]
    dynamic_update_slice x32 -> x8, other arithmetic: 33.3 us -> 8.22 us  [the longest x6 6.16 us: finish(): whole = lax.dynamic_update_slice_in_dim(whole, block, at, axis=0)]
  transfers between devices with their start and end apart: 108 -> 75, of which waited for: 41 -> 30; matrix products, arithmetic and copies ran while one was open for 34% -> 22% of each run, Pallas kernels for 0% -> 11%
where the time goes in v2:
time: 937 us; the launch traced here: 925 us
  waiting for transfers between devices  361 us (39%)
  starting transfers between devices  185 us (20%)
  Pallas kernels  112 us (12%)
  local copies, waits for them, and re-layouts  91.7 us (10%)
  other arithmetic  90.2 us (10%)
  matrix products  67.7 us (7%)
  between operations  16.6 us (2%)
    ppermute x26, waiting for transfers between devices, line_swap(): return lax.ppermute(value, 'head', [(i, i ^ bit) for i in range(n)])  227 us
    ppermute x26, starting transfers between devices, line_swap(): return lax.ppermute(value, 'head', [(i, i ^ bit) for i in range(n)])  70.5 us
    dot_general x11, matrix products, dot(): lax.dot_general(left, right, (((a,), (b,)), ((), ())), preferred_element_...  67.7 us
    pallas_call x3, Pallas kernels, back_through(): pl.pallas_call(back_kernel, grid=((width + tile - 1) // tile,), in_specs=...  41.4 us
    ppermute x4, waiting for transfers between devices, cube_gather(): got = lax.ppermute(own, 'ctx', flip(bit))  37.8 us
    all_gather x1, waiting for transfers between devices, per_device(): full_qkv = lax.all_gather(qkv_shard, 'ctx', axis=0, tiled=True)  37.7 us
    ppermute x4, starting transfers between devices, next(): self.landed = lax.ppermute(sent, 'ctx', flip(bit))  34.2 us
    pallas_call x2, Pallas kernels, feed(): pl.pallas_call(feed_kernel, grid=((units + tile - 1) // tile,), in_specs=...  34.1 us
  transfers between devices with their start and end apart: 75, of which 30 were waited for; matrix products, arithmetic and copies ran while one was open for 22% of the time, Pallas kernels for 11%

profile of v2, /device:TPU:0, one launch (start us, length us, event | category | flops | bytes accessed | tf_op | source)
XLA Modules:
  0.0 925.0 jit_solution(18065029323767221369)
XLA Ops:
  19.2 37.7 %all-gather.6.cloned.1.call-done.weight_ref = bf16[2560,1024]{1,0:T(8,128)(2,1)} async-done(((bf16[320,1024]{1,0:T(8,128)(2,1)}), bf16[2560,1024]{1,0:T(8,128)(2,1)}) %all-gather.6.cloned.1.call-update) | async-done | bytes 5242896 | tf_op jit(solution)/shard_map/all_gather | solution.py:669
  87.9 12.6 %collective-permute-done.1 = bf16[2,384,320]{1,2,0:T(8,128)(2,1)S(1)} collective-permute-done((bf16[2,384,320]{1,2,0:T(8,128)(2,1)S(1)}, bf16[2,384,320]{1,2,0:T(8,128)(2,1)S(1)}, u32[]{:S(2)}, u32[]{:S(2)}) %collective-permute-start.1) | collective-permute-done | bytes 491552 | tf_op jit(solution)/shard_map/ppermute | solution.py:62
  106.1 14.8 %collective-permute-done.15 = bf16[1,384,320]{2,1,0:T(8,128)(2,1)S(1)} collective-permute-done((bf16[1,384,320]{2,1,0:T(8,128)(2,1)S(1)}, bf16[1,384,320]{2,1,0:T(8,128)(2,1)S(1)}, u32[]{:S(2)}, u32[]{:S(2)}) %collective-permute-start.15) | collective-permute-done | bytes 245792 | tf_op jit(solution)/shard_map/ppermute | solution.py:62
  223.1 18.3 %collective-permute-start.9 = (bf16[96,2560]{1,0:T(8,128)(2,1)}, bf16[96,2560]{1,0:T(8,128)(2,1)S(1)}, u32[]{:S(2)}, u32[]{:S(2)}) collective-permute-start(bf16[96,2560]{1,0:T(8,128)(2,1)} %get-tuple-element.149), channel_id=1, source_target_pairs={{0,1},{1,2},{2,3},{4,5},{5,6},{6,7},{8,9},{9,10},{10,11},{12,13},{... | collective-permute-start | bytes 1474568 | tf_op jit(solution)/shard_map/ppermute | solution.py:202
  290.5 17.3 %feed.2 = (bf16[384,1728]{1,0:T(8,128)(2,1)S(1)}, bf16[384,1728]{1,0:T(8,128)(2,1)S(1)}, bf16[384,1728]{1,0:T(8,128)(2,1)S(1)}) custom-call(bf16[384,2560]{1,0:T(8,128)(2,1)} %select_dynamic-update-slice_fusion.3.input_ref, bf16[384,2560]{1,0:T(8,128)(2,1)} %get-tuple-element.155.grad_ref, bf16[2560,1728]{1,0:T(8,128)(2,1)} %all-gather.10.cloned.1.call-done.gate_ref.refs_2_, ...), custom_call_target="tpu_custom_call" | custom-call | flops 5096079360 | bytes 17227776 | tf_op jit(solution)/shard_map/feed/pallas_call | solution.py:319
  307.9 14.2 %back_through.3 = bf16[384,2560]{1,0:T(8,128)(2,1)S(1)} custom-call(bf16[384,1728]{1,0:T(8,128)(2,1)S(1)} %get-tuple-element.64.refs_0_, bf16[384,1728]{1,0:T(8,128)(2,1)S(1)} %get-tuple-element.65.refs_1_, bf16[2560,1728]{1,0:T(8,128)(2,1)} %all-gather.10.cloned.1.call-done.gate_ref.refs_2_, bf16[2560,1728]{1,0:T(8,128)(2,1)} %all-gather.12.cloned.1.call-done.up_ref.refs_3_), custom_call_target="tpu_custom_call" | custom-call | flops 3397386240 | bytes 11157504 | tf_op jit(solution)/shard_map/back_through/pallas_call | solution.py:349
  324.7 16.8 %feed.3 = (bf16[384,1728]{1,0:T(8,128)(2,1)S(1)}, bf16[384,1728]{1,0:T(8,128)(2,1)S(1)}, bf16[384,1728]{1,0:T(8,128)(2,1)S(1)}) custom-call(bf16[384,2560]{1,0:T(8,128)(2,1)S(1)} %select_dynamic-update-slice_fusion.input_ref, bf16[384,2560]{1,0:T(8,128)(2,1)} %get-tuple-element.154.grad_ref, ...), custom_call_target="tpu_custom_call" | custom-call | flops 5096079360 | bytes 17227776 | tf_op jit(solution)/shard_map/feed/pallas_call | solution.py:319
  341.6 14.2 %back_through.4 = bf16[384,2560]{1,0:T(8,128)(2,1)S(1)} custom-call(bf16[384,1728]{1,0:T(8,128)(2,1)S(1)} %get-tuple-element.68.refs_0_, bf16[384,1728]{1,0:T(8,128)(2,1)S(1)} %get-tuple-element.69.refs_1_, bf16[2560,1728]{1,0:T(8,128)(2,1)} %all-gather.10.cloned.1.call-done.gate_ref.refs_2_, bf16[2560,1728]{1,0:T(8,128)(2,1)} %all-gather.12.cloned.1.call-done.up_ref.refs_3_), custom_call_target="tpu_custom_call" | custom-call | flops 3397386240 | bytes 11157504 | tf_op jit(solution)/shard_map/back_through/pallas_call | solution.py:349
  363.3 28.9 %collective-permute-start.31 = (bf16[96,2560]{1,0:T(8,128)(2,1)S(1)}, bf16[96,2560]{1,0:T(8,128)(2,1)S(1)}, u32[]{:S(2)}, u32[]{:S(2)}) collective-permute-start(bf16[96,2560]{1,0:T(8,128)(2,1)S(1)} %dynamic-slice_convert_fusion.5), channel_id=1, source_target_pairs={{0,2},{1,3},{2,0},{3,1},{4,6},{5,7},{6,4},{7,5},{8,10},{9,11},{10,... | collective-permute-start | bytes 1474568 | tf_op jit(solution)/shard_map/ppermute | solution.py:81
  392.5 17.3 %collective-permute-start.39 = (bf16[96,2560]{1,0:T(8,128)(2,1)S(1)}, bf16[96,2560]{1,0:T(8,128)(2,1)S(1)}, u32[]{:S(2)}, u32[]{:S(2)}) collective-permute-start(bf16[96,2560]{1,0:T(8,128)(2,1)S(1)} %dynamic-slice_convert_fusion.3), channel_id=1, source_target_pairs={{0,2},{1,3},{2,0},{3,1},{4,6},{5,7},{6,4},{7,5},{8,10},{9,11},{10,... | collective-permute-start | bytes 1474568 | tf_op jit(solution)/shard_map/ppermute | solution.py:81
  409.9 13.0 %back_through.5 = bf16[768,2560]{1,0:T(8,128)(2,1)} custom-call(bf16[768,1728]{1,0:T(8,128)(2,1)S(1)} %constant_dynamic-update-slice_fusion.2.refs_0_, bf16[2560,1728]{1,0:T(8,128)(2,1)} %all-gather.14.cloned.1.call-done.down_ref.refs_1_), custom_call_target="tpu_custom_call" | custom-call | flops 3397386240 | bytes 7716864 | tf_op jit(solution)/shard_map/back_through/pallas_call | solution.py:349
  455.5 12.1 %convolution_convert_fusion.1 = bf16[2560,1728]{1,0:T(8,128)(2,1)} fusion(bf16[768,2560]{1,0:T(8,128)(2,1)} %pad_maximum_fusion, bf16[384,1728]{1,0:T(8,128)(2,1)} %copy-done.7, bf16[384,1728]{1,0:T(8,128)(2,1)S(1)} %copy-done.5), kind=kOutput, calls=%fused_computation.1 | convolution fusion | flops 6804504576 | bytes 15433728 | tf_op jit(solution)/shard_map/dot_general | solution.py:24
  468.9 11.6 %convolution_convert_fusion = bf16[2560,1728]{1,0:T(8,128)(2,1)} fusion(bf16[768,2560]{1,0:T(8,128)(2,1)} %pad_maximum_fusion, bf16[384,1728]{1,0:T(8,128)(2,1)} %copy-done.6, bf16[384,1728]{1,0:T(8,128)(2,1)S(1)} %copy-done.3), kind=kOutput, calls=%fused_computation | convolution fusion | flops 6804504576 | bytes 15433728 | tf_op jit(solution)/shard_map/dot_general | solution.py:24
  494.9 20.5 %collective-permute-done.40 = bf16[96,2560]{1,0:T(8,128)(2,1)S(1)} collective-permute-done((bf16[96,2560]{1,0:T(8,128)(2,1)S(1)}, bf16[96,2560]{1,0:T(8,128)(2,1)S(1)}, u32[]{:S(2)}, u32[]{:S(2)}) %collective-permute-start.40) | collective-permute-done | bytes 491552 | tf_op jit(solution)/shard_map/ppermute | solution.py:81
  516.3 12.0 %collective-permute-done.33 = bf16[192,2560]{1,0:T(8,128)(2,1)S(1)} collective-permute-done((bf16[192,2560]{1,0:T(8,128)(2,1)S(1)}, bf16[192,2560]{1,0:T(8,128)(2,1)S(1)}, u32[]{:S(2)}, u32[]{:S(2)}) %collective-permute-start.33) | collective-permute-done | bytes 983072 | tf_op jit(solution)/shard_map/ppermute | solution.py:81
  532.2 17.2 %collective-permute-done.41 = bf16[192,2560]{1,0:T(8,128)(2,1)S(1)} collective-permute-done((bf16[192,2560]{1,0:T(8,128)(2,1)S(1)}, bf16[192,2560]{1,0:T(8,128)(2,1)S(1)}, u32[]{:S(2)}, u32[]{:S(2)}) %collective-permute-start.41) | collective-permute-done | bytes 983072 | tf_op jit(solution)/shard_map/ppermute | solution.py:81
  584.8 16.5 %collective-permute-start.48 = (bf16[2,384,320]{1,2,0:T(8,128)(2,1)}, bf16[2,384,320]{1,2,0:T(8,128)(2,1)}, u32[]{:S(2)}, u32[]{:S(2)}) collective-permute-start(bf16[2,384,320]{1,2,0:T(8,128)(2,1)} %copy.60), channel_id=1, source_target_pairs={{0,16},{4,20},{8,24},{12,28},{16,0},{20,4},{24,8},{28,12},{1,17},{... | collective-permute-start | bytes 1474568 | tf_op jit(solution)/shard_map/ppermute | solution.py:241
  647.1 19.0 %collective-permute-done.36 = bf16[96,2560]{1,0:T(8,128)(2,1)} collective-permute-done((bf16[96,2560]{1,0:T(8,128)(2,1)}, bf16[96,2560]{1,0:T(8,128)(2,1)}, u32[]{:S(2)}, u32[]{:S(2)}) %collective-permute-start.36) | collective-permute-done | bytes 491552 | tf_op jit(solution)/shard_map/ppermute | solution.py:81
  736.8 12.6 %collective-permute-done.50 = bf16[96,2560]{1,0:T(8,128)(2,1)S(1)} collective-permute-done((bf16[96,2560]{1,0:T(8,128)(2,1)S(1)}, bf16[96,2560]{1,0:T(8,128)(2,1)S(1)}, u32[]{:S(2)}, u32[]{:S(2)}) %collective-permute-start.50) | collective-permute-done | bytes 491552 | tf_op jit(solution)/shard_map/ppermute | solution.py:81
  754.5 26.4 %collective-permute-done.56 = bf16[192,2560]{1,0:T(8,128)(2,1)S(1)} collective-permute-done((bf16[192,2560]{1,0:T(8,128)(2,1)S(1)}, bf16[192,2560]{1,0:T(8,128)(2,1)S(1)}, u32[]{:S(2)}, u32[]{:S(2)}) %collective-permute-start.56) | collective-permute-done | bytes 983072 | tf_op jit(solution)/shard_map/ppermute | solution.py:81
  786.3 17.8 %collective-permute-done.57 = bf16[96,2560]{1,0:T(8,128)(2,1)S(1)} collective-permute-done((bf16[96,2560]{1,0:T(8,128)(2,1)S(1)}, bf16[96,2560]{1,0:T(8,128)(2,1)S(1)}, u32[]{:S(2)}, u32[]{:S(2)}) %collective-permute-start.57) | collective-permute-done | bytes 491552 | tf_op jit(solution)/shard_map/ppermute | solution.py:81
  834.1 21.4 %collective-permute-done.54 = bf16[96,2560]{1,0:T(8,128)(2,1)S(1)} collective-permute-done((bf16[96,2560]{1,0:T(8,128)(2,1)S(1)}, bf16[96,2560]{1,0:T(8,128)(2,1)S(1)}, u32[]{:S(2)}, u32[]{:S(2)}) %collective-permute-start.54) | collective-permute-done | bytes 491552 | tf_op jit(solution)/shard_map/ppermute | solution.py:81
  866.3 20.8 %collective-permute-done.55 = bf16[192,2560]{1,0:T(8,128)(2,1)S(1)} collective-permute-done((bf16[192,2560]{1,0:T(8,128)(2,1)S(1)}, bf16[192,2560]{1,0:T(8,128)(2,1)S(1)}, u32[]{:S(2)}, u32[]{:S(2)}) %collective-permute-start.55) | collective-permute-done | bytes 983072 | tf_op jit(solution)/shard_map/ppermute | solution.py:81
  887.6 20.5 %collective-permute-done.59 = bf16[192,2560]{1,0:T(8,128)(2,1)S(1)} collective-permute-done((bf16[192,2560]{1,0:T(8,128)(2,1)S(1)}, bf16[192,2560]{1,0:T(8,128)(2,1)S(1)}, u32[]{:S(2)}, u32[]{:S(2)}) %collective-permute-start.59) | collective-permute-done | bytes 983072 | tf_op jit(solution)/shard_map/ppermute | solution.py:81
  (580 shorter events, 474.9 us)
Async XLA Ops:
  7.2 49.7 %all-gather.6.cloned.1.call-start = ((), (), s32[]{:S(2)}) async-start(), calls=%async_computation.5 | async-start | bytes 5898240 | tf_op jit(solution)/shard_map/all_gather | solution.py:669
  12.9 117.0 %all-gather.8.cloned.1.call-start = ((), (), s32[]{:S(2)}) async-start(), calls=%async_computation.6 | async-start | bytes 3686400 | tf_op jit(solution)/shard_map/all_gather | solution.py:670
  13.6 265.7 %all-gather.10.cloned.1.call-start = ((), (), s32[]{:S(2)}) async-start(), calls=%async_computation.7 | async-start | bytes 10321920 | tf_op jit(solution)/shard_map/all_gather | solution.py:671
  14.4 265.0 %all-gather.12.cloned.1.call-start = ((), (), s32[]{:S(2)}) async-start(), calls=%async_computation.8 | async-start | bytes 10321920 | tf_op jit(solution)/shard_map/all_gather | solution.py:672
  14.9 265.9 %all-gather.14.cloned.1.call-start = ((), (), s32[]{:S(2)}) async-start(), calls=%async_computation.9 | async-start | bytes 10321920 | tf_op jit(solution)/shard_map/all_gather | solution.py:673
  87.4 585.6 %reduce-scatter.6.cloned.1.call-start = ((), (), s32[]{:S(2)}) async-start(), calls=%async_computation.10 | async-start | bytes 10321920 | tf_op jit(solution)/shard_map/reduce_scatter | solution.py:761
  322.2 39.5 %collective-permute-start.30 = (bf16[192,2560]{1,0:T(8,128)(2,1)S(1)}, bf16[192,2560]{1,0:T(8,128)(2,1)}, u32[]{:S(2)}, u32[]{:S(2)}) collective-permute-start(bf16[192,2560]{1,0:T(8,128)(2,1)S(1)} %constant_dynamic-slice_fusion.11), channel_id=1, source_target_pairs={{0,1},{1,0},{2,3},{3,2},{4,5},{5,4},{6,7},{7,6},{8,9},{9,8},{10,11... | collective-permute-start | bytes 2949128 | tf_op jit(solution)/shard_map/ppermute | solution.py:81
  355.9 36.3 %collective-permute-start.38 = (bf16[192,2560]{1,0:T(8,128)(2,1)S(1)}, bf16[192,2560]{1,0:T(8,128)(2,1)S(1)}, u32[]{:S(2)}, u32[]{:S(2)}) collective-permute-start(bf16[192,2560]{1,0:T(8,128)(2,1)S(1)} %constant_dynamic-slice_fusion.9), channel_id=1, source_target_pairs={{0,1},{1,0},{2,3},{3,2},{4,5},{5,4},{6,7},{7,6},{8,9},{9,8},{10,11... | collective-permute-start | bytes 2949128 | tf_op jit(solution)/shard_map/ppermute | solution.py:81
  363.3 59.6 %collective-permute-start.31 = (bf16[96,2560]{1,0:T(8,128)(2,1)S(1)}, bf16[96,2560]{1,0:T(8,128)(2,1)S(1)}, u32[]{:S(2)}, u32[]{:S(2)}) collective-permute-start(bf16[96,2560]{1,0:T(8,128)(2,1)S(1)} %dynamic-slice_convert_fusion.5), channel_id=1, source_target_pairs={{0,2},{1,3},{2,0},{3,1},{4,6},{5,7},{6,4},{7,5},{8,10},{9,11},{10,... | collective-permute-start | bytes 1474568 | tf_op jit(solution)/shard_map/ppermute | solution.py:81
  392.5 38.8 %collective-permute-start.39 = (bf16[96,2560]{1,0:T(8,128)(2,1)S(1)}, bf16[96,2560]{1,0:T(8,128)(2,1)S(1)}, u32[]{:S(2)}, u32[]{:S(2)}) collective-permute-start(bf16[96,2560]{1,0:T(8,128)(2,1)S(1)} %dynamic-slice_convert_fusion.3), channel_id=1, source_target_pairs={{0,2},{1,3},{2,0},{3,1},{4,6},{5,7},{6,4},{7,5},{8,10},{9,11},{10,... | collective-permute-start | bytes 1474568 | tf_op jit(solution)/shard_map/ppermute | solution.py:81
  467.6 250.3 %reduce-scatter.8.cloned.1.call-start = ((), (), s32[]{:S(2)}) async-start(), calls=%async_computation.11 | async-start | bytes 10321920 | tf_op jit(solution)/shard_map/reduce_scatter | solution.py:761
  480.6 248.9 %reduce-scatter.14.cloned.1.call-start = ((), (), s32[]{:S(2)}) async-start(), calls=%async_computation.14 | async-start | bytes 10321920 | tf_op jit(solution)/shard_map/reduce_scatter | solution.py:761
  488.1 424.1 %reduce-scatter.12.cloned.1.call-start = ((), (), s32[]{:S(2)}) async-start(), calls=%async_computation.13 | async-start | bytes 3686400 | tf_op jit(solution)/shard_map/reduce_scatter | solution.py:761
  493.5 34.8 %collective-permute-start.33 = (bf16[192,2560]{1,0:T(8,128)(2,1)S(1)}, bf16[192,2560]{1,0:T(8,128)(2,1)S(1)}, u32[]{:S(2)}, u32[]{:S(2)}) collective-permute-start(bf16[192,2560]{1,0:T(8,128)(2,1)S(1)} %pad_maximum_fusion.11), channel_id=1, source_target_pairs={{0,1},{1,0},{2,3},{3,2},{4,5},{5,4},{6,7},{7,6},{8,9},{9,8},{10,11... | collective-permute-start | bytes 2949128 | tf_op jit(solution)/shard_map/ppermute | solution.py:81
  532.2 38.9 %collective-permute-start.34 = (bf16[192,2560]{1,0:T(8,128)(2,1)}, bf16[192,2560]{1,0:T(8,128)(2,1)}, u32[]{:S(2)}, u32[]{:S(2)}) collective-permute-start(bf16[192,2560]{1,0:T(8,128)(2,1)} %constant_dynamic-slice_fusion.10), channel_id=1, source_target_pairs={{0,1},{1,0},{2,3},{3,2},{4,5},{5,4},{6,7},{7,6},{8,9},{9,8},{10,11... | collective-permute-start | bytes 2949128 | tf_op jit(solution)/shard_map/ppermute | solution.py:81
  550.5 65.3 %collective-permute-start.42 = (bf16[192,2560]{1,0:T(8,128)(2,1)}, bf16[192,2560]{1,0:T(8,128)(2,1)}, u32[]{:S(2)}, u32[]{:S(2)}) collective-permute-start(bf16[192,2560]{1,0:T(8,128)(2,1)} %constant_dynamic-slice_fusion.8), channel_id=1, source_target_pairs={{0,1},{1,0},{2,3},{3,2},{4,5},{5,4},{6,7},{7,6},{8,9},{9,8},{10,11... | collective-permute-start | bytes 2949128 | tf_op jit(solution)/shard_map/ppermute | solution.py:81
  575.7 56.3 %collective-permute-start.35 = (bf16[96,2560]{1,0:T(8,128)(2,1)}, bf16[96,2560]{1,0:T(8,128)(2,1)}, u32[]{:S(2)}, u32[]{:S(2)}) collective-permute-start(bf16[96,2560]{1,0:T(8,128)(2,1)} %dynamic-slice_convert_fusion.4), channel_id=1, source_target_pairs={{0,2},{1,3},{2,0},{3,1},{4,6},{5,7},{6,4},{7,5},{8,10},{9,11},{10,... | collective-permute-start | bytes 1474568 | tf_op jit(solution)/shard_map/ppermute | solution.py:81
  584.8 35.8 %collective-permute-start.48 = (bf16[2,384,320]{1,2,0:T(8,128)(2,1)}, bf16[2,384,320]{1,2,0:T(8,128)(2,1)}, u32[]{:S(2)}, u32[]{:S(2)}) collective-permute-start(bf16[2,384,320]{1,2,0:T(8,128)(2,1)} %copy.60), channel_id=1, source_target_pairs={{0,16},{4,20},{8,24},{12,28},{16,0},{20,4},{24,8},{28,12},{1,17},{... | collective-permute-start | bytes 1474568 | tf_op jit(solution)/shard_map/ppermute | solution.py:241
  619.7 70.7 %collective-permute-start.43 = (bf16[96,2560]{1,0:T(8,128)(2,1)}, bf16[96,2560]{1,0:T(8,128)(2,1)}, u32[]{:S(2)}, u32[]{:S(2)}) collective-permute-start(bf16[96,2560]{1,0:T(8,128)(2,1)} %dynamic-slice_convert_fusion.2), channel_id=1, source_target_pairs={{0,2},{1,3},{2,0},{3,1},{4,6},{5,7},{6,4},{7,5},{8,10},{9,11},{10,... | collective-permute-start | bytes 1474568 | tf_op jit(solution)/shard_map/ppermute | solution.py:81
  623.1 69.8 %collective-permute-start.49 = (bf16[1,384,320]{2,1,0:T(8,128)(2,1)}, bf16[1,384,320]{2,1,0:T(8,128)(2,1)S(1)}, u32[]{:S(2)}, u32[]{:S(2)}) collective-permute-start(bf16[1,384,320]{2,1,0:T(8,128)(2,1)} %get-tuple-element.205), channel_id=1, source_target_pairs={{0,8},{4,12},{8,0},{12,4},{16,24},{20,28},{24,16},{28,20},{1,9},{5... | collective-permute-start | bytes 737288 | tf_op jit(solution)/shard_map/ppermute | solution.py:241
  669.2 35.5 %collective-permute-start.37 = (bf16[192,2560]{1,0:T(8,128)(2,1)}, bf16[192,2560]{1,0:T(8,128)(2,1)}, u32[]{:S(2)}, u32[]{:S(2)}) collective-permute-start(bf16[192,2560]{1,0:T(8,128)(2,1)} %pad_maximum_fusion.12), channel_id=1, source_target_pairs={{0,1},{1,0},{2,3},{3,2},{4,5},{5,4},{6,7},{7,6},{8,9},{9,8},{10,11... | collective-permute-start | bytes 2949128 | tf_op jit(solution)/shard_map/ppermute | solution.py:81
  680.8 233.4 %reduce-scatter.10.cloned.1.call-start = ((), (), s32[]{:S(2)}) async-start(), calls=%async_computation.12 | async-start | bytes 5898240 | tf_op jit(solution)/shard_map/reduce_scatter | solution.py:761
  712.6 37.0 %collective-permute-start.52 = (bf16[192,2560]{1,0:T(8,128)(2,1)}, bf16[192,2560]{1,0:T(8,128)(2,1)}, u32[]{:S(2)}, u32[]{:S(2)}) collective-permute-start(bf16[192,2560]{1,0:T(8,128)(2,1)} %constant_dynamic-slice_fusion.7), channel_id=1, source_target_pairs={{0,1},{1,0},{2,3},{3,2},{4,5},{5,4},{6,7},{7,6},{8,9},{9,8},{10,11... | collective-permute-start | bytes 2949128 | tf_op jit(solution)/shard_map/ppermute | solution.py:81
  866.2 41.9 %collective-permute-start.59 = (bf16[192,2560]{1,0:T(8,128)(2,1)S(1)}, bf16[192,2560]{1,0:T(8,128)(2,1)S(1)}, u32[]{:S(2)}, u32[]{:S(2)}) collective-permute-start(bf16[192,2560]{1,0:T(8,128)(2,1)S(1)} %pad_maximum_fusion.16), channel_id=1, source_target_pairs={{0,1},{1,0},{2,3},{3,2},{4,5},{5,4},{6,7},{7,6},{8,9},{9,8},{10,11... | collective-permute-start | bytes 2949128 | tf_op jit(solution)/shard_map/ppermute | solution.py:81
  (172 other events, 2095.8 us)
Sparse Core Ops, SparseCore 0:
  13.0 43.8 all-gather.5
  58.7 34.8 all-gather.7
  95.6 65.7 all-gather.9
  163.0 57.7 all-gather.11
  222.5 57.7 all-gather.13
  467.7 85.0 reduce-scatter.5
  556.9 84.8 reduce-scatter.7
  645.4 84.0 reduce-scatter.13
  733.4 46.8 reduce-scatter.11
  783.9 56.7 reduce-scatter.9

commit v3 on v2

--- a/solution.py
+++ b/solution.py
@@ -152,7 +152,7 @@
 
 class ChainScatter:
     def __init__(self, partial, *others):
-        self.partial = after(partial, *others)
+        self.partial = self.held = after(partial, *others)
         self.step = 0
         self.send()
 
@@ -238,6 +238,7 @@
         half = self.kept.shape[0] // 2
         sent = add_low(self.kept[half:], landed[half:])
         self.kept = add_low(self.kept[:half], landed[:half])
+        self.sent = sent
         self.landed = lax.ppermute(sent, "ctx", flip(bit))
 
     def finish(self):
@@ -575,7 +576,7 @@
         ],
         compiler_params=pltpu.CompilerParams(vmem_limit_bytes=VMEM_LIMIT),
         cost_estimate=pl.CostEstimate(
-            flops=12 * pairs * HD, bytes_accessed=4 * own.size, transcendentals=pairs
+            flops=12 * pairs * HD // COST, bytes_accessed=4 * own.size // COST, transcendentals=0
         ),
         name="attend",
     )(meta, slots, query, own, other)
@@ -613,7 +614,7 @@
         ],
         compiler_params=pltpu.CompilerParams(vmem_limit_bytes=VMEM_LIMIT),
         cost_estimate=pl.CostEstimate(
-            flops=30 * pairs * HD, bytes_accessed=8 * own.size, transcendentals=pairs
+            flops=30 * pairs * HD // COST, bytes_accessed=8 * own.size // COST, transcendentals=0
         ),
         name="attend_back",
     )(meta, slots, cos, sin, query, own, other, att, grad, lse_rows)
@@ -795,7 +796,7 @@
     two0.next()
     two0.next(full_gate, full_up)
     kept1 = residual(1, sum1.finish())
-    two1 = ChainGather(kept1[3])
+    two1 = Gather(kept1[3])
     input0 = two0.finish()
 
     act0, grad_gate0, grad_up0 = feed(
@@ -809,70 +810,84 @@
         after(input1, back_two0), piece_of(grad_out, 1), full_gate, full_up, full_down
     )
     back_sum0.next(act1)
-    back_two1 = back_through((grad_gate1, grad_up1), (full_gate, full_up))
-    back_sum1 = Scatter(back_two1)
     acts = jnp.concatenate([act0, act1], axis=0)
-    ffn = back_through((after(acts, back_two1),), (full_down,))
+    down_term = weight_grad(grad_out, acts, back_sum0.kept)
+    down_grad = scatter_weight(down_term)
+    back_two1 = back_through((after(grad_gate1, down_term), grad_up1), (full_gate, full_up))
     gain0, grad_hidden0, low0 = hidden_back(0, back_sum0.finish(back_two1), kept0)
     hidden0 = Gather(low0)
-    down_term = weight_grad(grad_out, acts, ffn, back_sum1.landed)
-    down_grad = scatter_weight(down_term)
-    back_sum1.next()
+    back_sum1 = Scatter(back_two1)
+    ffn = back_through((after(acts, low0, back_two1),), (full_down,))
     input_two = jnp.concatenate([input0, input1], axis=0)
     gate_term = weight_grad(
-        input_two, jnp.concatenate([grad_gate0, grad_gate1], axis=0), down_term, hidden0.landed
+        input_two,
+        jnp.concatenate([grad_gate0, grad_gate1], axis=0),
+        ffn,
+        back_sum1.landed,
+        hidden0.landed,
     )
     gate_grad = scatter_weight(gate_term)
     hidden0.next()
+    back_sum1.next()
     up_term = weight_grad(
-        input_two, jnp.concatenate([grad_up0, grad_up1], axis=0), gate_term, back_sum1.landed
+        input_two, jnp.concatenate([grad_up0, grad_up1], axis=0), gate_term
     )
     up_grad = scatter_weight(up_term)
-    gain1, grad_hidden1, low1 = hidden_back(1, back_sum1.finish(), kept1)
+    whole0 = hidden0.finish(up_term)
+    mixed0 = Scatter(piece_of(ffn, 0), whole0)
+    gain1, grad_hidden1, low1 = hidden_back(1, back_sum1.finish(up_term), kept1)
     hidden1 = Gather(low1)
-    whole0 = hidden0.finish()
-    mixed0 = Scatter(piece_of(ffn, 0), whole0)
-    query0, own0, other0 = attention_back(0, whole0, low1, up_term)
+    query0, own0, other0 = attention_back(0, whole0, low1)
     keys0 = Reduce(own0, other0, bits)
     hidden1.next()
-    mixed1 = Scatter(piece_of(ffn, 1), hidden1.landed)
+    keys0.next(mixed0.landed)
+    mixed0.next()
     whole1 = hidden1.finish()
-    query1, own1, other1 = attention_back(1, whole1, query0, mixed0.landed)
-    mixed0.next()
+    mixed1 = Scatter(piece_of(ffn, 1), whole1)
+    whole_mixed0 = Gather((kept0[0] + mixed0.finish()).astype(LOW))
+    query1, own1, other1 = attention_back(
+        1, whole1, query0, keys0.sent, mixed1.held
+    )
     keys1 = Reduce(own1, other1, bits)
-    keys0.next()
+    keys0.next(mixed1.landed)
+    mixed1.next()
+    whole_mixed0.next()
     keys1.next()
-    out_term = weight_grad(
-        jnp.concatenate([whole0, whole1], axis=0),
-        jnp.concatenate([att0, att1], axis=0),
-        query1,
-        mixed1.landed,
-        gate_grad,
-    )
-    out_grad = scatter_weight(out_term)
-    mixed1.next()
     back0 = join_back(query0, *keys0.finish(), *key_tables)
-    back_one0 = one_back(back0, out_term, mixed0.landed)
+    back_one0 = one_back(back0, query1, keys1.sent)
     one0 = Scatter(back_one0)
-    whole_mixed0 = Gather((kept0[0] + mixed0.finish()).astype(LOW))
+    whole_mixed1 = Gather((kept1[0] + mixed1.finish()).astype(LOW))
+    keys1.next()
     back1 = join_back(query1, *keys1.finish(), *key_tables)
-    back_one1 = one_back(back1, back_one0, mixed1.landed)
-    one1 = Scatter(back_one1, one0.landed)
-    qkv_term = weight_grad(input_one, jnp.concatenate([back0, back1], axis=0), back_one1, up_grad)
-    qkv_grad = scatter_weight(qkv_term).astype(jnp.float32)
-    whole_mixed1 = Gather((kept1[0] + mixed1.finish()).astype(LOW), qkv_term)
+    back_one1 = one_back(back1, back_one0, one0.held)
+    one1 = Scatter(back_one1)
     one0.next()
-    whole_mixed0.next()
+    whole_mixed1.next()
+    last_term = jnp.concatenate(
+        [
+            weight_grad(
+                input_one, jnp.concatenate([back0, back1], axis=0), back_one1, gate_grad
+            ),
+            weight_grad(
+                jnp.concatenate([whole0, whole1], axis=0),
+                jnp.concatenate([att0, att1], axis=0),
+                back_one1,
+            ),
+        ],
+        axis=1,
+    )
+    last_grad = scatter_weight(last_term).astype(jnp.float32)
+    qkv_grad, out_grad = last_grad[:, :used], last_grad[:, used:]
     gain2, total0 = tokens_back(0, one0.finish(), grad_hidden0)
-    tokens0 = Gather(total0)
+    tokens0 = ChainGather(total0)
+    tokens0_first = tokens0.landed
     one1.next()
-    whole_mixed1.next()
     tokens0.next()
-    gain3, total1 = tokens_back(1, one1.finish(), grad_hidden1)
-    tokens1 = Gather(total1)
+    gain3, total1 = tokens_back(1, one1.finish(tokens0_first), grad_hidden1)
+    tokens1 = ChainGather(total1)
     mixed_parts = [whole_mixed0.finish(), whole_mixed1.finish()]
     token_parts = [tokens0.finish(), tokens1.finish()]
-    gain_terms = jnp.stack([gain2 + gain3, gain0 + gain1])
+    gain_terms = after(jnp.stack([gain2 + gain3, gain0 + gain1]), tokens1.landed)
     for bit in line_bits():
         gain_terms = gain_terms + line_swap(gain_terms, bit)
     gain_terms = jnp.swapaxes(
@@ -893,7 +908,7 @@
         qkv_grad[:, :q_cols],
         qkv_grad[:, q_cols : q_cols + kv_cols],
         qkv_grad[:, q_cols + kv_cols :],
-        out_grad.T.astype(jnp.float32),
+        out_grad.T,
         gain_terms[1],
         gate_grad.astype(jnp.float32),
         up_grad.astype(jnp.float32),

time: 937 us -> 890 us (0.950)
  starting transfers between devices: 185 us -> 141 us
    ppermute x26 -> x24, waiting for transfers between devices: 227 us -> 169 us  [line_swap(): return lax.ppermute(value, 'head', [(i, i ^ bit) for i in range(n)])]
    ppermute x26 -> x24, starting transfers between devices: 70.5 us -> 40 us  [line_swap(): return lax.ppermute(value, 'head', [(i, i ^ bit) for i in range(n)])]
    ppermute x6 -> x9, waiting for transfers between devices: 17.6 us -> 45.7 us  [send(): lax.ppermute(self.landed[1], 'head', [(i, i - 1) for i in range(1, n - st...]
    ppermute x4, starting transfers between devices: 34.2 us -> 18.1 us  [next(): self.landed = lax.ppermute(sent, 'ctx', flip(bit))]
    all_gather x1, waiting for transfers between devices: 0.01 us -> 12 us  [per_device(): full_up = lax.all_gather(up_weight, 'ctx', axis=0, tiled=True)]
    concatenate x0 -> x1, other arithmetic: none -> 9.48 us  [per_device(): jnp.concatenate([weight_grad(input_one, jnp.concatenate([back0, back1], a...]
    ppermute x6 -> x9, starting transfers between devices: 30.6 us -> 29.3 us  [send(): lax.ppermute(self.landed[0], 'head', [(i, i + 1) for i in range(step, n -...]
    unnamed x257 -> x243, local copies, waits for them, and re-layouts: 33.5 us -> 33.4 us
  transfers between devices with their start and end apart: 75 -> 78, of which waited for: 30 -> 39; matrix products, arithmetic and copies ran while one was open for 22% -> 22% of each run, Pallas kernels for 11% -> 11%
where the time goes in v3:
time: 890 us; the launch traced here: 875 us
  waiting for transfers between devices  357 us (40%)
  starting transfers between devices  141 us (16%)
  Pallas kernels  110 us (12%)
  local copies, waits for them, and re-layouts  95.4 us (11%)
  other arithmetic  92.6 us (10%)
  matrix products  62.1 us (7%)
  between operations  16.9 us (2%)
    ppermute x24, waiting for transfers between devices, line_swap(): return lax.ppermute(value, 'head', [(i, i ^ bit) for i in range(n)])  169 us
    dot_general x11, matrix products, dot(): lax.dot_general(left, right, (((a,), (b,)), ((), ())), preferred_element_...  62.1 us
    ppermute x9, waiting for transfers between devices, send(): lax.ppermute(self.landed[1], 'head', [(i, i - 1) for i in range(1, n - st...  45.7 us
    pallas_call x3, Pallas kernels, back_through(): pl.pallas_call(back_kernel, grid=((width + tile - 1) // tile,), in_specs=...  40.4 us
    ppermute x24, starting transfers between devices, line_swap(): return lax.ppermute(value, 'head', [(i, i ^ bit) for i in range(n)])  40 us
    ppermute x4, waiting for transfers between devices, cube_gather(): got = lax.ppermute(own, 'ctx', flip(bit))  38.9 us
    all_gather x1, waiting for transfers between devices, per_device(): full_qkv = lax.all_gather(qkv_shard, 'ctx', axis=0, tiled=True)  37.8 us
    pallas_call x2, Pallas kernels, feed(): pl.pallas_call(feed_kernel, grid=((units + tile - 1) // tile,), in_specs=...  33.6 us
  transfers between devices with their start and end apart: 78, of which 39 were waited for; matrix products, arithmetic and copies ran while one was open for 22% of the time, Pallas kernels for 11%

profile of v3, /device:TPU:0, one launch (start us, length us, event | category | flops | bytes accessed | tf_op | source)
XLA Modules:
  0.0 874.6 jit_solution(16217998963531837268)
XLA Ops:
  19.1 37.8 %all-gather.6.cloned.1.call-done.weight_ref = bf16[2560,1024]{1,0:T(8,128)(2,1)} async-done(((bf16[320,1024]{1,0:T(8,128)(2,1)}), bf16[2560,1024]{1,0:T(8,128)(2,1)}) %all-gather.6.cloned.1.call-update) | async-done | bytes 5242896 | tf_op jit(solution)/shard_map/all_gather | solution.py:670
  62.2 10.5 %project.1 = (bf16[768,2560]{1,0:T(8,128)(2,1)}, bf16[768,640]{1,0:T(8,128)(2,1)S(1)}, bf16[768,320]{1,0:T(8,128)(2,1)S(1)}) custom-call(bf16[768,2560]{1,0:T(8,128)(2,1)} %bitcast.81, f32[1,2560]{1,0:T(1,128)S(1)} %copy.39.gain_ref, bf16[2560,1024]{1,0:T(8,128)(2,1)} %all-gather.6.cloned.1.call-done.weight_ref, f32[192,1024]{1,0:T(8,128)S(1)} %concatenate.106.cos_ref, ...), custom_call_target="tpu_custom_call" | custom-call | flops 4026531840 | bytes 13107200 | tf_op jit(solution)/shard_map/project/pallas_call | solution.py:275
  84.6 15.9 %collective-permute-done.1 = bf16[2,384,320]{1,2,0:T(8,128)(2,1)S(1)} collective-permute-done((bf16[2,384,320]{1,2,0:T(8,128)(2,1)S(1)}, bf16[2,384,320]{1,2,0:T(8,128)(2,1)S(1)}, u32[]{:S(2)}, u32[]{:S(2)}) %collective-permute-start.1) | collective-permute-done | bytes 491552 | tf_op jit(solution)/shard_map/ppermute | solution.py:62
  106.0 13.9 %collective-permute-done.15 = bf16[1,384,320]{2,1,0:T(8,128)(2,1)S(1)} collective-permute-done((bf16[1,384,320]{2,1,0:T(8,128)(2,1)S(1)}, bf16[1,384,320]{2,1,0:T(8,128)(2,1)S(1)}, u32[]{:S(2)}, u32[]{:S(2)}) %collective-permute-start.15) | collective-permute-done | bytes 245792 | tf_op jit(solution)/shard_map/ppermute | solution.py:62
  184.8 10.8 %collective-permute-done.18 = bf16[96,2560]{1,0:T(8,128)(2,1)S(1)} collective-permute-done((bf16[96,2560]{1,0:T(8,128)(2,1)S(1)}, bf16[96,2560]{1,0:T(8,128)(2,1)S(1)}, u32[]{:S(2)}, u32[]{:S(2)}) %collective-permute-start.18) | collective-permute-done | bytes 491552 | tf_op jit(solution)/shard_map/ppermute | solution.py:174
  235.4 9.9 %collective-permute-done.23 = bf16[96,2560]{1,0:T(8,128)(2,1)S(1)} collective-permute-done((bf16[96,2560]{1,0:T(8,128)(2,1)S(1)}, bf16[96,2560]{1,0:T(8,128)(2,1)S(1)}, u32[]{:S(2)}, u32[]{:S(2)}) %collective-permute-start.23) | collective-permute-done | bytes 491552 | tf_op jit(solution)/shard_map/ppermute | solution.py:175
  256.5 11.3 %collective-permute-done.24 = bf16[96,2560]{1,0:T(8,128)(2,1)} collective-permute-done((bf16[96,2560]{1,0:T(8,128)(2,1)S(1)}, bf16[96,2560]{1,0:T(8,128)(2,1)}, u32[]{:S(2)}, u32[]{:S(2)}) %collective-permute-start.24) | collective-permute-done | bytes 491552 | tf_op jit(solution)/shard_map/ppermute | solution.py:81
  267.8 12.0 %all-gather.12.cloned.1.call-done.up_ref.refs_3_ = bf16[2560,1728]{1,0:T(8,128)(2,1)} async-done(((bf16[320,1728]{1,0:T(8,128)(2,1)}), bf16[2560,1728]{1,0:T(8,128)(2,1)}) %all-gather.12.cloned.1.call-update) | async-done | bytes 8847376 | tf_op jit(solution)/shard_map/all_gather | solution.py:673
  279.8 12.1 %collective-permute-start.14 = (bf16[96,2560]{1,0:T(8,128)(2,1)}, bf16[96,2560]{1,0:T(8,128)(2,1)S(1)}, u32[]{:S(2)}, u32[]{:S(2)}) collective-permute-start(bf16[96,2560]{1,0:T(8,128)(2,1)} %copy-done.107), channel_id=1, source_target_pairs={{2,3},{6,7},{10,11},{14,15},{18,19},{22,23},{26,27},{30,31}} | collective-permute-start | bytes 1474568 | tf_op jit(solution)/shard_map/ppermute | solution.py:202
  295.3 16.8 %feed.2 = (bf16[384,1728]{1,0:T(8,128)(2,1)S(1)}, bf16[384,1728]{1,0:T(8,128)(2,1)S(1)}, bf16[384,1728]{1,0:T(8,128)(2,1)S(1)}) custom-call(bf16[384,2560]{1,0:T(8,128)(2,1)S(1)} %select_dynamic-update-slice_fusion.input_ref, bf16[384,2560]{1,0:T(8,128)(2,1)} %get-tuple-element.167.grad_ref, ...), custom_call_target="tpu_custom_call" | custom-call | flops 5096079360 | bytes 17227776 | tf_op jit(solution)/shard_map/feed/pallas_call | solution.py:320
  317.6 13.2 %back_through.3 = bf16[384,2560]{1,0:T(8,128)(2,1)S(1)} custom-call(bf16[384,1728]{1,0:T(8,128)(2,1)S(1)} %get-tuple-element.69.refs_0_, bf16[384,1728]{1,0:T(8,128)(2,1)S(1)} %get-tuple-element.70.refs_1_, bf16[2560,1728]{1,0:T(8,128)(2,1)} %all-gather.10.cloned.1.call-done.gate_ref.refs_2_, bf16[2560,1728]{1,0:T(8,128)(2,1)} %all-gather.12.cloned.1.call-done.up_ref.refs_3_), custom_call_target="tpu_custom_call" | custom-call | flops 3397386240 | bytes 11157504 | tf_op jit(solution)/shard_map/back_through/pallas_call | solution.py:350
  334.9 16.8 %feed.3 = (bf16[384,1728]{1,0:T(8,128)(2,1)S(1)}, bf16[384,1728]{1,0:T(8,128)(2,1)S(1)}, bf16[384,1728]{1,0:T(8,128)(2,1)S(1)}) custom-call(bf16[384,2560]{1,0:T(8,128)(2,1)S(1)} %pad_maximum_fusion.5.input_ref, bf16[384,2560]{1,0:T(8,128)(2,1)} %get-tuple-element.166.grad_ref, bf16[2560,1728]{1,0:T(8,128)(2,1)} %all-gather.10.cloned.1.call-done.gate_ref.refs_2_, ...), custom_call_target="tpu_custom_call" | custom-call | flops 5096079360 | bytes 17227776 | tf_op jit(solution)/shard_map/feed/pallas_call | solution.py:320
  376.4 13.4 %back_through.4 = bf16[384,2560]{1,0:T(8,128)(2,1)S(1)} custom-call(bf16[384,1728]{1,0:T(8,128)(2,1)S(1)} %copy-done.14, bf16[384,1728]{1,0:T(8,128)(2,1)S(1)} %copy-done.9, bf16[2560,1728]{1,0:T(8,128)(2,1)} %all-gather.10.cloned.1.call-done.gate_ref.refs_2_, bf16[2560,1728]{1,0:T(8,128)(2,1)} %all-gather.12.cloned.1.call-done.up_ref.refs_3_), custom_call_target="tpu_custom_call" | custom-call | flops 3397386240 | bytes 11157504 | tf_op jit(solution)/shard_map/back_through/pallas_call | solution.py:350
  398.8 13.8 %back_through.5 = bf16[768,2560]{1,0:T(8,128)(2,1)} custom-call(bf16[768,1728]{1,0:T(8,128)(2,1)S(1)} %copy-done.3, bf16[2560,1728]{1,0:T(8,128)(2,1)} %all-gather.14.cloned.1.call-done.down_ref.refs_1_), custom_call_target="tpu_custom_call" | custom-call | flops 3397386240 | bytes 7716864 | tf_op jit(solution)/shard_map/back_through/pallas_call | solution.py:350
  412.6 12.8 %collective-permute-done.30 = bf16[192,2560]{1,0:T(8,128)(2,1)S(1)} collective-permute-done((bf16[192,2560]{1,0:T(8,128)(2,1)S(1)}, bf16[192,2560]{1,0:T(8,128)(2,1)S(1)}, u32[]{:S(2)}, u32[]{:S(2)}) %collective-permute-start.30) | collective-permute-done | bytes 983072 | tf_op jit(solution)/shard_map/ppermute | solution.py:81
  448.7 10.1 %convolution_convert_fusion = bf16[2560,1728]{1,0:T(8,128)(2,1)} fusion(bf16[768,2560]{1,0:T(8,128)(2,1)S(1)} %copy-done.87, bf16[384,1728]{1,0:T(8,128)(2,1)S(1)} %copy-done.10, bf16[384,1728]{1,0:T(8,128)(2,1)S(1)} %copy-done.7), kind=kOutput, calls=%fused_computation | convolution fusion | flops 6804504576 | bytes 15433728 | tf_op jit(solution)/shard_map/dot_general | solution.py:24
  458.8 10.0 %collective-permute-done.35 = bf16[96,2560]{1,0:T(8,128)(2,1)} collective-permute-done((bf16[96,2560]{1,0:T(8,128)(2,1)}, bf16[96,2560]{1,0:T(8,128)(2,1)}, u32[]{:S(2)}, u32[]{:S(2)}) %collective-permute-start.35) | collective-permute-done | bytes 491552 | tf_op jit(solution)/shard_map/ppermute | solution.py:81
  473.5 10.3 %collective-permute-done.29 = bf16[192,2560]{1,0:T(8,128)(2,1)} collective-permute-done((bf16[192,2560]{1,0:T(8,128)(2,1)}, bf16[192,2560]{1,0:T(8,128)(2,1)}, u32[]{:S(2)}, u32[]{:S(2)}) %collective-permute-start.29) | collective-permute-done | bytes 983072 | tf_op jit(solution)/shard_map/ppermute | solution.py:81
  508.3 19.1 %collective-permute-done.31 = bf16[192,2560]{1,0:T(8,128)(2,1)} collective-permute-done((bf16[192,2560]{1,0:T(8,128)(2,1)}, bf16[192,2560]{1,0:T(8,128)(2,1)}, u32[]{:S(2)}, u32[]{:S(2)}) %collective-permute-start.31) | collective-permute-done | bytes 983072 | tf_op jit(solution)/shard_map/ppermute | solution.py:81
  529.8 18.1 %collective-permute-done.37 = bf16[192,2560]{1,0:T(8,128)(2,1)} collective-permute-done((bf16[192,2560]{1,0:T(8,128)(2,1)}, bf16[192,2560]{1,0:T(8,128)(2,1)}, u32[]{:S(2)}, u32[]{:S(2)}) %collective-permute-start.37) | collective-permute-done | bytes 983072 | tf_op jit(solution)/shard_map/ppermute | solution.py:81
  577.5 14.1 %collective-permute-start.43 = (bf16[2,384,320]{1,2,0:T(8,128)(2,1)}, bf16[2,384,320]{1,2,0:T(8,128)(2,1)S(1)}, u32[]{:S(2)}, u32[]{:S(2)}) collective-permute-start(bf16[2,384,320]{1,2,0:T(8,128)(2,1)} %copy.53), channel_id=1, source_target_pairs={{0,16},{4,20},{8,24},{12,28},{16,0},{20,4},{24,8},{28,12},{1,17},{... | collective-permute-start | bytes 1474568 | tf_op jit(solution)/shard_map/ppermute | solution.py:242
  666.2 24.9 %collective-permute-done.46 = bf16[192,2560]{1,0:T(8,128)(2,1)} collective-permute-done((bf16[192,2560]{1,0:T(8,128)(2,1)}, bf16[192,2560]{1,0:T(8,128)(2,1)}, u32[]{:S(2)}, u32[]{:S(2)}) %collective-permute-start.46) | collective-permute-done | bytes 983072 | tf_op jit(solution)/shard_map/ppermute | solution.py:81
  695.8 22.3 %collective-permute-done.47 = bf16[96,2560]{1,0:T(8,128)(2,1)S(1)} collective-permute-done((bf16[96,2560]{1,0:T(8,128)(2,1)S(1)}, bf16[96,2560]{1,0:T(8,128)(2,1)S(1)}, u32[]{:S(2)}, u32[]{:S(2)}) %collective-permute-start.47) | collective-permute-done | bytes 491552 | tf_op jit(solution)/shard_map/ppermute | solution.py:81
  758.7 21.4 %collective-permute-done.57 = bf16[96,2560]{1,0:T(8,128)(2,1)S(1)} collective-permute-done((bf16[96,2560]{1,0:T(8,128)(2,1)S(1)}, bf16[96,2560]{1,0:T(8,128)(2,1)S(1)}, u32[]{:S(2)}, u32[]{:S(2)}) %collective-permute-start.57) | collective-permute-done | bytes 491552 | tf_op jit(solution)/shard_map/ppermute | solution.py:81
  (575 shorter events, 486.6 us)
Async XLA Ops:
  7.2 49.7 %all-gather.6.cloned.1.call-start = ((), (), s32[]{:S(2)}) async-start(), calls=%async_computation.4 | async-start | bytes 5898240 | tf_op jit(solution)/shard_map/all_gather | solution.py:670
  12.9 118.1 %all-gather.8.cloned.1.call-start = ((), (), s32[]{:S(2)}) async-start(), calls=%async_computation.5 | async-start | bytes 3686400 | tf_op jit(solution)/shard_map/all_gather | solution.py:671
  13.6 254.2 %all-gather.14.cloned.1.call-start = ((), (), s32[]{:S(2)}) async-start(), calls=%async_computation.8 | async-start | bytes 10321920 | tf_op jit(solution)/shard_map/all_gather | solution.py:674
  14.4 253.4 %all-gather.10.cloned.1.call-start = ((), (), s32[]{:S(2)}) async-start(), calls=%async_computation.6 | async-start | bytes 10321920 | tf_op jit(solution)/shard_map/all_gather | solution.py:672
  14.9 264.9 %all-gather.12.cloned.1.call-start = ((), (), s32[]{:S(2)}) async-start(), calls=%async_computation.7 | async-start | bytes 10321920 | tf_op jit(solution)/shard_map/all_gather | solution.py:673
  15.5 704.3 %reduce-scatter.5.cloned.1.call-start = ((), (), s32[]{:S(2)}) async-start(), calls=%async_computation.9 | async-start | bytes 10321920 | tf_op jit(solution)/shard_map/reduce_scatter | solution.py:762
  223.8 32.0 %collective-permute-start.13 = (bf16[96,2560]{1,0:T(8,128)(2,1)S(1)}, bf16[96,2560]{1,0:T(8,128)(2,1)S(1)}, u32[]{:S(2)}, u32[]{:S(2)}) collective-permute-start(bf16[96,2560]{1,0:T(8,128)(2,1)S(1)} %collective-permute-done.9), channel_id=1, source_target_pairs={{1,2},{2,3},{5,6},{6,7},{9,10},{10,11},{13,14},{14,15},{17,18},{18... | collective-permute-start | bytes 1474568 | tf_op jit(solution)/shard_map/ppermute | solution.py:202
  389.9 35.6 %collective-permute-start.30 = (bf16[192,2560]{1,0:T(8,128)(2,1)S(1)}, bf16[192,2560]{1,0:T(8,128)(2,1)S(1)}, u32[]{:S(2)}, u32[]{:S(2)}) collective-permute-start(bf16[192,2560]{1,0:T(8,128)(2,1)S(1)} %constant_dynamic-slice_fusion.10), channel_id=1, source_target_pairs={{0,1},{1,0},{2,3},{3,2},{4,5},{5,4},{6,7},{7,6},{8,9},{9,8},{10,11... | collective-permute-start | bytes 2949128 | tf_op jit(solution)/shard_map/ppermute | solution.py:81
  396.8 28.6 %collective-permute-start.28 = (bf16[96,2560]{1,0:T(8,128)(2,1)S(1)}, bf16[96,2560]{1,0:T(8,128)(2,1)S(1)}, u32[]{:S(2)}, u32[]{:S(2)}) collective-permute-start(bf16[96,2560]{1,0:T(8,128)(2,1)S(1)} %get-tuple-element.156), channel_id=1, source_target_pairs={{0,2},{1,3},{2,0},{3,1},{4,6},{5,7},{6,4},{7,5},{8,10},{9,11},{10,... | collective-permute-start | bytes 1474568 | tf_op jit(solution)/shard_map/ppermute | solution.py:81
  436.9 418.2 %reduce-scatter.11.cloned.1.call-start = ((), (), s32[]{:S(2)}) async-start(), calls=%async_computation.12 | async-start | bytes 10321920 | tf_op jit(solution)/shard_map/reduce_scatter | solution.py:762
  437.7 421.7 %reduce-scatter.9.cloned.1.call-start = ((), (), s32[]{:S(2)}) async-start(), calls=%async_computation.11 | async-start | bytes 10321920 | tf_op jit(solution)/shard_map/reduce_scatter | solution.py:762
  446.2 37.5 %collective-permute-start.29 = (bf16[192,2560]{1,0:T(8,128)(2,1)}, bf16[192,2560]{1,0:T(8,128)(2,1)}, u32[]{:S(2)}, u32[]{:S(2)}) collective-permute-start(bf16[192,2560]{1,0:T(8,128)(2,1)} %pad_maximum_fusion.13), channel_id=1, source_target_pairs={{0,1},{1,0},{2,3},{3,2},{4,5},{5,4},{6,7},{7,6},{8,9},{9,8},{10,11... | collective-permute-start | bytes 2949128 | tf_op jit(solution)/shard_map/ppermute | solution.py:81
  473.5 29.0 %collective-permute-start.36 = (bf16[96,2560]{1,0:T(8,128)(2,1)}, bf16[96,2560]{1,0:T(8,128)(2,1)}, u32[]{:S(2)}, u32[]{:S(2)}) collective-permute-start(bf16[96,2560]{1,0:T(8,128)(2,1)} %get-tuple-element.154), channel_id=1, source_target_pairs={{0,2},{1,3},{2,0},{3,1},{4,6},{5,7},{6,4},{7,5},{8,10},{9,11},{10,... | collective-permute-start | bytes 1474568 | tf_op jit(solution)/shard_map/ppermute | solution.py:81
  505.0 43.0 %collective-permute-start.37 = (bf16[192,2560]{1,0:T(8,128)(2,1)}, bf16[192,2560]{1,0:T(8,128)(2,1)}, u32[]{:S(2)}, u32[]{:S(2)}) collective-permute-start(bf16[192,2560]{1,0:T(8,128)(2,1)} %pad_maximum_fusion.15), channel_id=1, source_target_pairs={{0,1},{1,0},{2,3},{3,2},{4,5},{5,4},{6,7},{7,6},{8,9},{9,8},{10,11... | collective-permute-start | bytes 2949128 | tf_op jit(solution)/shard_map/ppermute | solution.py:81
  508.2 354.1 %reduce-scatter.7.cloned.1.call-start = ((), (), s32[]{:S(2)}) async-start(), calls=%async_computation.10 | async-start | bytes 9584640 | tf_op jit(solution)/shard_map/reduce_scatter | solution.py:762
  553.5 50.0 %collective-permute-start.38 = (bf16[192,2560]{1,0:T(8,128)(2,1)}, bf16[192,2560]{1,0:T(8,128)(2,1)}, u32[]{:S(2)}, u32[]{:S(2)}) collective-permute-start(bf16[192,2560]{1,0:T(8,128)(2,1)} %constant_dynamic-slice_fusion.8), channel_id=1, source_target_pairs={{0,1},{1,0},{2,3},{3,2},{4,5},{5,4},{6,7},{7,6},{8,9},{9,8},{10,11... | collective-permute-start | bytes 2949128 | tf_op jit(solution)/shard_map/ppermute | solution.py:81
  558.7 32.9 %collective-permute-start.32 = (bf16[96,2560]{1,0:T(8,128)(2,1)}, bf16[96,2560]{1,0:T(8,128)(2,1)}, u32[]{:S(2)}, u32[]{:S(2)}) collective-permute-start(bf16[96,2560]{1,0:T(8,128)(2,1)} %dynamic-slice_convert_fusion.4), channel_id=1, source_target_pairs={{0,2},{1,3},{2,0},{3,1},{4,6},{5,7},{6,4},{7,5},{8,10},{9,11},{10,... | collective-permute-start | bytes 1474568 | tf_op jit(solution)/shard_map/ppermute | solution.py:81
  571.5 33.7 %collective-permute-start.45 = (bf16[4,384,320]{1,2,0:T(8,128)(2,1)}, bf16[4,384,320]{1,2,0:T(8,128)(2,1)}, u32[]{:S(2)}, u32[]{:S(2)}) collective-permute-start(bf16[4,384,320]{1,2,0:T(8,128)(2,1)} %copy.57), channel_id=1, source_target_pairs={{0,4},{4,0},{8,12},{12,8},{16,20},{20,16},{24,28},{28,24},{1,5},{5... | collective-permute-start | bytes 2949128 | tf_op jit(solution)/shard_map/ppermute | solution.py:233
  624.4 128.0 %collective-permute-start.34 = (bf16[192,2560]{1,0:T(8,128)(2,1)}, bf16[192,2560]{1,0:T(8,128)(2,1)}, u32[]{:S(2)}, u32[]{:S(2)}) collective-permute-start(bf16[192,2560]{1,0:T(8,128)(2,1)} %pad_maximum_fusion.14), channel_id=1, source_target_pairs={{0,1},{1,0},{2,3},{3,2},{4,5},{5,4},{6,7},{7,6},{8,9},{9,8},{10,11... | collective-permute-start | bytes 2949128 | tf_op jit(solution)/shard_map/ppermute | solution.py:81
  633.2 58.0 %collective-permute-start.46 = (bf16[192,2560]{1,0:T(8,128)(2,1)}, bf16[192,2560]{1,0:T(8,128)(2,1)}, u32[]{:S(2)}, u32[]{:S(2)}) collective-permute-start(bf16[192,2560]{1,0:T(8,128)(2,1)} %constant_dynamic-slice_fusion.7), channel_id=1, source_target_pairs={{0,1},{1,0},{2,3},{3,2},{4,5},{5,4},{6,7},{7,6},{8,9},{9,8},{10,11... | collective-permute-start | bytes 2949128 | tf_op jit(solution)/shard_map/ppermute | solution.py:81
  645.9 46.9 %collective-permute-start.40 = (bf16[96,2560]{1,0:T(8,128)(2,1)S(1)}, bf16[96,2560]{1,0:T(8,128)(2,1)S(1)}, u32[]{:S(2)}, u32[]{:S(2)}) collective-permute-start(bf16[96,2560]{1,0:T(8,128)(2,1)S(1)} %add_convert_fusion.4), channel_id=1, source_target_pairs={{0,2},{1,3},{2,0},{3,1},{4,6},{5,7},{6,4},{7,5},{8,10},{9,11},{10,... | collective-permute-start | bytes 1474568 | tf_op jit(solution)/shard_map/ppermute | solution.py:81
  659.8 86.4 %collective-permute-start.56 = (bf16[192,2560]{1,0:T(8,128)(2,1)}, bf16[192,2560]{1,0:T(8,128)(2,1)}, u32[]{:S(2)}, u32[]{:S(2)}) collective-permute-start(bf16[192,2560]{1,0:T(8,128)(2,1)} %constant_dynamic-slice_fusion.6), channel_id=1, source_target_pairs={{0,1},{1,0},{2,3},{3,2},{4,5},{5,4},{6,7},{7,6},{8,9},{9,8},{10,11... | collective-permute-start | bytes 2949128 | tf_op jit(solution)/shard_map/ppermute | solution.py:81
  694.3 94.0 %collective-permute-start.41 = (bf16[192,2560]{1,0:T(8,128)(2,1)}, bf16[192,2560]{1,0:T(8,128)(2,1)}, u32[]{:S(2)}, u32[]{:S(2)}) collective-permute-start(bf16[192,2560]{1,0:T(8,128)(2,1)} %pad_maximum_fusion.16), channel_id=1, source_target_pairs={{0,1},{1,0},{2,3},{3,2},{4,5},{5,4},{6,7},{7,6},{8,9},{9,8},{10,11... | collective-permute-start | bytes 2949128 | tf_op jit(solution)/shard_map/ppermute | solution.py:81
  748.0 32.0 %collective-permute-start.57 = (bf16[96,2560]{1,0:T(8,128)(2,1)S(1)}, bf16[96,2560]{1,0:T(8,128)(2,1)S(1)}, u32[]{:S(2)}, u32[]{:S(2)}) collective-permute-start(bf16[96,2560]{1,0:T(8,128)(2,1)S(1)} %dynamic-slice_convert_fusion), channel_id=1, source_target_pairs={{0,2},{1,3},{2,0},{3,1},{4,6},{5,7},{6,4},{7,5},{8,10},{9,11},{10,... | collective-permute-start | bytes 1474568 | tf_op jit(solution)/shard_map/ppermute | solution.py:81
  (170 other events, 1843.8 us)
Sparse Core Ops, SparseCore 0:
  13.0 43.8 all-gather.5
  58.7 37.5 all-gather.7
  98.2 62.5 all-gather.13
  162.6 57.7 all-gather.9
  222.0 57.7 all-gather.11
  437.1 74.8 reduce-scatter.4
  516.1 75.0 reduce-scatter.10
  594.8 82.2 reduce-scatter.8
  737.6 72.6 reduce-scatter.6

commit v4 on v3

--- a/solution.py
+++ b/solution.py
@@ -345,7 +345,7 @@
 def back_through(values, weights):
     rows, units = values[0].shape
     width = weights[0].shape[0]
-    tile = 256
+    tile = 512
     count = len(values)
     return pl.pallas_call(
         back_kernel,
@@ -885,9 +885,7 @@
     tokens0.next()
     gain3, total1 = tokens_back(1, one1.finish(tokens0_first), grad_hidden1)
     tokens1 = ChainGather(total1)
-    mixed_parts = [whole_mixed0.finish(), whole_mixed1.finish()]
-    token_parts = [tokens0.finish(), tokens1.finish()]
-    gain_terms = after(jnp.stack([gain2 + gain3, gain0 + gain1]), tokens1.landed)
+    gain_terms = after(jnp.stack([gain2 + gain3, gain0 + gain1]), total1)
     for bit in line_bits():
         gain_terms = gain_terms + line_swap(gain_terms, bit)
     gain_terms = jnp.swapaxes(
@@ -899,8 +897,16 @@
         got = lax.ppermute(take_chunk(gain_terms, 1 - mine, half), "ctx", flip(bit))
         gain_terms = take_chunk(gain_terms, mine, half) + got
     gain_terms = gain_terms[0]
-    mixed = jnp.stack(mixed_parts, axis=0).reshape(tokens.shape)
-    token_grad = jnp.stack(token_parts, axis=0).reshape(tokens.shape).astype(jnp.float32)
+    gate_out = gate_grad.astype(jnp.float32)
+    up_out = up_grad.astype(jnp.float32)
+    down_out = down_grad.T.astype(jnp.float32)
+    tokens1.next(gain_terms)
+    mixed = jnp.stack([whole_mixed0.finish(), whole_mixed1.finish()], axis=0).reshape(tokens.shape)
+    token_grad = (
+        jnp.stack([tokens0.finish(), tokens1.finish(gate_out, up_out, down_out)], axis=0)
+        .reshape(tokens.shape)
+        .astype(jnp.float32)
+    )
     return (
         mixed,
         token_grad,
@@ -910,9 +916,9 @@
         qkv_grad[:, q_cols + kv_cols :],
         out_grad.T,
         gain_terms[1],
-        gate_grad.astype(jnp.float32),
-        up_grad.astype(jnp.float32),
-        down_grad.T.astype(jnp.float32),
+        gate_out,
+        up_out,
+        down_out,
     )
 
 

time: 890 us -> 882 us (level)
    ppermute x9, waiting for transfers between devices: 45.7 us -> 35.1 us  [send(): lax.ppermute(self.landed[1], 'head', [(i, i - 1) for i in range(1, n - st...]
    ppermute x24, waiting for transfers between devices: 169 us -> 178 us  [line_swap(): return lax.ppermute(value, 'head', [(i, i ^ bit) for i in range(n)])]
    ppermute x9, starting transfers between devices: 29.3 us -> 20.1 us  [send(): lax.ppermute(self.landed[0], 'head', [(i, i + 1) for i in range(step, n -...]
    unnamed x243 -> x229, local copies, waits for them, and re-layouts: 33.4 us -> 32.8 us
  transfers between devices with their start and end apart: 78 -> 78, of which waited for: 39 -> 33; matrix products, arithmetic and copies ran while one was open for 22% -> 23% of each run, Pallas kernels for 11% -> 11%
where the time goes in v4:
time: 882 us; the launch traced here: 870 us
  waiting for transfers between devices  356 us (40%)
  starting transfers between devices  135 us (15%)
  Pallas kernels  104 us (12%)
  other arithmetic  99.2 us (11%)
  local copies, waits for them, and re-layouts  95.9 us (11%)
  matrix products  62.1 us (7%)
  between operations  16.8 us (2%)
    ppermute x24, waiting for transfers between devices, line_swap(): return lax.ppermute(value, 'head', [(i, i ^ bit) for i in range(n)])  178 us
    dot_general x11, matrix products, dot(): lax.dot_general(left, right, (((a,), (b,)), ((), ())), preferred_element_...  62.1 us
    ppermute x24, starting transfers between devices, line_swap(): return lax.ppermute(value, 'head', [(i, i ^ bit) for i in range(n)])  43.1 us
    ppermute x4, waiting for transfers between devices, cube_gather(): got = lax.ppermute(own, 'ctx', flip(bit))  39 us
    all_gather x1, waiting for transfers between devices, per_device(): full_qkv = lax.all_gather(qkv_shard, 'ctx', axis=0, tiled=True)  37.8 us
    ppermute x9, waiting for transfers between devices, send(): lax.ppermute(self.landed[1], 'head', [(i, i - 1) for i in range(1, n - st...  35.1 us
    pallas_call x3, Pallas kernels, back_through(): pl.pallas_call(back_kernel, grid=((width + tile - 1) // tile,), in_specs=...  34.6 us
    pallas_call x2, Pallas kernels, feed(): pl.pallas_call(feed_kernel, grid=((units + tile - 1) // tile,), in_specs=...  33.7 us
  transfers between devices with their start and end apart: 78, of which 33 were waited for; matrix products, arithmetic and copies ran while one was open for 23% of the time, Pallas kernels for 11%

profile of v4, /device:TPU:0, one launch (start us, length us, event | category | flops | bytes accessed | tf_op | source)
XLA Modules:
  0.0 869.7 jit_solution(13951522456448502296)
XLA Ops:
  19.1 37.8 %all-gather.6.cloned.1.call-done.weight_ref = bf16[2560,1024]{1,0:T(8,128)(2,1)} async-done(((bf16[320,1024]{1,0:T(8,128)(2,1)}), bf16[2560,1024]{1,0:T(8,128)(2,1)}) %all-gather.6.cloned.1.call-update) | async-done | bytes 5242896 | tf_op jit(solution)/shard_map/all_gather | solution.py:670
  62.2 10.5 %project.1 = (bf16[768,2560]{1,0:T(8,128)(2,1)}, bf16[768,640]{1,0:T(8,128)(2,1)S(1)}, bf16[768,320]{1,0:T(8,128)(2,1)S(1)}) custom-call(bf16[768,2560]{1,0:T(8,128)(2,1)} %bitcast.81, f32[1,2560]{1,0:T(1,128)S(1)} %copy.39.gain_ref, bf16[2560,1024]{1,0:T(8,128)(2,1)} %all-gather.6.cloned.1.call-done.weight_ref, f32[192,1024]{1,0:T(8,128)S(1)} %concatenate.106.cos_ref, ...), custom_call_target="tpu_custom_call" | custom-call | flops 4026531840 | bytes 13107200 | tf_op jit(solution)/shard_map/project/pallas_call | solution.py:275
  84.6 15.9 %collective-permute-done.1 = bf16[2,384,320]{1,2,0:T(8,128)(2,1)S(1)} collective-permute-done((bf16[2,384,320]{1,2,0:T(8,128)(2,1)S(1)}, bf16[2,384,320]{1,2,0:T(8,128)(2,1)S(1)}, u32[]{:S(2)}, u32[]{:S(2)}) %collective-permute-start.1) | collective-permute-done | bytes 491552 | tf_op jit(solution)/shard_map/ppermute | solution.py:62
  106.0 14.0 %collective-permute-done.15 = bf16[1,384,320]{2,1,0:T(8,128)(2,1)S(1)} collective-permute-done((bf16[1,384,320]{2,1,0:T(8,128)(2,1)S(1)}, bf16[1,384,320]{2,1,0:T(8,128)(2,1)S(1)}, u32[]{:S(2)}, u32[]{:S(2)}) %collective-permute-start.15) | collective-permute-done | bytes 245792 | tf_op jit(solution)/shard_map/ppermute | solution.py:62
  184.9 10.7 %collective-permute-done.18 = bf16[96,2560]{1,0:T(8,128)(2,1)S(1)} collective-permute-done((bf16[96,2560]{1,0:T(8,128)(2,1)S(1)}, bf16[96,2560]{1,0:T(8,128)(2,1)S(1)}, u32[]{:S(2)}, u32[]{:S(2)}) %collective-permute-start.18) | collective-permute-done | bytes 491552 | tf_op jit(solution)/shard_map/ppermute | solution.py:174
  256.6 11.3 %collective-permute-done.24 = bf16[96,2560]{1,0:T(8,128)(2,1)} collective-permute-done((bf16[96,2560]{1,0:T(8,128)(2,1)S(1)}, bf16[96,2560]{1,0:T(8,128)(2,1)}, u32[]{:S(2)}, u32[]{:S(2)}) %collective-permute-start.24) | collective-permute-done | bytes 491552 | tf_op jit(solution)/shard_map/ppermute | solution.py:81
  267.8 12.0 %all-gather.12.cloned.1.call-done.up_ref.refs_3_ = bf16[2560,1728]{1,0:T(8,128)(2,1)} async-done(((bf16[320,1728]{1,0:T(8,128)(2,1)}), bf16[2560,1728]{1,0:T(8,128)(2,1)}) %all-gather.12.cloned.1.call-update) | async-done | bytes 8847376 | tf_op jit(solution)/shard_map/all_gather | solution.py:673
  284.0 17.0 %feed.2 = (bf16[384,1728]{1,0:T(8,128)(2,1)S(1)}, bf16[384,1728]{1,0:T(8,128)(2,1)S(1)}, bf16[384,1728]{1,0:T(8,128)(2,1)S(1)}) custom-call(bf16[384,2560]{1,0:T(8,128)(2,1)S(1)} %select_dynamic-update-slice_fusion.input_ref, bf16[384,2560]{1,0:T(8,128)(2,1)} %get-tuple-element.167.grad_ref, ...), custom_call_target="tpu_custom_call" | custom-call | flops 5096079360 | bytes 17227776 | tf_op jit(solution)/shard_map/feed/pallas_call | solution.py:320
  306.3 11.1 %back_through.3 = bf16[384,2560]{1,0:T(8,128)(2,1)S(1)} custom-call(bf16[384,1728]{1,0:T(8,128)(2,1)S(1)} %get-tuple-element.70.refs_0_, bf16[384,1728]{1,0:T(8,128)(2,1)S(1)} %get-tuple-element.71.refs_1_, bf16[2560,1728]{1,0:T(8,128)(2,1)} %all-gather.10.cloned.1.call-done.gate_ref.refs_2_, bf16[2560,1728]{1,0:T(8,128)(2,1)} %all-gather.12.cloned.1.call-done.up_ref.refs_3_), custom_call_target="tpu_custom_call" | custom-call | flops 3397386240 | bytes 11157504 | tf_op jit(solution)/shard_map/back_through/pallas_call | solution.py:350
  321.6 16.8 %feed.3 = (bf16[384,1728]{1,0:T(8,128)(2,1)S(1)}, bf16[384,1728]{1,0:T(8,128)(2,1)S(1)}, bf16[384,1728]{1,0:T(8,128)(2,1)S(1)}) custom-call(bf16[384,2560]{1,0:T(8,128)(2,1)S(1)} %pad_maximum_fusion.5.input_ref, bf16[384,2560]{1,0:T(8,128)(2,1)} %get-tuple-element.166.grad_ref, bf16[2560,1728]{1,0:T(8,128)(2,1)} %all-gather.10.cloned.1.call-done.gate_ref.refs_2_, ...), custom_call_target="tpu_custom_call" | custom-call | flops 5096079360 | bytes 17227776 | tf_op jit(solution)/shard_map/feed/pallas_call | solution.py:320
  355.7 12.4 %collective-permute-start.27 = (bf16[96,2560]{1,0:T(8,128)(2,1)S(1)}, bf16[96,2560]{1,0:T(8,128)(2,1)S(1)}, u32[]{:S(2)}, u32[]{:S(2)}) collective-permute-start(bf16[96,2560]{1,0:T(8,128)(2,1)S(1)} %dynamic-slice_convert_fusion.5), channel_id=1, source_target_pairs={{0,2},{1,3},{2,0},{3,1},{4,6},{5,7},{6,4},{7,5},{8,10},{9,11},{10,... | collective-permute-start | bytes 1474568 | tf_op jit(solution)/shard_map/ppermute | solution.py:81
  370.8 11.2 %back_through.4 = bf16[384,2560]{1,0:T(8,128)(2,1)S(1)} custom-call(bf16[384,1728]{1,0:T(8,128)(2,1)S(1)} %copy-done.14, bf16[384,1728]{1,0:T(8,128)(2,1)S(1)} %copy-done.9, bf16[2560,1728]{1,0:T(8,128)(2,1)} %all-gather.10.cloned.1.call-done.gate_ref.refs_2_, bf16[2560,1728]{1,0:T(8,128)(2,1)} %all-gather.12.cloned.1.call-done.up_ref.refs_3_), custom_call_target="tpu_custom_call" | custom-call | flops 3397386240 | bytes 11157504 | tf_op jit(solution)/shard_map/back_through/pallas_call | solution.py:350
  394.0 12.3 %back_through.5 = bf16[768,2560]{1,0:T(8,128)(2,1)} custom-call(bf16[768,1728]{1,0:T(8,128)(2,1)S(1)} %copy-done.3, bf16[2560,1728]{1,0:T(8,128)(2,1)} %all-gather.14.cloned.1.call-done.down_ref.refs_1_), custom_call_target="tpu_custom_call" | custom-call | flops 3397386240 | bytes 7716864 | tf_op jit(solution)/shard_map/back_through/pallas_call | solution.py:350
  406.3 14.3 %collective-permute-done.30 = bf16[192,2560]{1,0:T(8,128)(2,1)S(1)} collective-permute-done((bf16[192,2560]{1,0:T(8,128)(2,1)S(1)}, bf16[192,2560]{1,0:T(8,128)(2,1)S(1)}, u32[]{:S(2)}, u32[]{:S(2)}) %collective-permute-start.30) | collective-permute-done | bytes 983072 | tf_op jit(solution)/shard_map/ppermute | solution.py:81
  422.4 10.2 %convolution_convert_fusion.1 = bf16[2560,1728]{1,0:T(8,128)(2,1)} fusion(bf16[768,2560]{1,0:T(8,128)(2,1)S(1)} %pad_maximum_fusion.1, bf16[384,1728]{1,0:T(8,128)(2,1)S(1)} %copy-done.15, bf16[384,1728]{1,0:T(8,128)(2,1)S(1)} %copy-done.12), kind=kOutput, calls=%fused_computation.1 | convolution fusion | flops 6804504576 | bytes 15433728 | tf_op jit(solution)/shard_map/dot_general | solution.py:24
  454.4 10.2 %collective-permute-done.35 = bf16[96,2560]{1,0:T(8,128)(2,1)} collective-permute-done((bf16[96,2560]{1,0:T(8,128)(2,1)}, bf16[96,2560]{1,0:T(8,128)(2,1)}, u32[]{:S(2)}, u32[]{:S(2)}) %collective-permute-start.35) | collective-permute-done | bytes 491552 | tf_op jit(solution)/shard_map/ppermute | solution.py:81
  469.2 10.5 %collective-permute-done.29 = bf16[192,2560]{1,0:T(8,128)(2,1)} collective-permute-done((bf16[192,2560]{1,0:T(8,128)(2,1)}, bf16[192,2560]{1,0:T(8,128)(2,1)}, u32[]{:S(2)}, u32[]{:S(2)}) %collective-permute-start.29) | collective-permute-done | bytes 983072 | tf_op jit(solution)/shard_map/ppermute | solution.py:81
  504.3 19.1 %collective-permute-done.31 = bf16[192,2560]{1,0:T(8,128)(2,1)} collective-permute-done((bf16[192,2560]{1,0:T(8,128)(2,1)}, bf16[192,2560]{1,0:T(8,128)(2,1)}, u32[]{:S(2)}, u32[]{:S(2)}) %collective-permute-start.31) | collective-permute-done | bytes 983072 | tf_op jit(solution)/shard_map/ppermute | solution.py:81
  525.8 18.3 %collective-permute-done.37 = bf16[192,2560]{1,0:T(8,128)(2,1)} collective-permute-done((bf16[192,2560]{1,0:T(8,128)(2,1)}, bf16[192,2560]{1,0:T(8,128)(2,1)}, u32[]{:S(2)}, u32[]{:S(2)}) %collective-permute-start.37) | collective-permute-done | bytes 983072 | tf_op jit(solution)/shard_map/ppermute | solution.py:81
  573.3 14.1 %collective-permute-start.43 = (bf16[2,384,320]{1,2,0:T(8,128)(2,1)}, bf16[2,384,320]{1,2,0:T(8,128)(2,1)S(1)}, u32[]{:S(2)}, u32[]{:S(2)}) collective-permute-start(bf16[2,384,320]{1,2,0:T(8,128)(2,1)} %copy.53), channel_id=1, source_target_pairs={{0,16},{4,20},{8,24},{12,28},{16,0},{20,4},{24,8},{28,12},{1,17},{... | collective-permute-start | bytes 1474568 | tf_op jit(solution)/shard_map/ppermute | solution.py:242
  658.4 32.6 %collective-permute-done.46 = bf16[192,2560]{1,0:T(8,128)(2,1)} collective-permute-done((bf16[192,2560]{1,0:T(8,128)(2,1)}, bf16[192,2560]{1,0:T(8,128)(2,1)}, u32[]{:S(2)}, u32[]{:S(2)}) %collective-permute-start.46) | collective-permute-done | bytes 983072 | tf_op jit(solution)/shard_map/ppermute | solution.py:81
  697.7 18.3 %collective-permute-done.47 = bf16[96,2560]{1,0:T(8,128)(2,1)S(1)} collective-permute-done((bf16[96,2560]{1,0:T(8,128)(2,1)S(1)}, bf16[96,2560]{1,0:T(8,128)(2,1)S(1)}, u32[]{:S(2)}, u32[]{:S(2)}) %collective-permute-start.47) | collective-permute-done | bytes 491552 | tf_op jit(solution)/shard_map/ppermute | solution.py:81
  762.2 18.0 %collective-permute-done.64 = f32[2,2560]{1,0:T(2,128)S(1)} collective-permute-done((f32[2,2560]{1,0:T(2,128)S(1)}, f32[2,2560]{1,0:T(2,128)S(1)}, u32[]{:S(2)}, u32[]{:S(2)}) %collective-permute-start.64) | collective-permute-done | bytes 20512 | tf_op jit(solution)/shard_map/ppermute | solution.py:81
  817.6 17.5 %collective-permute-done.60 = bf16[96,2560]{1,0:T(8,128)(2,1)} collective-permute-done((bf16[96,2560]{1,0:T(8,128)(2,1)S(1)}, bf16[96,2560]{1,0:T(8,128)(2,1)}, u32[]{:S(2)}, u32[]{:S(2)}) %collective-permute-start.60) | collective-permute-done | bytes 491552 | tf_op jit(solution)/shard_map/ppermute | solution.py:203
  (562 shorter events, 477.1 us)
Async XLA Ops:
  7.2 49.7 %all-gather.6.cloned.1.call-start = ((), (), s32[]{:S(2)}) async-start(), calls=%async_computation.4 | async-start | bytes 5898240 | tf_op jit(solution)/shard_map/all_gather | solution.py:670
  12.9 118.2 %all-gather.8.cloned.1.call-start = ((), (), s32[]{:S(2)}) async-start(), calls=%async_computation.5 | async-start | bytes 3686400 | tf_op jit(solution)/shard_map/all_gather | solution.py:671
  13.6 254.2 %all-gather.14.cloned.1.call-start = ((), (), s32[]{:S(2)}) async-start(), calls=%async_computation.8 | async-start | bytes 10321920 | tf_op jit(solution)/shard_map/all_gather | solution.py:674
  14.4 253.5 %all-gather.10.cloned.1.call-start = ((), (), s32[]{:S(2)}) async-start(), calls=%async_computation.6 | async-start | bytes 10321920 | tf_op jit(solution)/shard_map/all_gather | solution.py:672
  14.9 264.9 %all-gather.12.cloned.1.call-start = ((), (), s32[]{:S(2)}) async-start(), calls=%async_computation.7 | async-start | bytes 10321920 | tf_op jit(solution)/shard_map/all_gather | solution.py:673
  15.5 715.3 %reduce-scatter.5.cloned.1.call-start = ((), (), s32[]{:S(2)}) async-start(), calls=%async_computation.9 | async-start | bytes 10321920 | tf_op jit(solution)/shard_map/reduce_scatter | solution.py:762
  223.7 32.1 %collective-permute-start.13 = (bf16[96,2560]{1,0:T(8,128)(2,1)S(1)}, bf16[96,2560]{1,0:T(8,128)(2,1)S(1)}, u32[]{:S(2)}, u32[]{:S(2)}) collective-permute-start(bf16[96,2560]{1,0:T(8,128)(2,1)S(1)} %collective-permute-done.9), channel_id=1, source_target_pairs={{1,2},{2,3},{5,6},{6,7},{9,10},{10,11},{13,14},{14,15},{17,18},{18... | collective-permute-start | bytes 1474568 | tf_op jit(solution)/shard_map/ppermute | solution.py:202
  355.7 33.4 %collective-permute-start.27 = (bf16[96,2560]{1,0:T(8,128)(2,1)S(1)}, bf16[96,2560]{1,0:T(8,128)(2,1)S(1)}, u32[]{:S(2)}, u32[]{:S(2)}) collective-permute-start(bf16[96,2560]{1,0:T(8,128)(2,1)S(1)} %dynamic-slice_convert_fusion.5), channel_id=1, source_target_pairs={{0,2},{1,3},{2,0},{3,1},{4,6},{5,7},{6,4},{7,5},{8,10},{9,11},{10,... | collective-permute-start | bytes 1474568 | tf_op jit(solution)/shard_map/ppermute | solution.py:81
  382.1 38.5 %collective-permute-start.30 = (bf16[192,2560]{1,0:T(8,128)(2,1)S(1)}, bf16[192,2560]{1,0:T(8,128)(2,1)S(1)}, u32[]{:S(2)}, u32[]{:S(2)}) collective-permute-start(bf16[192,2560]{1,0:T(8,128)(2,1)S(1)} %constant_dynamic-slice_fusion.10), channel_id=1, source_target_pairs={{0,1},{1,0},{2,3},{3,2},{4,5},{5,4},{6,7},{7,6},{8,9},{9,8},{10,11... | collective-permute-start | bytes 2949128 | tf_op jit(solution)/shard_map/ppermute | solution.py:81
  432.6 408.6 %reduce-scatter.9.cloned.1.call-start = ((), (), s32[]{:S(2)}) async-start(), calls=%async_computation.11 | async-start | bytes 10321920 | tf_op jit(solution)/shard_map/reduce_scatter | solution.py:762
  433.3 412.3 %reduce-scatter.7.cloned.1.call-start = ((), (), s32[]{:S(2)}) async-start(), calls=%async_computation.10 | async-start | bytes 10321920 | tf_op jit(solution)/shard_map/reduce_scatter | solution.py:762
  442.0 37.7 %collective-permute-start.29 = (bf16[192,2560]{1,0:T(8,128)(2,1)}, bf16[192,2560]{1,0:T(8,128)(2,1)}, u32[]{:S(2)}, u32[]{:S(2)}) collective-permute-start(bf16[192,2560]{1,0:T(8,128)(2,1)} %pad_maximum_fusion.13), channel_id=1, source_target_pairs={{0,1},{1,0},{2,3},{3,2},{4,5},{5,4},{6,7},{7,6},{8,9},{9,8},{10,11... | collective-permute-start | bytes 2949128 | tf_op jit(solution)/shard_map/ppermute | solution.py:81
  501.0 43.0 %collective-permute-start.37 = (bf16[192,2560]{1,0:T(8,128)(2,1)}, bf16[192,2560]{1,0:T(8,128)(2,1)}, u32[]{:S(2)}, u32[]{:S(2)}) collective-permute-start(bf16[192,2560]{1,0:T(8,128)(2,1)} %pad_maximum_fusion.15), channel_id=1, source_target_pairs={{0,1},{1,0},{2,3},{3,2},{4,5},{5,4},{6,7},{7,6},{8,9},{9,8},{10,11... | collective-permute-start | bytes 2949128 | tf_op jit(solution)/shard_map/ppermute | solution.py:81
  504.2 353.1 %reduce-scatter.11.cloned.1.call-start = ((), (), s32[]{:S(2)}) async-start(), calls=%async_computation.12 | async-start | bytes 9584640 | tf_op jit(solution)/shard_map/reduce_scatter | solution.py:762
  549.4 49.9 %collective-permute-start.38 = (bf16[192,2560]{1,0:T(8,128)(2,1)}, bf16[192,2560]{1,0:T(8,128)(2,1)}, u32[]{:S(2)}, u32[]{:S(2)}) collective-permute-start(bf16[192,2560]{1,0:T(8,128)(2,1)} %constant_dynamic-slice_fusion.8), channel_id=1, source_target_pairs={{0,1},{1,0},{2,3},{3,2},{4,5},{5,4},{6,7},{7,6},{8,9},{9,8},{10,11... | collective-permute-start | bytes 2949128 | tf_op jit(solution)/shard_map/ppermute | solution.py:81
  554.6 32.8 %collective-permute-start.32 = (bf16[96,2560]{1,0:T(8,128)(2,1)}, bf16[96,2560]{1,0:T(8,128)(2,1)}, u32[]{:S(2)}, u32[]{:S(2)}) collective-permute-start(bf16[96,2560]{1,0:T(8,128)(2,1)} %dynamic-slice_convert_fusion.4), channel_id=1, source_target_pairs={{0,2},{1,3},{2,0},{3,1},{4,6},{5,7},{6,4},{7,5},{8,10},{9,11},{10,... | collective-permute-start | bytes 1474568 | tf_op jit(solution)/shard_map/ppermute | solution.py:81
  567.3 37.9 %collective-permute-start.45 = (bf16[4,384,320]{1,2,0:T(8,128)(2,1)}, bf16[4,384,320]{1,2,0:T(8,128)(2,1)}, u32[]{:S(2)}, u32[]{:S(2)}) collective-permute-start(bf16[4,384,320]{1,2,0:T(8,128)(2,1)} %copy.57), channel_id=1, source_target_pairs={{0,4},{4,0},{8,12},{12,8},{16,20},{20,16},{24,28},{28,24},{1,5},{5... | collective-permute-start | bytes 2949128 | tf_op jit(solution)/shard_map/ppermute | solution.py:233
  624.0 136.6 %collective-permute-start.34 = (bf16[192,2560]{1,0:T(8,128)(2,1)}, bf16[192,2560]{1,0:T(8,128)(2,1)}, u32[]{:S(2)}, u32[]{:S(2)}) collective-permute-start(bf16[192,2560]{1,0:T(8,128)(2,1)} %pad_maximum_fusion.14), channel_id=1, source_target_pairs={{0,1},{1,0},{2,3},{3,2},{4,5},{5,4},{6,7},{7,6},{8,9},{9,8},{10,11... | collective-permute-start | bytes 2949128 | tf_op jit(solution)/shard_map/ppermute | solution.py:81
  633.0 58.0 %collective-permute-start.46 = (bf16[192,2560]{1,0:T(8,128)(2,1)}, bf16[192,2560]{1,0:T(8,128)(2,1)}, u32[]{:S(2)}, u32[]{:S(2)}) collective-permute-start(bf16[192,2560]{1,0:T(8,128)(2,1)} %constant_dynamic-slice_fusion.7), channel_id=1, source_target_pairs={{0,1},{1,0},{2,3},{3,2},{4,5},{5,4},{6,7},{7,6},{8,9},{9,8},{10,11... | collective-permute-start | bytes 2949128 | tf_op jit(solution)/shard_map/ppermute | solution.py:81
  647.3 101.2 %collective-permute-start.40 = (bf16[96,2560]{1,0:T(8,128)(2,1)}, bf16[96,2560]{1,0:T(8,128)(2,1)}, u32[]{:S(2)}, u32[]{:S(2)}) collective-permute-start(bf16[96,2560]{1,0:T(8,128)(2,1)} %add_convert_fusion.4), channel_id=1, source_target_pairs={{0,2},{1,3},{2,0},{3,1},{4,6},{5,7},{6,4},{7,5},{8,10},{9,11},{10,... | collective-permute-start | bytes 1474568 | tf_op jit(solution)/shard_map/ppermute | solution.py:81
  658.3 67.3 %collective-permute-start.56 = (bf16[192,2560]{1,0:T(8,128)(2,1)S(1)}, bf16[192,2560]{1,0:T(8,128)(2,1)S(1)}, u32[]{:S(2)}, u32[]{:S(2)}) collective-permute-start(bf16[192,2560]{1,0:T(8,128)(2,1)S(1)} %constant_dynamic-slice_fusion.6), channel_id=1, source_target_pairs={{0,1},{1,0},{2,3},{3,2},{4,5},{5,4},{6,7},{7,6},{8,9},{9,8},{10,11... | collective-permute-start | bytes 2949128 | tf_op jit(solution)/shard_map/ppermute | solution.py:81
  719.2 32.6 %collective-permute-start.48 = (bf16[96,2560]{1,0:T(8,128)(2,1)}, bf16[96,2560]{1,0:T(8,128)(2,1)}, u32[]{:S(2)}, u32[]{:S(2)}) collective-permute-start(bf16[96,2560]{1,0:T(8,128)(2,1)} %get-tuple-element.153), channel_id=1, source_target_pairs={{0,1},{1,2},{2,3},{4,5},{5,6},{6,7},{8,9},{9,10},{10,11},{12,13},{... | collective-permute-start | bytes 1474568 | tf_op jit(solution)/shard_map/ppermute | solution.py:202
  750.9 34.5 %collective-permute-start.41 = (bf16[192,2560]{1,0:T(8,128)(2,1)}, bf16[192,2560]{1,0:T(8,128)(2,1)}, u32[]{:S(2)}, u32[]{:S(2)}) collective-permute-start(bf16[192,2560]{1,0:T(8,128)(2,1)} %pad_maximum_fusion.16), channel_id=1, source_target_pairs={{0,1},{1,0},{2,3},{3,2},{4,5},{5,4},{6,7},{7,6},{8,9},{9,8},{10,11... | collective-permute-start | bytes 2949128 | tf_op jit(solution)/shard_map/ppermute | solution.py:81
  802.1 34.3 %collective-permute-start.62 = (bf16[96,2560]{1,0:T(8,128)(2,1)S(1)}, bf16[96,2560]{1,0:T(8,128)(2,1)}, u32[]{:S(2)}, u32[]{:S(2)}) collective-permute-start(bf16[96,2560]{1,0:T(8,128)(2,1)S(1)} %collective-permute-done.58), channel_id=1, source_target_pairs={{1,2},{2,3},{5,6},{6,7},{9,10},{10,11},{13,14},{14,15},{17,18},{18... | collective-permute-start | bytes 1474568 | tf_op jit(solution)/shard_map/ppermute | solution.py:202
  (163 other events, 1876.1 us)
Sparse Core Ops, SparseCore 0:
  13.0 43.8 all-gather.5
  58.7 37.5 all-gather.7
  98.2 62.5 all-gather.13
  162.6 57.7 all-gather.9
  222.0 57.7 all-gather.11
  432.7 75.0 reduce-scatter.4
  511.9 75.0 reduce-scatter.8
  590.6 84.2 reduce-scatter.6
  748.6 70.1 reduce-scatter.10

commit v5 on v4

--- a/solution.py
+++ b/solution.py
@@ -836,7 +836,7 @@
     whole0 = hidden0.finish(up_term)
     mixed0 = Scatter(piece_of(ffn, 0), whole0)
     gain1, grad_hidden1, low1 = hidden_back(1, back_sum1.finish(up_term), kept1)
-    hidden1 = Gather(low1)
+    hidden1 = ChainGather(low1)
     query0, own0, other0 = attention_back(0, whole0, low1)
     keys0 = Reduce(own0, other0, bits)
     hidden1.next()
@@ -844,7 +844,7 @@
     mixed0.next()
     whole1 = hidden1.finish()
     mixed1 = Scatter(piece_of(ffn, 1), whole1)
-    whole_mixed0 = Gather((kept0[0] + mixed0.finish()).astype(LOW))
+    whole_mixed0 = ChainGather((kept0[0] + mixed0.finish()).astype(LOW))
     query1, own1, other1 = attention_back(
         1, whole1, query0, keys0.sent, mixed1.held
     )
@@ -856,7 +856,7 @@
     back0 = join_back(query0, *keys0.finish(), *key_tables)
     back_one0 = one_back(back0, query1, keys1.sent)
     one0 = Scatter(back_one0)
-    whole_mixed1 = Gather((kept1[0] + mixed1.finish()).astype(LOW))
+    whole_mixed1 = ChainGather((kept1[0] + mixed1.finish()).astype(LOW))
     keys1.next()
     back1 = join_back(query1, *keys1.finish(), *key_tables)
     back_one1 = one_back(back1, back_one0, one0.held)

time: 882 us -> 868 us (0.984)
  waiting for transfers between devices: 356 us -> 307 us
  starting transfers between devices: 135 us -> 176 us
    ppermute x24 -> x18, waiting for transfers between devices: 178 us -> 109 us  [line_swap(): return lax.ppermute(value, 'head', [(i, i ^ bit) for i in range(n)])]
    ppermute x9 -> x18, waiting for transfers between devices: 35.1 us -> 79.2 us  [send(): lax.ppermute(self.landed[1], 'head', [(i, i - 1) for i in range(1, n - st...]
    ppermute x9 -> x18, starting transfers between devices: 20.1 us -> 44.7 us  [send(): lax.ppermute(self.landed[0], 'head', [(i, i + 1) for i in range(step, n -...]
    ppermute x4, waiting for transfers between devices: 18.5 us -> 0.01 us  [next(): self.landed = lax.ppermute(sent, 'ctx', flip(bit))]
    ppermute x9 -> x18, starting transfers between devices: 11.7 us -> 23.4 us  [send(): lax.ppermute(self.landed[1], 'head', [(i, i - 1) for i in range(1, n - st...]
    dynamic_update_slice x9 -> x18, other arithmetic: 6.61 us -> 17.7 us  [finish(): whole = lax.dynamic_update_slice_in_dim(whole, block, at, axis=0)]
    ppermute x24 -> x18, starting transfers between devices: 43.1 us -> 53.7 us  [line_swap(): return lax.ppermute(value, 'head', [(i, i ^ bit) for i in range(n)])]
    select_n x10 -> x4, other arithmetic: 12.7 us -> 3.56 us  [land(): first = jnp.where(self.mine == 0, self.held, self.landed)]
  transfers between devices with their start and end apart: 78 -> 90, of which waited for: 33 -> 34; matrix products, arithmetic and copies ran while one was open for 23% -> 23% of each run, Pallas kernels for 11% -> 11%
where the time goes in v5:
time: 868 us; the launch traced here: 856 us
  waiting for transfers between devices  307 us (35%)
  starting transfers between devices  176 us (20%)
  Pallas kernels  105 us (12%)
  other arithmetic  98.6 us (11%)
  local copies, waits for them, and re-layouts  91.5 us (11%)
  matrix products  62.1 us (7%)
  between operations  16.7 us (2%)
    ppermute x18, waiting for transfers between devices, line_swap(): return lax.ppermute(value, 'head', [(i, i ^ bit) for i in range(n)])  109 us
    ppermute x18, waiting for transfers between devices, send(): lax.ppermute(self.landed[1], 'head', [(i, i - 1) for i in range(1, n - st...  79.2 us
    dot_general x11, matrix products, dot(): lax.dot_general(left, right, (((a,), (b,)), ((), ())), preferred_element_...  62.1 us
    ppermute x18, starting transfers between devices, line_swap(): return lax.ppermute(value, 'head', [(i, i ^ bit) for i in range(n)])  53.7 us
    ppermute x18, starting transfers between devices, send(): lax.ppermute(self.landed[0], 'head', [(i, i + 1) for i in range(step, n -...  44.7 us
    ppermute x4, waiting for transfers between devices, cube_gather(): got = lax.ppermute(own, 'ctx', flip(bit))  39 us
    all_gather x1, waiting for transfers between devices, per_device(): full_qkv = lax.all_gather(qkv_shard, 'ctx', axis=0, tiled=True)  37.8 us
    pallas_call x3, Pallas kernels, back_through(): pl.pallas_call(back_kernel, grid=((width + tile - 1) // tile,), in_specs=...  34.6 us
  transfers between devices with their start and end apart: 90, of which 34 were waited for; matrix products, arithmetic and copies ran while one was open for 23% of the time, Pallas kernels for 11%

profile of v5, /device:TPU:0, one launch (start us, length us, event | category | flops | bytes accessed | tf_op | source)
XLA Modules:
  0.0 856.1 jit_solution(8431450605877996463)
XLA Ops:
  19.1 37.8 %all-gather.6.cloned.1.call-done.weight_ref = bf16[2560,1024]{1,0:T(8,128)(2,1)} async-done(((bf16[320,1024]{1,0:T(8,128)(2,1)}), bf16[2560,1024]{1,0:T(8,128)(2,1)}) %all-gather.6.cloned.1.call-update) | async-done | bytes 5242896 | tf_op jit(solution)/shard_map/all_gather | solution.py:670
  62.2 10.5 %project.1 = (bf16[768,2560]{1,0:T(8,128)(2,1)}, bf16[768,640]{1,0:T(8,128)(2,1)S(1)}, bf16[768,320]{1,0:T(8,128)(2,1)S(1)}) custom-call(bf16[768,2560]{1,0:T(8,128)(2,1)} %bitcast.94, f32[1,2560]{1,0:T(1,128)S(1)} %copy.39.gain_ref, bf16[2560,1024]{1,0:T(8,128)(2,1)} %all-gather.6.cloned.1.call-done.weight_ref, f32[192,1024]{1,0:T(8,128)S(1)} %concatenate.87.cos_ref, ...), custom_call_target="tpu_custom_call" | custom-call | flops 4026531840 | bytes 13107200 | tf_op jit(solution)/shard_map/project/pallas_call | solution.py:275
  84.6 15.9 %collective-permute-done.1 = bf16[2,384,320]{1,2,0:T(8,128)(2,1)S(1)} collective-permute-done((bf16[2,384,320]{1,2,0:T(8,128)(2,1)S(1)}, bf16[2,384,320]{1,2,0:T(8,128)(2,1)S(1)}, u32[]{:S(2)}, u32[]{:S(2)}) %collective-permute-start.1) | collective-permute-done | bytes 491552 | tf_op jit(solution)/shard_map/ppermute | solution.py:62
  106.0 14.0 %collective-permute-done.15 = bf16[1,384,320]{2,1,0:T(8,128)(2,1)S(1)} collective-permute-done((bf16[1,384,320]{2,1,0:T(8,128)(2,1)S(1)}, bf16[1,384,320]{2,1,0:T(8,128)(2,1)S(1)}, u32[]{:S(2)}, u32[]{:S(2)}) %collective-permute-start.15) | collective-permute-done | bytes 245792 | tf_op jit(solution)/shard_map/ppermute | solution.py:62
  184.8 10.8 %collective-permute-done.18 = bf16[96,2560]{1,0:T(8,128)(2,1)S(1)} collective-permute-done((bf16[96,2560]{1,0:T(8,128)(2,1)S(1)}, bf16[96,2560]{1,0:T(8,128)(2,1)S(1)}, u32[]{:S(2)}, u32[]{:S(2)}) %collective-permute-start.18) | collective-permute-done | bytes 491552 | tf_op jit(solution)/shard_map/ppermute | solution.py:174
  256.6 11.3 %collective-permute-done.24 = bf16[96,2560]{1,0:T(8,128)(2,1)} collective-permute-done((bf16[96,2560]{1,0:T(8,128)(2,1)S(1)}, bf16[96,2560]{1,0:T(8,128)(2,1)}, u32[]{:S(2)}, u32[]{:S(2)}) %collective-permute-start.24) | collective-permute-done | bytes 491552 | tf_op jit(solution)/shard_map/ppermute | solution.py:81
  267.9 12.0 %all-gather.12.cloned.1.call-done.up_ref.refs_3_ = bf16[2560,1728]{1,0:T(8,128)(2,1)} async-done(((bf16[320,1728]{1,0:T(8,128)(2,1)}), bf16[2560,1728]{1,0:T(8,128)(2,1)}) %all-gather.12.cloned.1.call-update) | async-done | bytes 8847376 | tf_op jit(solution)/shard_map/all_gather | solution.py:673
  284.1 17.0 %feed.2 = (bf16[384,1728]{1,0:T(8,128)(2,1)S(1)}, bf16[384,1728]{1,0:T(8,128)(2,1)S(1)}, bf16[384,1728]{1,0:T(8,128)(2,1)S(1)}) custom-call(bf16[384,2560]{1,0:T(8,128)(2,1)S(1)} %select_dynamic-update-slice_fusion.3.input_ref, bf16[384,2560]{1,0:T(8,128)(2,1)} %get-tuple-element.172.grad_ref, ...), custom_call_target="tpu_custom_call" | custom-call | flops 5096079360 | bytes 17227776 | tf_op jit(solution)/shard_map/feed/pallas_call | solution.py:320
  306.4 11.1 %back_through.3 = bf16[384,2560]{1,0:T(8,128)(2,1)S(1)} custom-call(bf16[384,1728]{1,0:T(8,128)(2,1)S(1)} %get-tuple-element.70.refs_0_, bf16[384,1728]{1,0:T(8,128)(2,1)S(1)} %get-tuple-element.71.refs_1_, bf16[2560,1728]{1,0:T(8,128)(2,1)} %all-gather.10.cloned.1.call-done.gate_ref.refs_2_, bf16[2560,1728]{1,0:T(8,128)(2,1)} %all-gather.12.cloned.1.call-done.up_ref.refs_3_), custom_call_target="tpu_custom_call" | custom-call | flops 3397386240 | bytes 11157504 | tf_op jit(solution)/shard_map/back_through/pallas_call | solution.py:350
  321.7 16.8 %feed.3 = (bf16[384,1728]{1,0:T(8,128)(2,1)S(1)}, bf16[384,1728]{1,0:T(8,128)(2,1)S(1)}, bf16[384,1728]{1,0:T(8,128)(2,1)S(1)}) custom-call(bf16[384,2560]{1,0:T(8,128)(2,1)S(1)} %pad_maximum_fusion.5.input_ref, bf16[384,2560]{1,0:T(8,128)(2,1)} %get-tuple-element.171.grad_ref, bf16[2560,1728]{1,0:T(8,128)(2,1)} %all-gather.10.cloned.1.call-done.gate_ref.refs_2_, ...), custom_call_target="tpu_custom_call" | custom-call | flops 5096079360 | bytes 17227776 | tf_op jit(solution)/shard_map/feed/pallas_call | solution.py:320
  344.8 9.7 %convolution_convert_fusion.2 = bf16[2560,1728]{1,0:T(8,128)(2,1)} fusion(bf16[768,2560]{1,0:T(8,128)(2,1)S(1)} %copy-done.49, bf16[768,1728]{1,0:T(8,128)(2,1)S(1)} %constant_dynamic-update-slice_fusion.2.refs_0_), kind=kOutput, calls=%fused_computation.2 | convolution fusion | flops 6799196160 | bytes 15433728 | tf_op jit(solution)/shard_map/dot_general | solution.py:24
  355.8 12.4 %collective-permute-start.27 = (bf16[96,2560]{1,0:T(8,128)(2,1)S(1)}, bf16[96,2560]{1,0:T(8,128)(2,1)S(1)}, u32[]{:S(2)}, u32[]{:S(2)}) collective-permute-start(bf16[96,2560]{1,0:T(8,128)(2,1)S(1)} %dynamic-slice_convert_fusion.5), channel_id=1, source_target_pairs={{0,2},{1,3},{2,0},{3,1},{4,6},{5,7},{6,4},{7,5},{8,10},{9,11},{10,... | collective-permute-start | bytes 1474568 | tf_op jit(solution)/shard_map/ppermute | solution.py:81
  370.9 11.2 %back_through.4 = bf16[384,2560]{1,0:T(8,128)(2,1)S(1)} custom-call(bf16[384,1728]{1,0:T(8,128)(2,1)S(1)} %copy-done.14, bf16[384,1728]{1,0:T(8,128)(2,1)S(1)} %copy-done.9, bf16[2560,1728]{1,0:T(8,128)(2,1)} %all-gather.10.cloned.1.call-done.gate_ref.refs_2_, bf16[2560,1728]{1,0:T(8,128)(2,1)} %all-gather.12.cloned.1.call-done.up_ref.refs_3_), custom_call_target="tpu_custom_call" | custom-call | flops 3397386240 | bytes 11157504 | tf_op jit(solution)/shard_map/back_through/pallas_call | solution.py:350
  394.2 12.3 %back_through.5 = bf16[768,2560]{1,0:T(8,128)(2,1)} custom-call(bf16[768,1728]{1,0:T(8,128)(2,1)S(1)} %copy-done.3, bf16[2560,1728]{1,0:T(8,128)(2,1)} %all-gather.14.cloned.1.call-done.down_ref.refs_1_), custom_call_target="tpu_custom_call" | custom-call | flops 3397386240 | bytes 7716864 | tf_op jit(solution)/shard_map/back_through/pallas_call | solution.py:350
  406.5 14.3 %collective-permute-done.30 = bf16[192,2560]{1,0:T(8,128)(2,1)S(1)} collective-permute-done((bf16[192,2560]{1,0:T(8,128)(2,1)S(1)}, bf16[192,2560]{1,0:T(8,128)(2,1)S(1)}, u32[]{:S(2)}, u32[]{:S(2)}) %collective-permute-start.30) | collective-permute-done | bytes 983072 | tf_op jit(solution)/shard_map/ppermute | solution.py:81
  422.6 10.2 %convolution_convert_fusion.1 = bf16[2560,1728]{1,0:T(8,128)(2,1)} fusion(bf16[768,2560]{1,0:T(8,128)(2,1)S(1)} %pad_maximum_fusion.1, bf16[384,1728]{1,0:T(8,128)(2,1)S(1)} %copy-done.15, bf16[384,1728]{1,0:T(8,128)(2,1)S(1)} %copy-done.12), kind=kOutput, calls=%fused_computation.1 | convolution fusion | flops 6804504576 | bytes 15433728 | tf_op jit(solution)/shard_map/dot_general | solution.py:24
  444.6 9.8 %convolution_convert_fusion = bf16[2560,1728]{1,0:T(8,128)(2,1)} fusion(bf16[768,2560]{1,0:T(8,128)(2,1)S(1)} %copy-done.80, bf16[384,1728]{1,0:T(8,128)(2,1)S(1)} %copy-done.10, bf16[384,1728]{1,0:T(8,128)(2,1)S(1)} %copy-done.7), kind=kOutput, calls=%fused_computation | convolution fusion | flops 6804504576 | bytes 15433728 | tf_op jit(solution)/shard_map/dot_general | solution.py:24
  454.5 10.2 %collective-permute-done.39 = bf16[96,2560]{1,0:T(8,128)(2,1)} collective-permute-done((bf16[96,2560]{1,0:T(8,128)(2,1)}, bf16[96,2560]{1,0:T(8,128)(2,1)}, u32[]{:S(2)}, u32[]{:S(2)}) %collective-permute-start.39) | collective-permute-done | bytes 491552 | tf_op jit(solution)/shard_map/ppermute | solution.py:81
  500.3 30.7 %collective-permute-done.42 = bf16[96,2560]{1,0:T(8,128)(2,1)} collective-permute-done((bf16[96,2560]{1,0:T(8,128)(2,1)}, bf16[96,2560]{1,0:T(8,128)(2,1)}, u32[]{:S(2)}, u32[]{:S(2)}) %collective-permute-start.42) | collective-permute-done | bytes 491552 | tf_op jit(solution)/shard_map/ppermute | solution.py:203
  662.7 10.2 %collective-permute-done.49 = bf16[96,2560]{1,0:T(8,128)(2,1)} collective-permute-done((bf16[96,2560]{1,0:T(8,128)(2,1)S(1)}, bf16[96,2560]{1,0:T(8,128)(2,1)}, u32[]{:S(2)}, u32[]{:S(2)}) %collective-permute-start.49) | collective-permute-done | bytes 491552 | tf_op jit(solution)/shard_map/ppermute | solution.py:203
  684.2 22.9 %collective-permute-done.59 = bf16[96,2560]{1,0:T(8,128)(2,1)S(1)} collective-permute-done((bf16[96,2560]{1,0:T(8,128)(2,1)S(1)}, bf16[96,2560]{1,0:T(8,128)(2,1)S(1)}, u32[]{:S(2)}, u32[]{:S(2)}) %collective-permute-start.59) | collective-permute-done | bytes 491552 | tf_op jit(solution)/shard_map/ppermute | solution.py:81
  742.8 14.3 %collective-permute-done.69 = bf16[96,2560]{1,0:T(8,128)(2,1)S(1)} collective-permute-done((bf16[96,2560]{1,0:T(8,128)(2,1)S(1)}, bf16[96,2560]{1,0:T(8,128)(2,1)S(1)}, u32[]{:S(2)}, u32[]{:S(2)}) %collective-permute-start.69) | collective-permute-done | bytes 491552 | tf_op jit(solution)/shard_map/ppermute | solution.py:81
  765.9 12.2 %collective-permute-start.77 = (f32[2,2560]{1,0:T(2,128)S(1)}, f32[2,2560]{1,0:T(2,128)S(1)}, u32[]{:S(2)}, u32[]{:S(2)}) collective-permute-start(f32[2,2560]{1,0:T(2,128)S(1)} %add.551), channel_id=1, source_target_pairs={{0,2},{1,3},{2,0},{3,1},{4,6},{5,7},{6,4},{7,5},{8,10},{9,11},{10,... | collective-permute-start | bytes 61448 | tf_op jit(solution)/shard_map/ppermute | solution.py:81
  810.6 14.4 %collective-permute-done.72 = bf16[96,2560]{1,0:T(8,128)(2,1)} collective-permute-done((bf16[96,2560]{1,0:T(8,128)(2,1)S(1)}, bf16[96,2560]{1,0:T(8,128)(2,1)}, u32[]{:S(2)}, u32[]{:S(2)}) %collective-permute-start.72) | collective-permute-done | bytes 491552 | tf_op jit(solution)/shard_map/ppermute | solution.py:203
  (582 shorter events, 487.6 us)
Async XLA Ops:
  7.2 49.7 %all-gather.6.cloned.1.call-start = ((), (), s32[]{:S(2)}) async-start(), calls=%async_computation.4 | async-start | bytes 5898240 | tf_op jit(solution)/shard_map/all_gather | solution.py:670
  12.9 118.1 %all-gather.8.cloned.1.call-start = ((), (), s32[]{:S(2)}) async-start(), calls=%async_computation.5 | async-start | bytes 3686400 | tf_op jit(solution)/shard_map/all_gather | solution.py:671
  13.6 254.2 %all-gather.14.cloned.1.call-start = ((), (), s32[]{:S(2)}) async-start(), calls=%async_computation.8 | async-start | bytes 10321920 | tf_op jit(solution)/shard_map/all_gather | solution.py:674
  14.4 253.5 %all-gather.10.cloned.1.call-start = ((), (), s32[]{:S(2)}) async-start(), calls=%async_computation.6 | async-start | bytes 10321920 | tf_op jit(solution)/shard_map/all_gather | solution.py:672
  14.9 264.9 %all-gather.12.cloned.1.call-start = ((), (), s32[]{:S(2)}) async-start(), calls=%async_computation.7 | async-start | bytes 10321920 | tf_op jit(solution)/shard_map/all_gather | solution.py:673
  15.5 702.5 %reduce-scatter.5.cloned.1.call-start = ((), (), s32[]{:S(2)}) async-start(), calls=%async_computation.9 | async-start | bytes 10321920 | tf_op jit(solution)/shard_map/reduce_scatter | solution.py:762
  382.2 38.6 %collective-permute-start.30 = (bf16[192,2560]{1,0:T(8,128)(2,1)S(1)}, bf16[192,2560]{1,0:T(8,128)(2,1)S(1)}, u32[]{:S(2)}, u32[]{:S(2)}) collective-permute-start(bf16[192,2560]{1,0:T(8,128)(2,1)S(1)} %constant_dynamic-slice_fusion.10), channel_id=1, source_target_pairs={{0,1},{1,0},{2,3},{3,2},{4,5},{5,4},{6,7},{7,6},{8,9},{9,8},{10,11... | collective-permute-start | bytes 2949128 | tf_op jit(solution)/shard_map/ppermute | solution.py:81
  432.8 396.6 %reduce-scatter.9.cloned.1.call-start = ((), (), s32[]{:S(2)}) async-start(), calls=%async_computation.11 | async-start | bytes 10321920 | tf_op jit(solution)/shard_map/reduce_scatter | solution.py:762
  433.6 400.3 %reduce-scatter.7.cloned.1.call-start = ((), (), s32[]{:S(2)}) async-start(), calls=%async_computation.10 | async-start | bytes 10321920 | tf_op jit(solution)/shard_map/reduce_scatter | solution.py:762
  442.1 35.2 %collective-permute-start.29 = (bf16[192,2560]{1,0:T(8,128)(2,1)}, bf16[192,2560]{1,0:T(8,128)(2,1)}, u32[]{:S(2)}, u32[]{:S(2)}) collective-permute-start(bf16[192,2560]{1,0:T(8,128)(2,1)} %pad_maximum_fusion.10), channel_id=1, source_target_pairs={{0,1},{1,0},{2,3},{3,2},{4,5},{5,4},{6,7},{7,6},{8,9},{9,8},{10,11... | collective-permute-start | bytes 2949128 | tf_op jit(solution)/shard_map/ppermute | solution.py:81
  493.8 40.0 %collective-permute-start.54 = (bf16[4,384,320]{1,2,0:T(8,128)(2,1)}, bf16[4,384,320]{1,2,0:T(8,128)(2,1)S(1)}, u32[]{:S(2)}, u32[]{:S(2)}) collective-permute-start(bf16[4,384,320]{1,2,0:T(8,128)(2,1)} %copy.50), channel_id=1, source_target_pairs={{0,4},{4,0},{8,12},{12,8},{16,20},{20,16},{24,28},{28,24},{1,5},{5... | collective-permute-start | bytes 2949128 | tf_op jit(solution)/shard_map/ppermute | solution.py:233
  496.1 38.7 %collective-permute-start.31 = (bf16[192,2560]{1,0:T(8,128)(2,1)}, bf16[192,2560]{1,0:T(8,128)(2,1)}, u32[]{:S(2)}, u32[]{:S(2)}) collective-permute-start(bf16[192,2560]{1,0:T(8,128)(2,1)} %constant_dynamic-slice_fusion.9), channel_id=1, source_target_pairs={{0,1},{1,0},{2,3},{3,2},{4,5},{5,4},{6,7},{7,6},{8,9},{9,8},{10,11... | collective-permute-start | bytes 2949128 | tf_op jit(solution)/shard_map/ppermute | solution.py:81
  496.1 34.9 %collective-permute-start.42 = (bf16[96,2560]{1,0:T(8,128)(2,1)}, bf16[96,2560]{1,0:T(8,128)(2,1)}, u32[]{:S(2)}, u32[]{:S(2)}) collective-permute-start(bf16[96,2560]{1,0:T(8,128)(2,1)} %collective-permute-done.41), channel_id=1, source_target_pairs={{1,0},{2,1},{5,4},{6,5},{9,8},{10,9},{13,12},{14,13},{17,16},{18,1... | collective-permute-start | bytes 1474568 | tf_op jit(solution)/shard_map/ppermute | solution.py:203
  497.4 34.9 %collective-permute-start.44 = (bf16[96,2560]{1,0:T(8,128)(2,1)}, bf16[96,2560]{1,0:T(8,128)(2,1)}, u32[]{:S(2)}, u32[]{:S(2)}) collective-permute-start(bf16[96,2560]{1,0:T(8,128)(2,1)} %collective-permute-done.40), channel_id=1, source_target_pairs={{1,2},{2,3},{5,6},{6,7},{9,10},{10,11},{13,14},{14,15},{17,18},{18... | collective-permute-start | bytes 1474568 | tf_op jit(solution)/shard_map/ppermute | solution.py:202
  500.3 343.7 %reduce-scatter.11.cloned.1.call-start = ((), (), s32[]{:S(2)}) async-start(), calls=%async_computation.12 | async-start | bytes 9584640 | tf_op jit(solution)/shard_map/reduce_scatter | solution.py:762
  539.9 45.1 %collective-permute-start.55 = (bf16[2,384,320]{1,2,0:T(8,128)(2,1)}, bf16[2,384,320]{1,2,0:T(8,128)(2,1)}, u32[]{:S(2)}, u32[]{:S(2)}) collective-permute-start(bf16[2,384,320]{1,2,0:T(8,128)(2,1)} %copy.53), channel_id=1, source_target_pairs={{0,16},{4,20},{8,24},{12,28},{16,0},{20,4},{24,8},{28,12},{1,17},{... | collective-permute-start | bytes 1474568 | tf_op jit(solution)/shard_map/ppermute | solution.py:242
  578.4 36.1 %collective-permute-start.34 = (bf16[96,2560]{1,0:T(8,128)(2,1)}, bf16[96,2560]{1,0:T(8,128)(2,1)}, u32[]{:S(2)}, u32[]{:S(2)}) collective-permute-start(bf16[96,2560]{1,0:T(8,128)(2,1)} %get-tuple-element.155), channel_id=1, source_target_pairs={{1,0},{2,1},{3,2},{5,4},{6,5},{7,6},{9,8},{10,9},{11,10},{13,12},{... | collective-permute-start | bytes 1474568 | tf_op jit(solution)/shard_map/ppermute | solution.py:203
  579.6 36.2 %collective-permute-start.33 = (bf16[96,2560]{1,0:T(8,128)(2,1)}, bf16[96,2560]{1,0:T(8,128)(2,1)}, u32[]{:S(2)}, u32[]{:S(2)}) collective-permute-start(bf16[96,2560]{1,0:T(8,128)(2,1)} %get-tuple-element.155), channel_id=1, source_target_pairs={{0,1},{1,2},{2,3},{4,5},{5,6},{6,7},{8,9},{9,10},{10,11},{12,13},{... | collective-permute-start | bytes 1474568 | tf_op jit(solution)/shard_map/ppermute | solution.py:202
  615.8 119.9 %collective-permute-start.37 = (bf16[96,2560]{1,0:T(8,128)(2,1)}, bf16[96,2560]{1,0:T(8,128)(2,1)}, u32[]{:S(2)}, u32[]{:S(2)}) collective-permute-start(bf16[96,2560]{1,0:T(8,128)(2,1)} %collective-permute-done.33), channel_id=1, source_target_pairs={{1,2},{2,3},{5,6},{6,7},{9,10},{10,11},{13,14},{14,15},{17,18},{18... | collective-permute-start | bytes 1474568 | tf_op jit(solution)/shard_map/ppermute | solution.py:202
  624.6 48.3 %collective-permute-start.58 = (bf16[192,2560]{1,0:T(8,128)(2,1)}, bf16[192,2560]{1,0:T(8,128)(2,1)}, u32[]{:S(2)}, u32[]{:S(2)}) collective-permute-start(bf16[192,2560]{1,0:T(8,128)(2,1)} %constant_dynamic-slice_fusion.7), channel_id=1, source_target_pairs={{0,1},{1,0},{2,3},{3,2},{4,5},{5,4},{6,7},{7,6},{8,9},{9,8},{10,11... | collective-permute-start | bytes 2949128 | tf_op jit(solution)/shard_map/ppermute | solution.py:81
  641.3 98.0 %collective-permute-start.48 = (bf16[96,2560]{1,0:T(8,128)(2,1)S(1)}, bf16[96,2560]{1,0:T(8,128)(2,1)}, u32[]{:S(2)}, u32[]{:S(2)}) collective-permute-start(bf16[96,2560]{1,0:T(8,128)(2,1)S(1)} %get-tuple-element.157), channel_id=1, source_target_pairs={{0,1},{1,2},{2,3},{4,5},{5,6},{6,7},{8,9},{9,10},{10,11},{12,13},{... | collective-permute-start | bytes 1474568 | tf_op jit(solution)/shard_map/ppermute | solution.py:202
  672.9 42.0 %collective-permute-start.68 = (bf16[192,2560]{1,0:T(8,128)(2,1)S(1)}, bf16[192,2560]{1,0:T(8,128)(2,1)S(1)}, u32[]{:S(2)}, u32[]{:S(2)}) collective-permute-start(bf16[192,2560]{1,0:T(8,128)(2,1)S(1)} %constant_dynamic-slice_fusion.6), channel_id=1, source_target_pairs={{0,1},{1,0},{2,3},{3,2},{4,5},{5,4},{6,7},{7,6},{8,9},{9,8},{10,11... | collective-permute-start | bytes 2949128 | tf_op jit(solution)/shard_map/ppermute | solution.py:81
  672.9 67.1 %collective-permute-start.50 = (bf16[96,2560]{1,0:T(8,128)(2,1)}, bf16[96,2560]{1,0:T(8,128)(2,1)}, u32[]{:S(2)}, u32[]{:S(2)}) collective-permute-start(bf16[96,2560]{1,0:T(8,128)(2,1)} %collective-permute-done.49), channel_id=1, source_target_pairs={{1,0},{2,1},{5,4},{6,5},{9,8},{10,9},{13,12},{14,13},{17,16},{18,1... | collective-permute-start | bytes 1474568 | tf_op jit(solution)/shard_map/ppermute | solution.py:203
  741.5 36.7 %collective-permute-start.51 = (bf16[96,2560]{1,0:T(8,128)(2,1)}, bf16[96,2560]{1,0:T(8,128)(2,1)S(1)}, u32[]{:S(2)}, u32[]{:S(2)}) collective-permute-start(bf16[96,2560]{1,0:T(8,128)(2,1)} %collective-permute-done.50), channel_id=1, source_target_pairs={{1,0},{5,4},{9,8},{13,12},{17,16},{21,20},{25,24},{29,28}} | collective-permute-start | bytes 1474568 | tf_op jit(solution)/shard_map/ppermute | solution.py:203
  (173 other events, 2239.4 us)
Sparse Core Ops, SparseCore 0:
  13.0 43.8 all-gather.5
  58.7 37.5 all-gather.7
  98.3 62.5 all-gather.13
  162.6 57.7 all-gather.9
  222.1 57.7 all-gather.11
  432.9 74.9 reduce-scatter.4
  512.0 86.6 reduce-scatter.8
  602.4 78.3 reduce-scatter.6
  735.8 70.6 reduce-scatter.10
